TPU v7x, 512 devices: a whole 4x4x16 slice. The times are simulated.
512 devices in a mesh: dp: 2 (over core), section: 8 (over y, z_hi), tensor: 32 (over z_lo, x).
Axes of the slice: x: 4, y: 4, z: 16 (z_hi: 2, z_lo: 8; z = z_hi * 8 + z_lo), core: 2. Of those that a mesh axis runs over, the one named last changes fastest.
Arguments:
- layer_saved_input: bfloat16 [8, 1536, 16384], P('section', 'dp', 'tensor'), may hold values from -8 to 8
- key_value_gradient: bfloat16 [8, 1536, 2048], P('section', ('dp', 'tensor')), may hold values from -6 to 6
- key_value_weight: bfloat16 [8, 16384, 2048], P('section', 'tensor'), may hold values from -0.046875 to 0.046875
- adapter_down_weight: bfloat16 [8, 16384, 32], P('section', 'tensor'), may hold values from -0.046875 to 0.046875
- adapter_up_weight: bfloat16 [8, 2, 16, 1024], P('section'), may hold values from -0.1875 to 0.1875
- attention_norm_scale: float32 [8, 16384], P('section', 'tensor'), may hold values from 0.25 to 1.75
Outputs:
- input_grad: bfloat16 [8, 1536, 16384], P('section', 'dp', 'tensor')
- down_grad: float32 [8, 16384, 32], P('section', 'tensor')
- up_grad: float32 [8, 2, 16, 1024], P('section')
All inputs are finite; a program needn't handle non-finite values.
Results may differ from a plain program's by a relative error of at most 0.0095.
Values may be sent and summed in bfloat16 or wider, within the bound.
No kernel may reach another device: no remote copies, remote signals or barrier semaphores. Data moves between devices by JAX's collectives and lax.ppermute only.
A program may use at most 128 MiB of HBM per device.

v0:
```python
import jax
import jax.numpy as jnp
from jax import lax
from jax.sharding import PartitionSpec as P

adapter_scale = 2.0
norm_epsilon = 1e-05


def from_behind(value, axis, steps):
    count = lax.axis_size(axis)
    first, last = (max(0, -steps), min(count, count - steps))
    return lax.ppermute(value, axis, [(source, source + steps) for source in range(first, last)])


def local(
    layer_saved_input,
    key_value_gradient,
    key_value_weight,
    adapter_down_weight,
    adapter_up_weight,
    attention_norm_scale,
):
    inputs = layer_saved_input[0]
    kv_grads = key_value_gradient[0]
    weight = key_value_weight[0]
    down_share = adapter_down_weight[0]
    adapter_up_matrix = adapter_up_weight[0]
    gain_part = attention_norm_scale[0]
    row_count = inputs.shape[0]
    span = inputs.shape[1]
    own_rows = kv_grads.shape[0]
    half_width = kv_grads.shape[1] // 2
    rank_two = down_share.shape[1]
    groups = lax.axis_size("tensor")
    width = span * groups
    total_tokens = row_count * lax.axis_size("dp")
    factor = adapter_scale / total_tokens
    widened = inputs.astype(jnp.float32)
    square_sum = lax.psum(jnp.sum(widened * widened, axis=1), "tensor")
    inverse = lax.rsqrt(square_sum[:, None] / width + norm_epsilon)
    scaled = widened * inverse
    normed = (scaled * gain_part[None, :]).astype(jnp.bfloat16)
    lowered_part = jnp.dot(normed, down_share, preferred_element_type=jnp.float32)
    grads_three = kv_grads.reshape(own_rows, 2, half_width)
    hidden_own = jnp.einsum(
        "tck,crk->tcr", grads_three, adapter_up_matrix, preferred_element_type=jnp.float32
    )
    hidden_own = hidden_own.reshape(own_rows, rank_two).astype(jnp.bfloat16)
    hidden_all = lax.all_gather(hidden_own, "tensor", axis=0, tiled=True)
    base_term = lax.dot_general(
        lax.all_gather(kv_grads, "tensor", axis=0, tiled=True),
        weight,
        (((1,), (1,)), ((), ())),
        preferred_element_type=jnp.float32,
    )
    adapter_term = lax.dot_general(
        hidden_all, down_share, (((1,), (1,)), ((), ())), preferred_element_type=jnp.float32
    )
    normed_grad = base_term + adapter_scale * adapter_term
    scaled_grad = normed_grad * gain_part[None, :]
    center_sum, lowered_sum = lax.psum(
        (jnp.sum(scaled_grad * scaled, axis=1), lowered_part), "tensor"
    )
    center = center_sum[:, None] / width
    lowered = lowered_sum.astype(jnp.bfloat16)
    branch_index = ((scaled_grad - scaled * center) * inverse).astype(jnp.bfloat16)
    branch_wide = branch_index.astype(jnp.float32)
    running = branch_wide
    carried = branch_index
    for step in range(lax.axis_size("section") - 1):
        carried = from_behind(carried, "section", -1)
        running = running + carried.astype(jnp.float32)
    result_grad = running.astype(jnp.bfloat16)
    down_local = factor * lax.dot_general(
        normed, hidden_all, (((0,), (0,)), ((), ())), preferred_element_type=jnp.float32
    )
    down_gradient_total = lax.psum(down_local, "dp")
    offset = lax.axis_index("tensor") * own_rows
    lowered_own = lax.dynamic_slice_in_dim(lowered, offset, own_rows, 0)
    lowered_three = lowered_own.reshape(own_rows, 2, rank_two // 2)
    up_local = factor * jnp.einsum(
        "tcr,tck->crk", lowered_three, grads_three, preferred_element_type=jnp.float32
    )
    up_gradient_total = lax.psum(up_local, ("dp", "tensor"))
    return (result_grad[None], down_gradient_total[None], up_gradient_total[None])


def solution(mesh):
    in_specs = (
        P("section", "dp", "tensor"),
        P("section", ("dp", "tensor"), None),
        P("section", "tensor", None),
        P("section", "tensor", None),
        P("section", None, None, None),
        P("section", "tensor"),
    )
    out_specs = (
        P("section", "dp", "tensor"),
        P("section", "tensor", None),
        P("section", None, None, None),
    )
    return jax.shard_map(local, mesh=mesh, in_specs=in_specs, out_specs=out_specs, check_vma=False)
```

profile of v0, /device:TPU:1, one launch (start us, length us, event | category | flops | bytes accessed | tf_op | source)
XLA Modules:
  0.0 1784.5 jit_solution(15563849266348538261)
XLA Ops:
  8.0 0.0 all-gather.3.cloned.1.call-start
  8.1 0.7 all-gather.3.cloned.1.call-update
  8.8 0.0 all-reduce.4.cloned.1.call-start
  8.8 0.9 reshape_squeeze.3
  9.8 1.0 convolution_convert_fusion
  10.8 0.1 copy.19
  10.9 1.4 copy.20
  12.3 0.2 fusion.13
  12.5 114.2 %psum.35 = f32[768]{0:T(1024)S(1)} all-reduce(f32[768]{0:T(1024)S(1)} %fusion.13), channel_id=1, replica_groups=mesh['dp'=2,'section'=8,'tensor'=32] {'tensor'}, use_global_device_ids=true, to_apply=%region_1.0 | all-reduce | flops 768 | bytes 6144 | tf_op jit(solution)/shard_map/psum | solution.py:40
  126.7 99.9 %all_gather.7 = bf16[768,32]{1,0:T(8,128)(2,1)S(1)} all-gather(bf16[24,32]{1,0:T(8,128)(2,1)S(1)} %copy.19), channel_id=1, replica_groups=mesh['dp'=2,'section'=8,'tensor'=32] {'tensor'}, dimensions={0}, use_global_device_ids=true | all-gather | bytes 50688 | tf_op jit(solution)/shard_map/all_gather | solution.py:50
  226.6 0.5 fusion.20
  227.1 0.0 all-gather.3.cloned.1.call-done
  227.1 3.7 fusion
  230.9 1.7 fusion.8
  232.6 210.6 %all-reduce = (f32[768]{0:T(1024)S(1)}, bf16[768,32]{1,0:T(8,128)(2,1)}) all-reduce(f32[768]{0:T(1024)S(1)} %get-tuple-element.14, f32[768,32]{1,0:T(8,128)S(1)} %fusion.20), channel_id=1, replica_groups=mesh['dp'=2,'section'=8,'tensor'=32] {'tensor'}, use_global_device_ids=true, to_apply=%region_3.0 | all-reduce | flops 25344 | bytes 153600 | tf_op jit(solution)/shard_map/psum | solution.py:62
  443.2 1.7 fusion.11
  444.9 0.9 copy-done.1
  445.8 1.4 collective-permute-start
  447.2 20.3 %collective-permute-done = bf16[768,512]{0,1:T(8,128)(2,1)S(1)} collective-permute-done((bf16[768,512]{0,1:T(8,128)(2,1)S(1)}, bf16[768,512]{0,1:T(8,128)(2,1)S(1)}, u32[]{:S(2)}, u32[]{:S(2)}) %collective-permute-start) | collective-permute-done | bytes 786464 | tf_op jit(solution)/shard_map/ppermute | solution.py:13
  467.6 0.9 copy-done.2
  468.5 1.3 collective-permute-start.1
  469.8 77.5 %collective-permute-done.1 = bf16[768,512]{0,1:T(8,128)(2,1)S(1)} collective-permute-done((bf16[768,512]{0,1:T(8,128)(2,1)S(1)}, bf16[768,512]{0,1:T(8,128)(2,1)S(1)}, u32[]{:S(2)}, u32[]{:S(2)}) %collective-permute-start.1) | collective-permute-done | bytes 786464 | tf_op jit(solution)/shard_map/ppermute | solution.py:13
  547.3 0.9 copy-done.3
  548.2 1.3 collective-permute-start.2
  549.5 106.8 %collective-permute-done.2 = bf16[768,512]{0,1:T(8,128)(2,1)S(1)} collective-permute-done((bf16[768,512]{0,1:T(8,128)(2,1)S(1)}, bf16[768,512]{0,1:T(8,128)(2,1)S(1)}, u32[]{:S(2)}, u32[]{:S(2)}) %collective-permute-start.2) | collective-permute-done | bytes 786464 | tf_op jit(solution)/shard_map/ppermute | solution.py:13
  656.2 0.9 copy-done.4
  657.1 1.3 collective-permute-start.3
  658.4 65.1 %collective-permute-done.3 = bf16[768,512]{0,1:T(8,128)(2,1)S(1)} collective-permute-done((bf16[768,512]{0,1:T(8,128)(2,1)S(1)}, bf16[768,512]{0,1:T(8,128)(2,1)S(1)}, u32[]{:S(2)}, u32[]{:S(2)}) %collective-permute-start.3) | collective-permute-done | bytes 786464 | tf_op jit(solution)/shard_map/ppermute | solution.py:13
  723.5 0.9 copy-done.5
  724.3 1.3 collective-permute-start.4
  725.6 49.6 %collective-permute-done.4 = bf16[768,512]{0,1:T(8,128)(2,1)S(1)} collective-permute-done((bf16[768,512]{0,1:T(8,128)(2,1)S(1)}, bf16[768,512]{0,1:T(8,128)(2,1)S(1)}, u32[]{:S(2)}, u32[]{:S(2)}) %collective-permute-start.4) | collective-permute-done | bytes 786464 | tf_op jit(solution)/shard_map/ppermute | solution.py:13
  775.2 0.9 copy-done.6
  776.1 1.3 collective-permute-start.5
  777.4 48.5 %collective-permute-done.5 = bf16[768,512]{0,1:T(8,128)(2,1)} collective-permute-done((bf16[768,512]{0,1:T(8,128)(2,1)S(1)}, bf16[768,512]{0,1:T(8,128)(2,1)}, u32[]{:S(2)}, u32[]{:S(2)}) %collective-permute-start.5) | collective-permute-done | bytes 786464 | tf_op jit(solution)/shard_map/ppermute | solution.py:13
  825.9 1.3 collective-permute-start.6
  827.2 1.1 fusion.17
  828.3 0.0 all-reduce.4.cloned.1.call-update
  828.3 0.0 all-reduce.6.cloned.1.call-start
  828.3 0.7 dynamic-slice_convert_fusion
  829.0 0.1 copy.21
  829.1 0.8 fusion.16
  830.0 42.3 %collective-permute-done.6 = bf16[768,512]{0,1:T(8,128)(2,1)} collective-permute-done((bf16[768,512]{0,1:T(8,128)(2,1)}, bf16[768,512]{0,1:T(8,128)(2,1)}, u32[]{:S(2)}, u32[]{:S(2)}) %collective-permute-start.6) | collective-permute-done | bytes 786464 | tf_op jit(solution)/shard_map/ppermute | solution.py:13
  872.3 3.6 fusion.18
  875.9 1.2 copy.23
  877.0 126.3 %all-reduce.4.cloned.1.call-done = f32[1,512,32]{1,2,0:T(8,128)} async-done(((f32[1,512,32]{1,2,0:T(8,128)}), f32[1,512,32]{1,2,0:T(8,128)}) %all-reduce.4.cloned.1.call-update) | async-done | bytes 65552 | tf_op jit(solution)/shard_map/psum | solution.py:78
  1003.4 770.6 %all-reduce.6.cloned.1.call-done = f32[1,2,16,1024]{3,2,1,0:T(8,128)} async-done(((f32[1,2,16,1024]{3,2,1,0:T(8,128)}), f32[1,2,16,1024]{3,2,1,0:T(8,128)}) %all-reduce.6.cloned.1.call-update) | async-done | bytes 131088 | tf_op jit(solution)/shard_map/psum | solution.py:85
  1774.0 1.5 copy.30
  1775.5 1.6 copy.31
  (19 shorter events, 0.1 us)
Async XLA Ops:
  8.0 219.1 %copy-start = (bf16[1,512,2048]{2,1,0:T(8,128)(2,1)S(1)}, bf16[1,512,2048]{2,1,0:T(8,128)(2,1)}, u32[]{:S(2)}) copy-start(bf16[1,512,2048]{2,1,0:T(8,128)(2,1)} %param.8) | copy-start | bytes 6291460
  8.0 218.6 %copy-start.9 = (bf16[1,512,32]{1,2,0:T(8,128)(2,1)S(1)}, bf16[1,512,32]{1,2,0:T(8,128)(2,1)}, u32[]{:S(2)}) copy-start(bf16[1,512,32]{1,2,0:T(8,128)(2,1)} %param.9) | copy-start | bytes 98308
  8.0 218.6 %copy-start.10 = (f32[1,512]{1,0:T(1,128)S(1)}, f32[1,512]{1,0:T(1,128)}, u32[]{:S(2)}) copy-start(f32[1,512]{1,0:T(1,128)} %param.11) | copy-start | bytes 6148
  8.0 219.1 %all-gather.3.cloned.1.call-start = ((), (), s32[]{:S(2)}) async-start(), calls=%async_computation.2 | async-start | bytes 3244032 | tf_op jit(solution)/shard_map/all_gather | solution.py:52
  8.8 994.6 %all-reduce.4.cloned.1.call-start = ((), (), s32[]{:S(2)}) async-start(), calls=%async_computation | async-start | bytes 131072 | tf_op jit(solution)/shard_map/psum | solution.py:78
  9.8 1.0 copy-start.7
  444.9 0.9 copy-start.1
  445.8 383.3 %copy-start.8 = (bf16[24,2,1024]{2,1,0:T(2,128)(2,1)S(1)}, bf16[24,2,1024]{2,1,0:T(2,128)(2,1)}, u32[]{:S(2)}) copy-start(bf16[24,2,1024]{2,1,0:T(2,128)(2,1)} %copy-done.7) | copy-start | bytes 294916
  445.8 21.8 %collective-permute-start = (bf16[768,512]{0,1:T(8,128)(2,1)S(1)}, bf16[768,512]{0,1:T(8,128)(2,1)S(1)}, u32[]{:S(2)}, u32[]{:S(2)}) collective-permute-start(bf16[768,512]{0,1:T(8,128)(2,1)S(1)} %fusion.11), channel_id=1, source_target_pairs={{32,0},{64,32},{96,64},{128,96},{160,128},{192,160},{224,192},{33,... | collective-permute-start | bytes 2359304 | tf_op jit(solution)/shard_map/ppermute | solution.py:13
  467.6 0.9 copy-start.2
  468.5 78.8 %collective-permute-start.1 = (bf16[768,512]{0,1:T(8,128)(2,1)S(1)}, bf16[768,512]{0,1:T(8,128)(2,1)S(1)}, u32[]{:S(2)}, u32[]{:S(2)}) collective-permute-start(bf16[768,512]{0,1:T(8,128)(2,1)S(1)} %collective-permute-done), channel_id=1, source_target_pairs={{32,0},{64,32},{96,64},{128,96},{160,128},{192,160},{224,192},{33,... | collective-permute-start | bytes 2359304 | tf_op jit(solution)/shard_map/ppermute | solution.py:13
  547.3 0.9 copy-start.3
  548.2 108.1 %collective-permute-start.2 = (bf16[768,512]{0,1:T(8,128)(2,1)S(1)}, bf16[768,512]{0,1:T(8,128)(2,1)S(1)}, u32[]{:S(2)}, u32[]{:S(2)}) collective-permute-start(bf16[768,512]{0,1:T(8,128)(2,1)S(1)} %collective-permute-done.1), channel_id=1, source_target_pairs={{32,0},{64,32},{96,64},{128,96},{160,128},{192,160},{224,192},{33,... | collective-permute-start | bytes 2359304 | tf_op jit(solution)/shard_map/ppermute | solution.py:13
  656.2 0.9 copy-start.4
  657.1 66.3 %collective-permute-start.3 = (bf16[768,512]{0,1:T(8,128)(2,1)S(1)}, bf16[768,512]{0,1:T(8,128)(2,1)S(1)}, u32[]{:S(2)}, u32[]{:S(2)}) collective-permute-start(bf16[768,512]{0,1:T(8,128)(2,1)S(1)} %collective-permute-done.2), channel_id=1, source_target_pairs={{32,0},{64,32},{96,64},{128,96},{160,128},{192,160},{224,192},{33,... | collective-permute-start | bytes 2359304 | tf_op jit(solution)/shard_map/ppermute | solution.py:13
  723.5 0.9 copy-start.5
  724.3 50.9 %collective-permute-start.4 = (bf16[768,512]{0,1:T(8,128)(2,1)S(1)}, bf16[768,512]{0,1:T(8,128)(2,1)S(1)}, u32[]{:S(2)}, u32[]{:S(2)}) collective-permute-start(bf16[768,512]{0,1:T(8,128)(2,1)S(1)} %collective-permute-done.3), channel_id=1, source_target_pairs={{32,0},{64,32},{96,64},{128,96},{160,128},{192,160},{224,192},{33,... | collective-permute-start | bytes 2359304 | tf_op jit(solution)/shard_map/ppermute | solution.py:13
  775.2 0.9 copy-start.6
  776.1 49.8 %collective-permute-start.5 = (bf16[768,512]{0,1:T(8,128)(2,1)S(1)}, bf16[768,512]{0,1:T(8,128)(2,1)}, u32[]{:S(2)}, u32[]{:S(2)}) collective-permute-start(bf16[768,512]{0,1:T(8,128)(2,1)S(1)} %collective-permute-done.4), channel_id=1, source_target_pairs={{32,0},{64,32},{96,64},{128,96},{160,128},{192,160},{224,192},{33,... | collective-permute-start | bytes 2359304 | tf_op jit(solution)/shard_map/ppermute | solution.py:13
  825.9 46.4 %collective-permute-start.6 = (bf16[768,512]{0,1:T(8,128)(2,1)}, bf16[768,512]{0,1:T(8,128)(2,1)}, u32[]{:S(2)}, u32[]{:S(2)}) collective-permute-start(bf16[768,512]{0,1:T(8,128)(2,1)} %collective-permute-done.5), channel_id=1, source_target_pairs={{32,0},{64,32},{96,64},{128,96},{160,128},{192,160},{224,192},{33,... | collective-permute-start | bytes 2359304 | tf_op jit(solution)/shard_map/ppermute | solution.py:13
  828.3 945.7 %all-reduce.6.cloned.1.call-start = ((), (), s32[]{:S(2)}) async-start(), calls=%async_computation.1 | async-start | bytes 262144 | tf_op jit(solution)/shard_map/psum | solution.py:85
Sparse Core Ops, SparseCore 0:
  10.9 210.6 all-gather.2
Sparse Core Ops, SparseCore 1:
  828.4 175.0 all-reduce.3
  1006.7 767.2 all-reduce.5
where the time goes:
time: 1790 us; the launch traced here: 1780 us
  waiting for transfers between devices  1310 us (73%)
  blocking collectives  425 us (24%)
    psum x1, waiting for transfers between devices, local(): up_gradient_total = lax.psum(up_local, ('dp', 'tensor'))  771 us
    ppermute x7, waiting for transfers between devices, from_behind(): lax.ppermute(value, axis, [(source, source + steps) for source in range(f...  410 us
    psum x1, blocking collectives, local(): lax.psum((jnp.sum(scaled_grad * scaled, axis=1), lowered_part), 'tensor')  211 us
    psum x1, waiting for transfers between devices, local(): down_gradient_total = lax.psum(down_local, 'dp')  126 us
    psum x1, blocking collectives, local(): square_sum = lax.psum(jnp.sum(widened * widened, axis=1), 'tensor')  114 us
    all_gather x1, blocking collectives, local(): hidden_all = lax.all_gather(hidden_own, 'tensor', axis=0, tiled=True)  99.9 us
  transfers between devices with their start and end apart: 10, of which 9 were waited for; matrix products, arithmetic and copies ran while one was open for 1% of the time, Pallas kernels for 0%

commit v1 on v0

v1 whole, which is shorter than its diff:
```python
import jax
import jax.numpy as jnp
from jax import lax
from jax.sharding import PartitionSpec as P

adapter_scale = 2.0
norm_epsilon = 1e-05
rows_x = 4
rows_z = 8


def swap(value, axis, mask):
    count = lax.axis_size(axis)
    return lax.ppermute(value, axis, [(i, i ^ mask) for i in range(count)])


def ordered(mine, other, bit, axis):
    low = jnp.where(bit, other, mine)
    high = jnp.where(bit, mine, other)
    return jnp.stack([low, high], axis=axis)


def y_pairs(pairs):
    return [(2 * a + z, 2 * b + z) for a, b in pairs for z in range(2)]


def y_scan(value, y):
    first = lax.ppermute(value, "section", y_pairs([(3, 2), (2, 3), (1, 0)]))
    pair = (value.astype(jnp.float32) + first.astype(jnp.float32)).astype(jnp.bfloat16)
    second = lax.ppermute(pair, "section", y_pairs([(2, 1), (3, 0)]))
    return jnp.where(y == 3, 0.0, first.astype(jnp.float32)) + second.astype(jnp.float32)


def local(
    layer_saved_input,
    key_value_gradient,
    key_value_weight,
    adapter_down_weight,
    adapter_up_weight,
    attention_norm_scale,
):
    f32, b16 = jnp.float32, jnp.bfloat16
    x = layer_saved_input[0]
    kv_own = key_value_gradient[0]
    weight = key_value_weight[0]
    down_map = adapter_down_weight[0]
    up_map = adapter_up_weight[0]
    gain = attention_norm_scale[0]
    tokens, span = x.shape
    own, kv_width = kv_own.shape
    half = kv_width // 2
    rank_two = down_map.shape[1]
    rank = rank_two // 2
    width = span * lax.axis_size("tensor")
    factor = adapter_scale / (tokens * lax.axis_size("dp"))
    me = lax.axis_index("tensor")
    section = lax.axis_index("section")
    x_at, z_at = me % rows_x, me // rows_x
    y, zh = section // 2, section % 2

    wide = x.astype(f32)
    square = jnp.sum(wide * wide, axis=1)
    gained = (down_map.astype(f32) * gain[:, None]).astype(b16)
    low = lax.dot_general(gained, x, (((0,), (1,)), ((), ())), preferred_element_type=f32)

    def stats_step(low, square, mask):
        top = square.astype(b16)
        rest = (square - top.astype(f32)).astype(b16)
        got = swap(jnp.concatenate([low.astype(b16), top[None], rest[None]], axis=0), "tensor", mask)
        got = got.astype(f32)
        return low + got[:rank_two], square + (got[rank_two] + got[rank_two + 1])

    have = kv_own
    for depth, bit in enumerate((2, 1, 0)):
        other = swap(have, "tensor", rows_x << bit)
        if depth > 0:
            low, square = stats_step(low, square, (1, 3)[depth - 1])
        have = ordered(have, other, (z_at >> bit) & 1 == 1, depth)
        if depth > 0:
            have, low, square = lax.optimization_barrier((have, low, square))
    have = have.reshape(rows_z, 1, own, kv_width)
    kv_all = jnp.zeros((rows_z, rows_x, own, kv_width), b16)
    kv_all = lax.dynamic_update_slice_in_dim(kv_all, have, x_at, 1)
    parts = [swap(have, "tensor", mask) for mask in (1, 3, 2)]
    for mask in (16, 8, 4):
        low, square = stats_step(low, square, mask)
    inverse = lax.rsqrt(square / width + norm_epsilon)
    lowered = (low * inverse[None, :]).astype(b16)
    parts, inverse, lowered = lax.optimization_barrier((parts, inverse, lowered))
    for mask, part in zip((1, 3, 2), parts):
        kv_all = lax.dynamic_update_slice_in_dim(kv_all, part, x_at ^ mask, 1)
    kv_all = kv_all.reshape(tokens, kv_width)

    base = lax.dot_general(kv_all, weight, (((1,), (1,)), ((), ())), preferred_element_type=f32)
    hidden = jnp.concatenate(
        [
            lax.dot_general(
                kv_all[:, c * half : (c + 1) * half], up_map[c], (((1,), (1,)), ((), ())), preferred_element_type=f32
            )
            for c in range(2)
        ],
        axis=1,
    ).astype(b16)
    adapter = lax.dot_general(hidden, down_map, (((1,), (1,)), ((), ())), preferred_element_type=f32)
    scaled_grad = (base + adapter_scale * adapter) * gain[None, :]
    center = jnp.sum(scaled_grad * wide, axis=1)
    for mask in (1, 3, 4, 8, 16):
        center = center + swap(center, "tensor", mask)
    pull = center * (inverse * inverse / width)
    branch = ((scaled_grad - wide * pull[:, None]) * inverse[:, None]).astype(b16)

    cut = tokens // 2
    early, late = branch[:cut], branch[cut:]
    late_other = swap(late, "section", 1).astype(f32)
    early_tail = y_scan(early, y)
    early_sum = early.astype(f32) + early_tail
    early_send = jnp.where(zh == 1, early_sum, early_tail).astype(b16)
    late_pair = late.astype(f32) + late_other
    late_tail = y_scan(late_pair.astype(b16), y)
    late_out = jnp.where(zh == 0, late_pair, late.astype(f32)) + late_tail
    early_out = early_sum + swap(early_send, "section", 1).astype(f32)
    result = jnp.concatenate([early_out.astype(b16), late_out.astype(b16)], axis=0)

    normed_hidden = (hidden.astype(f32) * inverse[:, None]).astype(b16)
    down = lax.dot_general(x, normed_hidden, (((0,), (0,)), ((), ())), preferred_element_type=f32)
    down = down * (factor * gain[:, None])
    down = down + swap(down, "dp", 1)
    up = factor * jnp.stack(
        [
            jnp.dot(
                lowered[c * rank : (c + 1) * rank],
                kv_all[:, c * half : (c + 1) * half],
                preferred_element_type=f32,
            )
            for c in range(2)
        ]
    )
    up = up + swap(up, "dp", 1)
    return (result[None], down[None], up[None])


def solution(mesh):
    in_specs = (
        P("section", "dp", "tensor"),
        P("section", ("dp", "tensor"), None),
        P("section", "tensor", None),
        P("section", "tensor", None),
        P("section", None, None, None),
        P("section", "tensor"),
    )
    out_specs = (
        P("section", "dp", "tensor"),
        P("section", "tensor", None),
        P("section", None, None, None),
    )
    return jax.shard_map(local, mesh=mesh, in_specs=in_specs, out_specs=out_specs, check_vma=False)
```

time: 1790 us -> 262 us (0.15)
  the two profiles are of different devices: /device:TPU:1 before, /device:TPU:160 now
where the time goes in v1:
time: 262 us; the launch traced here: 261 us
  waiting for transfers between devices  162 us (62%)
  starting transfers between devices  81.1 us (31%)
  other arithmetic  8.63 us (3%)
  matrix products  5.79 us (2%)
    ppermute x20, waiting for transfers between devices, swap(): return lax.ppermute(value, axis, [(i, i ^ mask) for i in range(count)])  133 us
    ppermute x20, starting transfers between devices, swap(): return lax.ppermute(value, axis, [(i, i ^ mask) for i in range(count)])  76 us
    ppermute x2, waiting for transfers between devices, y_scan(): first = lax.ppermute(value, 'section', y_pairs([(3, 2), (2, 3), (1, 0)]))  17.2 us
    ppermute x2, waiting for transfers between devices, y_scan(): second = lax.ppermute(pair, 'section', y_pairs([(2, 1), (3, 0)]))  11.1 us
  transfers between devices with their start and end apart: 24, of which 19 were waited for; matrix products, arithmetic and copies ran while one was open for 2% of the time, Pallas kernels for 0%

profile of v1, /device:TPU:160, one launch (start us, length us, event | category | flops | bytes accessed | tf_op | source)
XLA Modules:
  0.0 261.0 jit_solution(7034339668716680929)
XLA Ops:
  0.7 1.5 fusion.2
  2.2 1.5 fusion.65
  3.7 3.4 %collective-permute-start.2 = (bf16[34,768]{1,0:T(8,128)(2,1)S(1)}, bf16[34,768]{1,0:T(8,128)(2,1)S(1)}, u32[]{:S(2)}, u32[]{:S(2)}) collective-permute-start(bf16[34,768]{1,0:T(8,128)(2,1)S(1)} %pad_maximum_fusion.3), channel_id=1, source_target_pairs={{0,1},{1,0},{2,3},{3,2},{4,5},{5,4},{6,7},{7,6},{8,9},{9,8},{10,11... | collective-permute-start | bytes 156680 | tf_op jit(solution)/shard_map/ppermute | solution.py:14
  7.2 1.9 collective-permute-start
  9.9 9.2 %collective-permute-done = bf16[24,2048]{1,0:T(8,128)(2,1)S(1)} collective-permute-done((bf16[24,2048]{1,0:T(8,128)(2,1)S(1)}, bf16[24,2048]{1,0:T(8,128)(2,1)S(1)}, u32[]{:S(2)}, u32[]{:S(2)}) %collective-permute-start) | collective-permute-done | bytes 98336 | tf_op jit(solution)/shard_map/ppermute | solution.py:14
  19.1 8.3 %collective-permute-start.1 = (bf16[2,24,2048]{2,1,0:T(8,128)(2,1)S(1)}, bf16[2,24,2048]{2,1,0:T(8,128)(2,1)S(1)}, u32[]{:S(2)}, u32[]{:S(2)}) collective-permute-start(bf16[2,24,2048]{2,1,0:T(8,128)(2,1)S(1)} %pad_maximum_fusion.2), channel_id=1, source_target_pairs={{0,8},{1,9},{2,10},{3,11},{4,12},{5,13},{6,14},{7,15},{8,0},{9,1},... | collective-permute-start | bytes 589832 | tf_op jit(solution)/shard_map/ppermute | solution.py:14
  27.4 6.4 %collective-permute-done.1 = bf16[2,24,2048]{2,1,0:T(8,128)(2,1)S(1)} collective-permute-done((bf16[2,24,2048]{2,1,0:T(8,128)(2,1)S(1)}, bf16[2,24,2048]{2,1,0:T(8,128)(2,1)S(1)}, u32[]{:S(2)}, u32[]{:S(2)}) %collective-permute-start.1) | collective-permute-done | bytes 196640 | tf_op jit(solution)/shard_map/ppermute | solution.py:14
  34.0 4.0 %collective-permute-start.4 = (bf16[34,768]{1,0:T(8,128)(2,1)S(1)}, bf16[34,768]{1,0:T(8,128)(2,1)S(1)}, u32[]{:S(2)}, u32[]{:S(2)}) collective-permute-start(bf16[34,768]{1,0:T(8,128)(2,1)S(1)} %pad_maximum_fusion.4), channel_id=1, source_target_pairs={{0,3},{1,2},{2,1},{3,0},{4,7},{5,6},{6,5},{7,4},{8,11},{9,10},{10,... | collective-permute-start | bytes 156680 | tf_op jit(solution)/shard_map/ppermute | solution.py:14
  38.0 3.2 %collective-permute-start.3 = (bf16[2,2,24,2048]{3,2,1,0:T(8,128)(2,1)S(1)}, bf16[2,2,24,2048]{3,2,1,0:T(8,128)(2,1)S(1)}, u32[]{:S(2)}, u32[]{:S(2)}) collective-permute-start(bf16[2,2,24,2048]{3,2,1,0:T(8,128)(2,1)S(1)} %pad_maximum_fusion.1), channel_id=1, source_target_pairs={{0,4},{1,5},{2,6},{3,7},{4,0},{5,1},{6,2},{7,3},{8,12},{9,13},{10,... | collective-permute-start | bytes 1179656 | tf_op jit(solution)/shard_map/ppermute | solution.py:14
  41.4 9.3 %collective-permute-done.3 = bf16[2,2,24,2048]{3,2,1,0:T(8,128)(2,1)S(1)} collective-permute-done((bf16[2,2,24,2048]{3,2,1,0:T(8,128)(2,1)S(1)}, bf16[2,2,24,2048]{3,2,1,0:T(8,128)(2,1)S(1)}, u32[]{:S(2)}, u32[]{:S(2)}) %collective-permute-start.3) | collective-permute-done | bytes 393248 | tf_op jit(solution)/shard_map/ppermute | solution.py:14
  50.9 1.9 collective-permute-start.8
  52.8 8.8 %collective-permute-done.8 = bf16[34,768]{1,0:T(8,128)(2,1)S(1)} collective-permute-done((bf16[34,768]{1,0:T(8,128)(2,1)S(1)}, bf16[34,768]{1,0:T(8,128)(2,1)S(1)}, u32[]{:S(2)}, u32[]{:S(2)}) %collective-permute-start.8) | collective-permute-done | bytes 52256 | tf_op jit(solution)/shard_map/ppermute | solution.py:14
  61.8 5.7 %collective-permute-start.9 = (bf16[34,768]{1,0:T(8,128)(2,1)S(1)}, bf16[34,768]{1,0:T(8,128)(2,1)S(1)}, u32[]{:S(2)}, u32[]{:S(2)}) collective-permute-start(bf16[34,768]{1,0:T(8,128)(2,1)S(1)} %pad_maximum_fusion.6), channel_id=1, source_target_pairs={{0,8},{1,9},{2,10},{3,11},{4,12},{5,13},{6,14},{7,15},{8,0},{9,1},... | collective-permute-start | bytes 156680 | tf_op jit(solution)/shard_map/ppermute | solution.py:14
  67.6 2.5 collective-permute-start.5
  70.1 3.1 %collective-permute-start.6 = (bf16[8,1,24,2048]{3,2,0,1:T(8,128)(2,1)S(1)}, bf16[8,1,24,2048]{3,2,0,1:T(8,128)(2,1)S(1)}, u32[]{:S(2)}, u32[]{:S(2)}) collective-permute-start(bf16[8,1,24,2048]{3,2,0,1:T(8,128)(2,1)S(1)} %bitcast.78), channel_id=1, source_target_pairs={{0,3},{1,2},{2,1},{3,0},{4,7},{5,6},{6,5},{7,4},{8,11},{9,10},{10,... | collective-permute-start | bytes 2359304 | tf_op jit(solution)/shard_map/ppermute | solution.py:14
  73.2 4.2 %collective-permute-start.7 = (bf16[8,1,24,2048]{3,2,0,1:T(8,128)(2,1)S(1)}, bf16[8,1,24,2048]{3,2,0,1:T(8,128)(2,1)S(1)}, u32[]{:S(2)}, u32[]{:S(2)}) collective-permute-start(bf16[8,1,24,2048]{3,2,0,1:T(8,128)(2,1)S(1)} %bitcast.79), channel_id=1, source_target_pairs={{0,2},{1,3},{2,0},{3,1},{4,6},{5,7},{6,4},{7,5},{8,10},{9,11},{10,... | collective-permute-start | bytes 2359304 | tf_op jit(solution)/shard_map/ppermute | solution.py:14
  77.6 1.9 collective-permute-start.10
  80.0 3.7 %collective-permute-done.10 = bf16[34,768]{1,0:T(8,128)(2,1)S(1)} collective-permute-done((bf16[34,768]{1,0:T(8,128)(2,1)S(1)}, bf16[34,768]{1,0:T(8,128)(2,1)S(1)}, u32[]{:S(2)}, u32[]{:S(2)}) %collective-permute-start.10) | collective-permute-done | bytes 52256 | tf_op jit(solution)/shard_map/ppermute | solution.py:14
  83.8 6.2 %collective-permute-done.5 = bf16[8,1,24,2048]{3,2,0,1:T(8,128)(2,1)S(1)} collective-permute-done((bf16[8,1,24,2048]{3,2,0,1:T(8,128)(2,1)S(1)}, bf16[8,1,24,2048]{3,2,0,1:T(8,128)(2,1)S(1)}, u32[]{:S(2)}, u32[]{:S(2)}) %collective-permute-start.5) | collective-permute-done | bytes 786464 | tf_op jit(solution)/shard_map/ppermute | solution.py:14
  89.9 18.6 %collective-permute-done.6 = bf16[8,1,24,2048]{3,2,0,1:T(8,128)(2,1)S(1)} collective-permute-done((bf16[8,1,24,2048]{3,2,0,1:T(8,128)(2,1)S(1)}, bf16[8,1,24,2048]{3,2,0,1:T(8,128)(2,1)S(1)}, u32[]{:S(2)}, u32[]{:S(2)}) %collective-permute-start.6) | collective-permute-done | bytes 786464 | tf_op jit(solution)/shard_map/ppermute | solution.py:14
  110.5 1.8 fusion
  113.0 2.1 collective-permute-start.11
  115.1 3.4 %collective-permute-done.11 = f32[768]{0:T(1024)S(1)} collective-permute-done((f32[768]{0:T(1024)S(1)}, f32[768]{0:T(1024)S(1)}, u32[]{:S(2)}, u32[]{:S(2)}) %collective-permute-start.11) | collective-permute-done | bytes 3104 | tf_op jit(solution)/shard_map/ppermute | solution.py:14
  118.5 3.5 %collective-permute-start.12 = (f32[768]{0:T(1024)S(1)}, f32[768]{0:T(1024)S(1)}, u32[]{:S(2)}, u32[]{:S(2)}) collective-permute-start(f32[768]{0:T(1024)S(1)} %add.163), channel_id=1, source_target_pairs={{0,3},{1,2},{2,1},{3,0},{4,7},{5,6},{6,5},{7,4},{8,11},{9,10},{10,... | collective-permute-start | bytes 9224 | tf_op jit(solution)/shard_map/ppermute | solution.py:14
  122.0 3.2 %collective-permute-done.12 = f32[768]{0:T(1024)S(1)} collective-permute-done((f32[768]{0:T(1024)S(1)}, f32[768]{0:T(1024)S(1)}, u32[]{:S(2)}, u32[]{:S(2)}) %collective-permute-start.12) | collective-permute-done | bytes 3104 | tf_op jit(solution)/shard_map/ppermute | solution.py:14
  125.2 1.9 collective-permute-start.13
  127.1 3.6 %collective-permute-done.13 = f32[768]{0:T(1024)S(1)} collective-permute-done((f32[768]{0:T(1024)S(1)}, f32[768]{0:T(1024)S(1)}, u32[]{:S(2)}, u32[]{:S(2)}) %collective-permute-start.13) | collective-permute-done | bytes 3104 | tf_op jit(solution)/shard_map/ppermute | solution.py:14
  130.7 2.2 collective-permute-start.14
  132.9 4.2 %collective-permute-done.14 = f32[768]{0:T(1024)S(1)} collective-permute-done((f32[768]{0:T(1024)S(1)}, f32[768]{0:T(1024)S(1)}, u32[]{:S(2)}, u32[]{:S(2)}) %collective-permute-start.14) | collective-permute-done | bytes 3104 | tf_op jit(solution)/shard_map/ppermute | solution.py:14
  137.1 1.9 collective-permute-start.15
  139.0 7.5 %collective-permute-done.15 = f32[768]{0:T(1024)S(1)} collective-permute-done((f32[768]{0:T(1024)S(1)}, f32[768]{0:T(1024)S(1)}, u32[]{:S(2)}, u32[]{:S(2)}) %collective-permute-start.15) | collective-permute-done | bytes 3104 | tf_op jit(solution)/shard_map/ppermute | solution.py:14
  146.9 0.9 fusion.64
  147.7 1.3 collective-permute-start.16
  149.0 8.4 %collective-permute-done.16 = bf16[384,512]{1,0:T(8,128)(2,1)S(1)} collective-permute-done((bf16[384,512]{1,0:T(8,128)(2,1)S(1)}, bf16[384,512]{1,0:T(8,128)(2,1)S(1)}, u32[]{:S(2)}, u32[]{:S(2)}) %collective-permute-start.16) | collective-permute-done | bytes 393248 | tf_op jit(solution)/shard_map/ppermute | solution.py:28
  158.2 1.3 collective-permute-start.17
  159.6 10.3 %collective-permute-start.19 = (bf16[384,512]{1,0:T(8,128)(2,1)}, bf16[384,512]{1,0:T(8,128)(2,1)S(1)}, u32[]{:S(2)}, u32[]{:S(2)}) collective-permute-start(bf16[384,512]{1,0:T(8,128)(2,1)} %get-tuple-element.38), channel_id=1, source_target_pairs={{0,32},{32,0},{64,96},{96,64},{128,160},{160,128},{192,224},{224,1... | collective-permute-start | bytes 1179656 | tf_op jit(solution)/shard_map/ppermute | solution.py:14
  169.9 1.3 fusion.30
  171.2 9.7 %collective-permute-start.18 = (bf16[384,512]{1,0:T(8,128)(2,1)S(1)}, bf16[384,512]{1,0:T(8,128)(2,1)S(1)}, u32[]{:S(2)}, u32[]{:S(2)}) collective-permute-start(bf16[384,512]{1,0:T(8,128)(2,1)S(1)} %fusion.30), channel_id=1, source_target_pairs={{0,32},{32,0},{64,96},{96,64},{128,160},{160,128},{192,224},{224,1... | collective-permute-start | bytes 1179656 | tf_op jit(solution)/shard_map/ppermute | solution.py:14
  181.2 2.2 collective-permute-start.22
  183.4 35.8 %collective-permute-done.19 = bf16[384,512]{1,0:T(8,128)(2,1)S(1)} collective-permute-done((bf16[384,512]{1,0:T(8,128)(2,1)}, bf16[384,512]{1,0:T(8,128)(2,1)S(1)}, u32[]{:S(2)}, u32[]{:S(2)}) %collective-permute-start.19) | collective-permute-done | bytes 393248 | tf_op jit(solution)/shard_map/ppermute | solution.py:14
  219.2 12.7 %collective-permute-done.18 = bf16[384,512]{1,0:T(8,128)(2,1)S(1)} collective-permute-done((bf16[384,512]{1,0:T(8,128)(2,1)S(1)}, bf16[384,512]{1,0:T(8,128)(2,1)S(1)}, u32[]{:S(2)}, u32[]{:S(2)}) %collective-permute-start.18) | collective-permute-done | bytes 393248 | tf_op jit(solution)/shard_map/ppermute | solution.py:14
  231.9 1.3 fusion.31
  233.3 1.3 collective-permute-start.20
  235.2 1.9 collective-permute-start.23
  237.2 8.8 %collective-permute-done.20 = bf16[384,512]{1,0:T(8,128)(2,1)S(1)} collective-permute-done((bf16[384,512]{1,0:T(8,128)(2,1)S(1)}, bf16[384,512]{1,0:T(8,128)(2,1)S(1)}, u32[]{:S(2)}, u32[]{:S(2)}) %collective-permute-start.20) | collective-permute-done | bytes 393248 | tf_op jit(solution)/shard_map/ppermute | solution.py:28
  246.1 1.3 collective-permute-start.21
  248.7 11.1 %collective-permute-done.21 = bf16[384,512]{1,0:T(8,128)(2,1)S(1)} collective-permute-done((bf16[384,512]{1,0:T(8,128)(2,1)S(1)}, bf16[384,512]{1,0:T(8,128)(2,1)S(1)}, u32[]{:S(2)}, u32[]{:S(2)}) %collective-permute-start.21) | collective-permute-done | bytes 393248 | tf_op jit(solution)/shard_map/ppermute | solution.py:30
  260.1 0.9 maximum_bitcast_fusion
  (96 shorter events, 8.3 us)
Async XLA Ops:
  0.6 109.9 %copy-start = (bf16[1,512,2048]{2,1,0:T(8,128)(2,1)S(1)}, bf16[1,512,2048]{2,1,0:T(8,128)(2,1)}, u32[]{:S(2)}) copy-start(bf16[1,512,2048]{2,1,0:T(8,128)(2,1)} %param.8) | copy-start | bytes 6291460
  0.6 6.5 %copy-start.7 = (bf16[1,24,2048]{2,1,0:T(8,128)(2,1)S(1)}, bf16[1,24,2048]{2,1,0:T(8,128)(2,1)}, u32[]{:S(2)}) copy-start(bf16[1,24,2048]{2,1,0:T(8,128)(2,1)} %param.7) | copy-start | bytes 294916
  3.7 6.1 %collective-permute-start.2 = (bf16[34,768]{1,0:T(8,128)(2,1)S(1)}, bf16[34,768]{1,0:T(8,128)(2,1)S(1)}, u32[]{:S(2)}, u32[]{:S(2)}) collective-permute-start(bf16[34,768]{1,0:T(8,128)(2,1)S(1)} %pad_maximum_fusion.3), channel_id=1, source_target_pairs={{0,1},{1,0},{2,3},{3,2},{4,5},{5,4},{6,7},{7,6},{8,9},{9,8},{10,11... | collective-permute-start | bytes 156680 | tf_op jit(solution)/shard_map/ppermute | solution.py:14
  7.2 11.9 %collective-permute-start = (bf16[24,2048]{1,0:T(8,128)(2,1)S(1)}, bf16[24,2048]{1,0:T(8,128)(2,1)S(1)}, u32[]{:S(2)}, u32[]{:S(2)}) collective-permute-start(bf16[24,2048]{1,0:T(8,128)(2,1)S(1)} %bitcast.81), channel_id=1, source_target_pairs={{0,16},{1,17},{2,18},{3,19},{4,20},{5,21},{6,22},{7,23},{8,24},{9,... | collective-permute-start | bytes 294920 | tf_op jit(solution)/shard_map/ppermute | solution.py:14
  19.1 14.8 %collective-permute-start.1 = (bf16[2,24,2048]{2,1,0:T(8,128)(2,1)S(1)}, bf16[2,24,2048]{2,1,0:T(8,128)(2,1)S(1)}, u32[]{:S(2)}, u32[]{:S(2)}) collective-permute-start(bf16[2,24,2048]{2,1,0:T(8,128)(2,1)S(1)} %pad_maximum_fusion.2), channel_id=1, source_target_pairs={{0,8},{1,9},{2,10},{3,11},{4,12},{5,13},{6,14},{7,15},{8,0},{9,1},... | collective-permute-start | bytes 589832 | tf_op jit(solution)/shard_map/ppermute | solution.py:14
  34.0 7.3 %collective-permute-start.4 = (bf16[34,768]{1,0:T(8,128)(2,1)S(1)}, bf16[34,768]{1,0:T(8,128)(2,1)S(1)}, u32[]{:S(2)}, u32[]{:S(2)}) collective-permute-start(bf16[34,768]{1,0:T(8,128)(2,1)S(1)} %pad_maximum_fusion.4), channel_id=1, source_target_pairs={{0,3},{1,2},{2,1},{3,0},{4,7},{5,6},{6,5},{7,4},{8,11},{9,10},{10,... | collective-permute-start | bytes 156680 | tf_op jit(solution)/shard_map/ppermute | solution.py:14
  38.0 12.7 %collective-permute-start.3 = (bf16[2,2,24,2048]{3,2,1,0:T(8,128)(2,1)S(1)}, bf16[2,2,24,2048]{3,2,1,0:T(8,128)(2,1)S(1)}, u32[]{:S(2)}, u32[]{:S(2)}) collective-permute-start(bf16[2,2,24,2048]{3,2,1,0:T(8,128)(2,1)S(1)} %pad_maximum_fusion.1), channel_id=1, source_target_pairs={{0,4},{1,5},{2,6},{3,7},{4,0},{5,1},{6,2},{7,3},{8,12},{9,13},{10,... | collective-permute-start | bytes 1179656 | tf_op jit(solution)/shard_map/ppermute | solution.py:14
  50.9 10.7 %collective-permute-start.8 = (bf16[34,768]{1,0:T(8,128)(2,1)S(1)}, bf16[34,768]{1,0:T(8,128)(2,1)S(1)}, u32[]{:S(2)}, u32[]{:S(2)}) collective-permute-start(bf16[34,768]{1,0:T(8,128)(2,1)S(1)} %pad_maximum_fusion.5), channel_id=1, source_target_pairs={{0,16},{1,17},{2,18},{3,19},{4,20},{5,21},{6,22},{7,23},{8,24},{9,... | collective-permute-start | bytes 156680 | tf_op jit(solution)/shard_map/ppermute | solution.py:14
  61.8 15.6 %collective-permute-start.9 = (bf16[34,768]{1,0:T(8,128)(2,1)S(1)}, bf16[34,768]{1,0:T(8,128)(2,1)S(1)}, u32[]{:S(2)}, u32[]{:S(2)}) collective-permute-start(bf16[34,768]{1,0:T(8,128)(2,1)S(1)} %pad_maximum_fusion.6), channel_id=1, source_target_pairs={{0,8},{1,9},{2,10},{3,11},{4,12},{5,13},{6,14},{7,15},{8,0},{9,1},... | collective-permute-start | bytes 156680 | tf_op jit(solution)/shard_map/ppermute | solution.py:14
  67.6 22.4 %collective-permute-start.5 = (bf16[8,1,24,2048]{3,2,0,1:T(8,128)(2,1)S(1)}, bf16[8,1,24,2048]{3,2,0,1:T(8,128)(2,1)S(1)}, u32[]{:S(2)}, u32[]{:S(2)}) collective-permute-start(bf16[8,1,24,2048]{3,2,0,1:T(8,128)(2,1)S(1)} %bitcast.77), channel_id=1, source_target_pairs={{0,1},{1,0},{2,3},{3,2},{4,5},{5,4},{6,7},{7,6},{8,9},{9,8},{10,11... | collective-permute-start | bytes 2359304 | tf_op jit(solution)/shard_map/ppermute | solution.py:14
  70.1 38.5 %collective-permute-start.6 = (bf16[8,1,24,2048]{3,2,0,1:T(8,128)(2,1)S(1)}, bf16[8,1,24,2048]{3,2,0,1:T(8,128)(2,1)S(1)}, u32[]{:S(2)}, u32[]{:S(2)}) collective-permute-start(bf16[8,1,24,2048]{3,2,0,1:T(8,128)(2,1)S(1)} %bitcast.78), channel_id=1, source_target_pairs={{0,3},{1,2},{2,1},{3,0},{4,7},{5,6},{6,5},{7,4},{8,11},{9,10},{10,... | collective-permute-start | bytes 2359304 | tf_op jit(solution)/shard_map/ppermute | solution.py:14
  73.2 35.3 %collective-permute-start.7 = (bf16[8,1,24,2048]{3,2,0,1:T(8,128)(2,1)S(1)}, bf16[8,1,24,2048]{3,2,0,1:T(8,128)(2,1)S(1)}, u32[]{:S(2)}, u32[]{:S(2)}) collective-permute-start(bf16[8,1,24,2048]{3,2,0,1:T(8,128)(2,1)S(1)} %bitcast.79), channel_id=1, source_target_pairs={{0,2},{1,3},{2,0},{3,1},{4,6},{5,7},{6,4},{7,5},{8,10},{9,11},{10,... | collective-permute-start | bytes 2359304 | tf_op jit(solution)/shard_map/ppermute | solution.py:14
  77.6 6.1 %collective-permute-start.10 = (bf16[34,768]{1,0:T(8,128)(2,1)S(1)}, bf16[34,768]{1,0:T(8,128)(2,1)S(1)}, u32[]{:S(2)}, u32[]{:S(2)}) collective-permute-start(bf16[34,768]{1,0:T(8,128)(2,1)S(1)} %pad_maximum_fusion.7), channel_id=1, source_target_pairs={{0,4},{1,5},{2,6},{3,7},{4,0},{5,1},{6,2},{7,3},{8,12},{9,13},{10,... | collective-permute-start | bytes 156680 | tf_op jit(solution)/shard_map/ppermute | solution.py:14
  108.6 0.8 copy-start.9
  108.8 1.7 copy-start.4
  110.5 1.9 copy-start.1
  110.5 1.9 copy-start.6
  110.5 1.9 copy-start.8
  113.0 5.5 %collective-permute-start.11 = (f32[768]{0:T(1024)S(1)}, f32[768]{0:T(1024)S(1)}, u32[]{:S(2)}, u32[]{:S(2)}) collective-permute-start(f32[768]{0:T(1024)S(1)} %get-tuple-element.47), channel_id=1, source_target_pairs={{0,1},{1,0},{2,3},{3,2},{4,5},{5,4},{6,7},{7,6},{8,9},{9,8},{10,11... | collective-permute-start | bytes 9224 | tf_op jit(solution)/shard_map/ppermute | solution.py:14
  118.5 6.7 %collective-permute-start.12 = (f32[768]{0:T(1024)S(1)}, f32[768]{0:T(1024)S(1)}, u32[]{:S(2)}, u32[]{:S(2)}) collective-permute-start(f32[768]{0:T(1024)S(1)} %add.163), channel_id=1, source_target_pairs={{0,3},{1,2},{2,1},{3,0},{4,7},{5,6},{6,5},{7,4},{8,11},{9,10},{10,... | collective-permute-start | bytes 9224 | tf_op jit(solution)/shard_map/ppermute | solution.py:14
  125.2 5.5 %collective-permute-start.13 = (f32[768]{0:T(1024)S(1)}, f32[768]{0:T(1024)S(1)}, u32[]{:S(2)}, u32[]{:S(2)}) collective-permute-start(f32[768]{0:T(1024)S(1)} %add.164), channel_id=1, source_target_pairs={{0,4},{1,5},{2,6},{3,7},{4,0},{5,1},{6,2},{7,3},{8,12},{9,13},{10,... | collective-permute-start | bytes 9224 | tf_op jit(solution)/shard_map/ppermute | solution.py:14
  130.7 6.4 %collective-permute-start.14 = (f32[768]{0:T(1024)S(1)}, f32[768]{0:T(1024)S(1)}, u32[]{:S(2)}, u32[]{:S(2)}) collective-permute-start(f32[768]{0:T(1024)S(1)} %add.165), channel_id=1, source_target_pairs={{0,8},{1,9},{2,10},{3,11},{4,12},{5,13},{6,14},{7,15},{8,0},{9,1},... | collective-permute-start | bytes 9224 | tf_op jit(solution)/shard_map/ppermute | solution.py:14
  137.1 9.4 %collective-permute-start.15 = (f32[768]{0:T(1024)S(1)}, f32[768]{0:T(1024)S(1)}, u32[]{:S(2)}, u32[]{:S(2)}) collective-permute-start(f32[768]{0:T(1024)S(1)} %add.166), channel_id=1, source_target_pairs={{0,16},{1,17},{2,18},{3,19},{4,20},{5,21},{6,22},{7,23},{8,24},{9,... | collective-permute-start | bytes 9224 | tf_op jit(solution)/shard_map/ppermute | solution.py:14
  146.8 10.5 %copy-start.2 = (bf16[768,512]{1,0:T(8,128)(2,1)}, bf16[768,512]{1,0:T(8,128)(2,1)S(1)}, u32[]{:S(2)}) copy-start(bf16[768,512]{1,0:T(8,128)(2,1)S(1)} %fusion.6) | copy-start | bytes 2359300
  147.7 9.7 %collective-permute-start.16 = (bf16[384,512]{1,0:T(8,128)(2,1)S(1)}, bf16[384,512]{1,0:T(8,128)(2,1)S(1)}, u32[]{:S(2)}, u32[]{:S(2)}) collective-permute-start(bf16[384,512]{1,0:T(8,128)(2,1)S(1)} %get-tuple-element.37), channel_id=1, source_target_pairs={{192,128},{224,160},{128,192},{160,224},{64,0},{96,32},{193,129},{... | collective-permute-start | bytes 1179656 | tf_op jit(solution)/shard_map/ppermute | solution.py:28
  158.2 11.7 %collective-permute-start.17 = (bf16[384,512]{1,0:T(8,128)(2,1)}, bf16[384,512]{1,0:T(8,128)(2,1)}, u32[]{:S(2)}, u32[]{:S(2)}) collective-permute-start(bf16[384,512]{1,0:T(8,128)(2,1)} %fusion.33), channel_id=1, source_target_pairs={{128,64},{160,96},{192,0},{224,32},{129,65},{161,97},{193,1},{225,... | collective-permute-start | bytes 1179656 | tf_op jit(solution)/shard_map/ppermute | solution.py:30
  159.6 72.4 %copy-start.3 = (bf16[768,512]{1,0:T(8,128)(2,1)S(1)}, bf16[768,512]{1,0:T(8,128)(2,1)}, u32[]{:S(2)}) copy-start(bf16[768,512]{1,0:T(8,128)(2,1)} %copy-done.2) | copy-start | bytes 2359300
  159.6 59.6 %collective-permute-start.19 = (bf16[384,512]{1,0:T(8,128)(2,1)}, bf16[384,512]{1,0:T(8,128)(2,1)S(1)}, u32[]{:S(2)}, u32[]{:S(2)}) collective-permute-start(bf16[384,512]{1,0:T(8,128)(2,1)} %get-tuple-element.38), channel_id=1, source_target_pairs={{0,32},{32,0},{64,96},{96,64},{128,160},{160,128},{192,224},{224,1... | collective-permute-start | bytes 1179656 | tf_op jit(solution)/shard_map/ppermute | solution.py:14
  171.2 60.7 %collective-permute-start.18 = (bf16[384,512]{1,0:T(8,128)(2,1)S(1)}, bf16[384,512]{1,0:T(8,128)(2,1)S(1)}, u32[]{:S(2)}, u32[]{:S(2)}) collective-permute-start(bf16[384,512]{1,0:T(8,128)(2,1)S(1)} %fusion.30), channel_id=1, source_target_pairs={{0,32},{32,0},{64,96},{96,64},{128,160},{160,128},{192,224},{224,1... | collective-permute-start | bytes 1179656 | tf_op jit(solution)/shard_map/ppermute | solution.py:14
  181.2 53.4 %copy-start.5 = (bf16[8,4,24,2048]{3,2,1,0:T(8,128)(2,1)S(1)}, bf16[8,4,24,2048]{3,2,1,0:T(8,128)(2,1)}, u32[]{:S(2)}) copy-start(bf16[8,4,24,2048]{3,2,1,0:T(8,128)(2,1)} %copy-done.4) | copy-start | bytes 9437188
  181.2 66.2 %collective-permute-start.22 = (f32[512,32]{0,1:T(8,128)S(1)}, f32[512,32]{0,1:T(8,128)S(1)}, u32[]{:S(2)}, u32[]{:S(2)}) collective-permute-start(f32[512,32]{0,1:T(8,128)S(1)} %fusion.21), channel_id=1, source_target_pairs={{0,256},{256,0},{1,257},{257,1},{2,258},{258,2},{3,259},{259,3},{4... | collective-permute-start | bytes 196616 | tf_op jit(solution)/shard_map/ppermute | solution.py:14
  233.3 12.7 %collective-permute-start.20 = (bf16[384,512]{1,0:T(8,128)(2,1)S(1)}, bf16[384,512]{1,0:T(8,128)(2,1)S(1)}, u32[]{:S(2)}, u32[]{:S(2)}) collective-permute-start(bf16[384,512]{1,0:T(8,128)(2,1)S(1)} %get-tuple-element.36), channel_id=1, source_target_pairs={{192,128},{224,160},{128,192},{160,224},{64,0},{96,32},{193,129},{... | collective-permute-start | bytes 1179656 | tf_op jit(solution)/shard_map/ppermute | solution.py:28
  235.2 12.8 %collective-permute-start.23 = (f32[2,16,1024]{2,1,0:T(8,128)S(1)}, f32[2,16,1024]{2,1,0:T(8,128)S(1)}, u32[]{:S(2)}, u32[]{:S(2)}) collective-permute-start(f32[2,16,1024]{2,1,0:T(8,128)S(1)} %maximum_multiply_fusion), channel_id=1, source_target_pairs={{0,256},{256,0},{1,257},{257,1},{2,258},{258,2},{3,259},{259,3},{4... | collective-permute-start | bytes 393224 | tf_op jit(solution)/shard_map/ppermute | solution.py:14
  246.1 13.8 %collective-permute-start.21 = (bf16[384,512]{1,0:T(8,128)(2,1)S(1)}, bf16[384,512]{1,0:T(8,128)(2,1)S(1)}, u32[]{:S(2)}, u32[]{:S(2)}) collective-permute-start(bf16[384,512]{1,0:T(8,128)(2,1)S(1)} %fusion.37), channel_id=1, source_target_pairs={{128,64},{160,96},{192,0},{224,32},{129,65},{161,97},{193,1},{225,... | collective-permute-start | bytes 1179656 | tf_op jit(solution)/shard_map/ppermute | solution.py:30

commit v2 on v1

v2 whole, which is shorter than its diff:
```python
import jax
import jax.numpy as jnp
from jax import lax
from jax.sharding import Mesh, PartitionSpec as P

adapter_scale = 2.0
norm_epsilon = 1e-05
sizes = {"dp": 2, "y": 4, "zh": 2, "zl": 8, "x": 4}
section_axes = ("y", "zh")
tensor_axes = ("zl", "x")
together = lax.optimization_barrier


def swap(value, axis, mask):
    count = lax.axis_size(axis)
    return lax.ppermute(value, axis, [(i, i ^ mask) for i in range(count)])


def ordered(mine, other, bit, axis):
    low = jnp.where(bit, other, mine)
    high = jnp.where(bit, mine, other)
    return jnp.stack([low, high], axis=axis)


def y_first(value):
    return lax.ppermute(value, "y", [(3, 2), (2, 3), (1, 0)])


def y_second(value):
    return lax.ppermute(value, "y", [(2, 1), (3, 0)])


def local(
    layer_saved_input,
    key_value_gradient,
    key_value_weight,
    adapter_down_weight,
    adapter_up_weight,
    attention_norm_scale,
):
    f32, b16 = jnp.float32, jnp.bfloat16
    x = layer_saved_input[0]
    kv_own = key_value_gradient[0]
    weight = key_value_weight[0]
    down_map = adapter_down_weight[0]
    up_map = adapter_up_weight[0]
    gain = attention_norm_scale[0]
    tokens, span = x.shape
    own, kv_width = kv_own.shape
    half = kv_width // 2
    rank_two = down_map.shape[1]
    rank = rank_two // 2
    width = span * lax.axis_size(tensor_axes)
    factor = adapter_scale / (tokens * lax.axis_size("dp"))
    x_at, z_at = lax.axis_index("x"), lax.axis_index("zl")
    y, zh = lax.axis_index("y"), lax.axis_index("zh")

    wide = x.astype(f32)
    gained = (down_map.astype(f32) * gain[:, None]).astype(b16)
    low = lax.dot_general(gained, x, (((0,), (1,)), ((), ())), preferred_element_type=f32)

    def low_step(low, axis, mask):
        return low + swap(low.astype(b16), axis, mask).astype(f32)

    kv_all = jnp.zeros((2, 2, 2, sizes["x"], own, kv_width), b16)
    bits = [(z_at >> i) & 1 for i in range(3)]

    def place(kv_all, part, middle, bit, at):
        part = part.reshape((2, -1, 1, 1, own, kv_width))
        return lax.dynamic_update_slice(kv_all, part, (0, middle, bit, at, 0, 0))

    other = swap(kv_own, "zl", 4)
    two = ordered(kv_own, other, bits[2] == 1, 0)
    square = jnp.sum(wide * wide, axis=1)
    two, low, square = together((two, low, square))

    other_two = swap(two, "zl", 2)
    parts = [swap(two, "x", mask) for mask in (2, 1, 3)]
    low = low_step(low, "zl", 4)
    other_two, parts, low = together((other_two, parts, low))
    for mask, part in zip((2, 1, 3), parts):
        kv_all = place(kv_all, part, bits[1], bits[0], x_at ^ mask)
    far = parts[0]

    four = ordered(two, other_two, bits[1] == 1, 1)
    other_four = swap(four, "zl", 1)
    parts = [swap(other_two, "x", mask) for mask in (2, 1, 3)]
    low = low_step(low, "zl", 2)
    other_four, parts, low = together((other_four, parts, low))
    kv_all = place(kv_all, four, 0, bits[0], x_at)
    kv_all = place(kv_all, other_four, 0, 1 - bits[0], x_at)
    for mask, part in zip((2, 1, 3), parts):
        kv_all = place(kv_all, part, 1 - bits[1], bits[0], x_at ^ mask)
    far = ordered(far, parts[0], bits[1] == 1, 1)

    parts = [swap(far, "zl", 1)] + [swap(other_four, "x", mask) for mask in (1, 3)]
    low = low_step(low, "zl", 1)
    parts, low = together((parts, low))
    for mask, part in zip((2, 1, 3), parts):
        kv_all = place(kv_all, part, 0, 1 - bits[0], x_at ^ mask)
    kv_all = kv_all.reshape(tokens, kv_width)

    base = lax.dot_general(kv_all, weight, (((1,), (1,)), ((), ())), preferred_element_type=f32)
    hidden = jnp.concatenate(
        [
            lax.dot_general(
                kv_all[:, c * half : (c + 1) * half], up_map[c], (((1,), (1,)), ((), ())), preferred_element_type=f32
            )
            for c in range(2)
        ],
        axis=1,
    ).astype(b16)
    adapter = lax.dot_general(hidden, down_map, (((1,), (1,)), ((), ())), preferred_element_type=f32)
    scaled_grad = (base + adapter_scale * adapter) * gain[None, :]
    center = jnp.sum(scaled_grad * wide, axis=1)
    square, center = reduce_rows(jnp.stack([square, center]))
    inverse = lax.rsqrt(square / width + norm_epsilon)
    pull = center * (inverse * inverse / width)
    branch = ((scaled_grad - wide * pull[:, None]) * inverse[:, None]).astype(b16)

    cut = tokens // 2
    early, late = branch[:cut], branch[cut:]
    late_other = swap(late, "zh", 1)
    early_one = y_first(early)
    low = low_step(low, "x", 1)
    late_other, early_one, low = together((late_other, early_one, low))
    late_pair = late.astype(f32) + late_other.astype(f32)
    early_pair = early.astype(f32) + early_one.astype(f32)
    early_two = y_second(early_pair.astype(b16))
    late_sent = late_pair.astype(b16)
    late_one = y_first(late_sent)
    low = low_step(low, "x", 3)
    early_two, late_one, low = together((early_two, late_one, low))
    lowered = (low * inverse[None, :]).astype(b16)
    early_tail = jnp.where(y == 3, 0.0, early_one.astype(f32)) + early_two.astype(f32)
    early_sum = early.astype(f32) + early_tail
    early_other = swap(jnp.where(zh == 1, early_sum, early_tail).astype(b16), "zh", 1)
    late_two = y_second((late_sent.astype(f32) + late_one.astype(f32)).astype(b16))
    late_tail = jnp.where(y == 3, 0.0, late_one.astype(f32)) + late_two.astype(f32)
    late_out = jnp.where(zh == 0, late_pair, late.astype(f32)) + late_tail
    early_out = early_sum + early_other.astype(f32)
    result = jnp.concatenate([early_out.astype(b16), late_out.astype(b16)], axis=0)

    normed_hidden = (hidden.astype(f32) * inverse[:, None]).astype(b16)
    down = lax.dot_general(x, normed_hidden, (((0,), (0,)), ((), ())), preferred_element_type=f32)
    down = down * (factor * gain[:, None])
    down = down + swap(down, "dp", 1)
    up = factor * jnp.stack(
        [
            jnp.dot(
                lowered[c * rank : (c + 1) * rank],
                kv_all[:, c * half : (c + 1) * half],
                preferred_element_type=f32,
            )
            for c in range(2)
        ]
    )
    up = up + swap(up, "dp", 1)
    return (result[None], down[None], up[None])


def reduce_rows(rows):
    rows = lax.psum(rows, "x")
    count = sizes["zl"]
    spread = jnp.broadcast_to(rows.reshape(1, -1, 128), (count, rows.size // 128, 128))
    return jnp.sum(lax.all_to_all(spread, "zl", 0, 0), axis=0).reshape(rows.shape)


def solution(mesh):
    mesh = Mesh(mesh.devices.reshape(tuple(sizes.values())), tuple(sizes))
    in_specs = (
        P(section_axes, "dp", tensor_axes),
        P(section_axes, ("dp",) + tensor_axes, None),
        P(section_axes, tensor_axes, None),
        P(section_axes, tensor_axes, None),
        P(section_axes, None, None, None),
        P(section_axes, tensor_axes),
    )
    out_specs = (
        P(section_axes, "dp", tensor_axes),
        P(section_axes, tensor_axes, None),
        P(section_axes, None, None, None),
    )
    return jax.shard_map(local, mesh=mesh, in_specs=in_specs, out_specs=out_specs, check_vma=False)
```

time: 262 us -> 216 us (0.82)
  the two profiles are of different devices: /device:TPU:160 before, /device:TPU:81 now
where the time goes in v2:
time: 216 us; the launch traced here: 215 us
  starting transfers between devices  115 us (53%)
  waiting for transfers between devices  72.4 us (34%)
  other arithmetic  9.85 us (5%)
  matrix products  6.9 us (3%)
  blocking collectives  6.48 us (3%)
  local copies, waits for them, and re-layouts  3.2 us (1%)
    ppermute x21, starting transfers between devices, swap(): return lax.ppermute(value, axis, [(i, i ^ mask) for i in range(count)])  102 us
    ppermute x21, waiting for transfers between devices, swap(): return lax.ppermute(value, axis, [(i, i ^ mask) for i in range(count)])  68.1 us
    psum x1, blocking collectives, reduce_rows(): rows = lax.psum(rows, 'x')  6.48 us
    ppermute x2, starting transfers between devices, y_first(): return lax.ppermute(value, 'y', [(3, 2), (2, 3), (1, 0)])  5.6 us
    all_to_all x1, waiting for transfers between devices, reduce_rows(): lax.all_to_all(spread, 'zl', 0, 0)  4.32 us
  transfers between devices with their start and end apart: 26, of which 9 were waited for; matrix products, arithmetic and copies ran while one was open for 4% of the time, Pallas kernels for 0%

profile of v2, /device:TPU:81, one launch (start us, length us, event | category | flops | bytes accessed | tf_op | source)
XLA Modules:
  0.0 215.0 jit_solution(1480974559324489506)
XLA Ops:
  0.6 9.0 %collective-permute-start = (bf16[24,2048]{1,0:T(8,128)(2,1)}, bf16[24,2048]{1,0:T(8,128)(2,1)S(1)}, u32[]{:S(2)}, u32[]{:S(2)}) collective-permute-start(bf16[24,2048]{1,0:T(8,128)(2,1)} %bitcast.111), channel_id=1, source_target_pairs={{0,16},{4,20},{8,24},{12,28},{16,0},{20,4},{24,8},{28,12},{1,17},{... | collective-permute-start | bytes 294920 | tf_op jit(solution)/shard_map/ppermute | solution.py:16
  9.6 1.5 fusion.39
  11.1 1.4 fusion.2
  12.5 3.3 %collective-permute-done = bf16[24,2048]{1,0:T(8,128)(2,1)S(1)} collective-permute-done((bf16[24,2048]{1,0:T(8,128)(2,1)}, bf16[24,2048]{1,0:T(8,128)(2,1)S(1)}, u32[]{:S(2)}, u32[]{:S(2)}) %collective-permute-start) | collective-permute-done | bytes 98336 | tf_op jit(solution)/shard_map/ppermute | solution.py:16
  15.8 0.9 select_bitcast_fusion.5
  16.7 7.9 %collective-permute-start.5 = (bf16[32,768]{1,0:T(8,128)(2,1)S(1)}, bf16[32,768]{1,0:T(8,128)(2,1)S(1)}, u32[]{:S(2)}, u32[]{:S(2)}) collective-permute-start(bf16[32,768]{1,0:T(8,128)(2,1)S(1)} %convert_element_type.109), channel_id=1, source_target_pairs={{0,16},{4,20},{8,24},{12,28},{16,0},{20,4},{24,8},{28,12},{1,17},{... | collective-permute-start | bytes 147464 | tf_op jit(solution)/shard_map/ppermute | solution.py:16
  24.7 1.9 collective-permute-start.1
  26.6 4.7 %collective-permute-start.2 = (bf16[2,24,2048]{2,1,0:T(8,128)(2,1)S(1)}, bf16[2,24,2048]{2,1,0:T(8,128)(2,1)S(1)}, u32[]{:S(2)}, u32[]{:S(2)}) collective-permute-start(bf16[2,24,2048]{2,1,0:T(8,128)(2,1)S(1)} %pad_maximum_fusion.2), channel_id=1, source_target_pairs={{0,2},{1,3},{2,0},{3,1},{4,6},{5,7},{6,4},{7,5},{8,10},{9,11},{10,... | collective-permute-start | bytes 589832 | tf_op jit(solution)/shard_map/ppermute | solution.py:16
  31.3 2.2 %collective-permute-start.3 = (bf16[2,24,2048]{2,1,0:T(8,128)(2,1)S(1)}, bf16[2,24,2048]{2,1,0:T(8,128)(2,1)S(1)}, u32[]{:S(2)}, u32[]{:S(2)}) collective-permute-start(bf16[2,24,2048]{2,1,0:T(8,128)(2,1)S(1)} %pad_maximum_fusion.2), channel_id=1, source_target_pairs={{0,1},{1,0},{2,3},{3,2},{4,5},{5,4},{6,7},{7,6},{8,9},{9,8},{10,11... | collective-permute-start | bytes 589832 | tf_op jit(solution)/shard_map/ppermute | solution.py:16
  33.5 2.5 %collective-permute-start.4 = (bf16[2,24,2048]{2,1,0:T(8,128)(2,1)S(1)}, bf16[2,24,2048]{2,1,0:T(8,128)(2,1)S(1)}, u32[]{:S(2)}, u32[]{:S(2)}) collective-permute-start(bf16[2,24,2048]{2,1,0:T(8,128)(2,1)S(1)} %pad_maximum_fusion.2), channel_id=1, source_target_pairs={{0,3},{1,2},{2,1},{3,0},{4,7},{5,6},{6,5},{7,4},{8,11},{9,10},{10,... | collective-permute-start | bytes 589832 | tf_op jit(solution)/shard_map/ppermute | solution.py:16
  36.0 4.1 %collective-permute-done.3 = bf16[2,24,2048]{2,1,0:T(8,128)(2,1)S(1)} collective-permute-done((bf16[2,24,2048]{2,1,0:T(8,128)(2,1)S(1)}, bf16[2,24,2048]{2,1,0:T(8,128)(2,1)S(1)}, u32[]{:S(2)}, u32[]{:S(2)}) %collective-permute-start.3) | collective-permute-done | bytes 196640 | tf_op jit(solution)/shard_map/ppermute | solution.py:16
  40.1 1.5 collective-permute-done.4
  41.6 3.6 %collective-permute-start.7 = (bf16[2,24,2048]{2,1,0:T(8,128)(2,1)S(1)}, bf16[2,24,2048]{2,1,0:T(8,128)(2,1)S(1)}, u32[]{:S(2)}, u32[]{:S(2)}) collective-permute-start(bf16[2,24,2048]{2,1,0:T(8,128)(2,1)S(1)} %collective-permute-done.1), channel_id=1, source_target_pairs={{0,2},{1,3},{2,0},{3,1},{4,6},{5,7},{6,4},{7,5},{8,10},{9,11},{10,... | collective-permute-start | bytes 589832 | tf_op jit(solution)/shard_map/ppermute | solution.py:16
  45.2 2.3 %collective-permute-start.8 = (bf16[2,24,2048]{2,1,0:T(8,128)(2,1)S(1)}, bf16[2,24,2048]{2,1,0:T(8,128)(2,1)S(1)}, u32[]{:S(2)}, u32[]{:S(2)}) collective-permute-start(bf16[2,24,2048]{2,1,0:T(8,128)(2,1)S(1)} %collective-permute-done.1), channel_id=1, source_target_pairs={{0,1},{1,0},{2,3},{3,2},{4,5},{5,4},{6,7},{7,6},{8,9},{9,8},{10,11... | collective-permute-start | bytes 589832 | tf_op jit(solution)/shard_map/ppermute | solution.py:16
  47.5 3.1 %collective-permute-start.9 = (bf16[2,24,2048]{2,1,0:T(8,128)(2,1)S(1)}, bf16[2,24,2048]{2,1,0:T(8,128)(2,1)S(1)}, u32[]{:S(2)}, u32[]{:S(2)}) collective-permute-start(bf16[2,24,2048]{2,1,0:T(8,128)(2,1)S(1)} %collective-permute-done.1), channel_id=1, source_target_pairs={{0,3},{1,2},{2,1},{3,0},{4,7},{5,6},{6,5},{7,4},{8,11},{9,10},{10,... | collective-permute-start | bytes 589832 | tf_op jit(solution)/shard_map/ppermute | solution.py:16
  50.7 5.2 %collective-permute-start.6 = (bf16[2,2,24,2048]{3,2,1,0:T(8,128)(2,1)S(1)}, bf16[2,2,24,2048]{3,2,1,0:T(8,128)(2,1)S(1)}, u32[]{:S(2)}, u32[]{:S(2)}) collective-permute-start(bf16[2,2,24,2048]{3,2,1,0:T(8,128)(2,1)S(1)} %pad_maximum_fusion), channel_id=1, source_target_pairs={{0,4},{4,0},{8,12},{12,8},{16,20},{20,16},{24,28},{28,24},{1,5},{5... | collective-permute-start | bytes 1179656 | tf_op jit(solution)/shard_map/ppermute | solution.py:16
  55.9 3.7 %collective-permute-start.10 = (bf16[32,768]{1,0:T(8,128)(2,1)S(1)}, bf16[32,768]{1,0:T(8,128)(2,1)S(1)}, u32[]{:S(2)}, u32[]{:S(2)}) collective-permute-start(bf16[32,768]{1,0:T(8,128)(2,1)S(1)} %convert_element_type.111), channel_id=1, source_target_pairs={{0,8},{4,12},{8,0},{12,4},{16,24},{20,28},{24,16},{28,20},{1,9},{5... | collective-permute-start | bytes 147464 | tf_op jit(solution)/shard_map/ppermute | solution.py:16
  60.2 3.8 %collective-permute-done.10 = bf16[32,768]{1,0:T(8,128)(2,1)S(1)} collective-permute-done((bf16[32,768]{1,0:T(8,128)(2,1)S(1)}, bf16[32,768]{1,0:T(8,128)(2,1)S(1)}, u32[]{:S(2)}, u32[]{:S(2)}) %collective-permute-start.10) | collective-permute-done | bytes 49184 | tf_op jit(solution)/shard_map/ppermute | solution.py:16
  64.0 3.1 %collective-permute-start.12 = (bf16[2,2,24,2048]{3,2,1,0:T(8,128)(2,1)S(1)}, bf16[2,2,24,2048]{3,2,1,0:T(8,128)(2,1)S(1)}, u32[]{:S(2)}, u32[]{:S(2)}) collective-permute-start(bf16[2,2,24,2048]{3,2,1,0:T(8,128)(2,1)S(1)} %collective-permute-done.6), channel_id=1, source_target_pairs={{0,1},{1,0},{2,3},{3,2},{4,5},{5,4},{6,7},{7,6},{8,9},{9,8},{10,11... | collective-permute-start | bytes 1179656 | tf_op jit(solution)/shard_map/ppermute | solution.py:16
  67.1 4.2 %collective-permute-start.13 = (bf16[2,2,24,2048]{3,2,1,0:T(8,128)(2,1)S(1)}, bf16[2,2,24,2048]{3,2,1,0:T(8,128)(2,1)S(1)}, u32[]{:S(2)}, u32[]{:S(2)}) collective-permute-start(bf16[2,2,24,2048]{3,2,1,0:T(8,128)(2,1)S(1)} %collective-permute-done.6), channel_id=1, source_target_pairs={{0,3},{1,2},{2,1},{3,0},{4,7},{5,6},{6,5},{7,4},{8,11},{9,10},{10,... | collective-permute-start | bytes 1179656 | tf_op jit(solution)/shard_map/ppermute | solution.py:16
  71.4 1.9 collective-permute-start.11
  73.3 3.4 %collective-permute-start.14 = (bf16[32,768]{1,0:T(8,128)(2,1)S(1)}, bf16[32,768]{1,0:T(8,128)(2,1)S(1)}, u32[]{:S(2)}, u32[]{:S(2)}) collective-permute-start(bf16[32,768]{1,0:T(8,128)(2,1)S(1)} %convert_element_type.113), channel_id=1, source_target_pairs={{0,4},{4,0},{8,12},{12,8},{16,20},{20,16},{24,28},{28,24},{1,5},{5... | collective-permute-start | bytes 147464 | tf_op jit(solution)/shard_map/ppermute | solution.py:16
  76.8 3.9 %collective-permute-done.14 = bf16[32,768]{1,0:T(8,128)(2,1)S(1)} collective-permute-done((bf16[32,768]{1,0:T(8,128)(2,1)S(1)}, bf16[32,768]{1,0:T(8,128)(2,1)S(1)}, u32[]{:S(2)}, u32[]{:S(2)}) %collective-permute-start.14) | collective-permute-done | bytes 49184 | tf_op jit(solution)/shard_map/ppermute | solution.py:16
  82.0 1.8 fusion
  83.9 1.7 fusion.3
  85.6 6.5 %psum.7 = f32[12,128]{1,0:T(8,128)S(1)} all-reduce(f32[12,128]{1,0:T(8,128)S(1)} %broadcast_in_dim.29), channel_id=1, replica_groups=mesh['dp'=2,'y'=4,'zh'=2,'zl'=8,'x'=4] {'x'}, use_global_device_ids=true, to_apply=%region_2.3 | all-reduce | flops 1536 | bytes 12288 | tf_op jit(solution)/shard_map/psum | solution.py:163
  92.7 3.6 %all-to-all-start = ((f32[8,12,128]{2,1,0:T(8,128)}), f32[8,12,128]{2,1,0:T(8,128)S(1)}, u32[]{:S(2)}, u32[]{:S(2)}) async-start(f32[8,12,128]{2,1,0:T(8,128)} %broadcast_in_dim.30), calls=%async_computation | async-start | bytes 131072 | tf_op jit(solution)/shard_map/all_to_all | solution.py:166
  96.4 3.0 %collective-permute-start.17 = (bf16[32,768]{1,0:T(8,128)(2,1)S(1)}, bf16[32,768]{1,0:T(8,128)(2,1)S(1)}, u32[]{:S(2)}, u32[]{:S(2)}) collective-permute-start(bf16[32,768]{1,0:T(8,128)(2,1)S(1)} %convert_element_type.117), channel_id=1, source_target_pairs={{0,1},{1,0},{2,3},{3,2},{4,5},{5,4},{6,7},{7,6},{8,9},{9,8},{10,11... | collective-permute-start | bytes 147464 | tf_op jit(solution)/shard_map/ppermute | solution.py:16
  99.4 4.3 %all-to-all-done = f32[8,12,128]{2,1,0:T(8,128)S(1)} async-done(((f32[8,12,128]{2,1,0:T(8,128)}), f32[8,12,128]{2,1,0:T(8,128)S(1)}, u32[]{:S(2)}, u32[]{:S(2)}) %all-to-all-start) | async-done | bytes 49184 | tf_op jit(solution)/shard_map/all_to_all | solution.py:166
  103.7 1.7 fusion.6
  105.5 0.9 copy-done.2
  106.4 0.9 fusion.59
  107.3 11.2 %collective-permute-start.15 = (bf16[384,512]{1,0:T(8,128)(2,1)}, bf16[384,512]{1,0:T(8,128)(2,1)}, u32[]{:S(2)}, u32[]{:S(2)}) collective-permute-start(bf16[384,512]{1,0:T(8,128)(2,1)} %get-tuple-element.54), channel_id=1, source_target_pairs={{0,32},{32,0},{1,33},{33,1},{2,34},{34,2},{3,35},{35,3},{4,36},{36... | collective-permute-start | bytes 1179656 | tf_op jit(solution)/shard_map/ppermute | solution.py:16
  118.5 2.9 %collective-permute-start.16 = (bf16[384,512]{1,0:T(8,128)(2,1)}, bf16[384,512]{1,0:T(8,128)(2,1)S(1)}, u32[]{:S(2)}, u32[]{:S(2)}) collective-permute-start(bf16[384,512]{1,0:T(8,128)(2,1)} %get-tuple-element.53), channel_id=1, source_target_pairs={{192,128},{128,192},{64,0},{193,129},{129,193},{65,1},{194,130},{1... | collective-permute-start | bytes 1179656 | tf_op jit(solution)/shard_map/ppermute | solution.py:26
  121.5 21.9 %collective-permute-done.15 = bf16[384,512]{1,0:T(8,128)(2,1)} collective-permute-done((bf16[384,512]{1,0:T(8,128)(2,1)}, bf16[384,512]{1,0:T(8,128)(2,1)}, u32[]{:S(2)}, u32[]{:S(2)}) %collective-permute-start.15) | collective-permute-done | bytes 393248 | tf_op jit(solution)/shard_map/ppermute | solution.py:16
  143.4 1.4 fusion.41
  144.8 2.1 collective-permute-start.18
  147.0 2.7 %collective-permute-start.19 = (bf16[384,512]{1,0:T(8,128)(2,1)S(1)}, bf16[384,512]{1,0:T(8,128)(2,1)S(1)}, u32[]{:S(2)}, u32[]{:S(2)}) collective-permute-start(bf16[384,512]{1,0:T(8,128)(2,1)S(1)} %get-tuple-element.51), channel_id=1, source_target_pairs={{192,128},{128,192},{64,0},{193,129},{129,193},{65,1},{194,130},{1... | collective-permute-start | bytes 1179656 | tf_op jit(solution)/shard_map/ppermute | solution.py:26
  149.7 3.1 %collective-permute-start.20 = (bf16[32,768]{1,0:T(8,128)(2,1)S(1)}, bf16[32,768]{1,0:T(8,128)(2,1)S(1)}, u32[]{:S(2)}, u32[]{:S(2)}) collective-permute-start(bf16[32,768]{1,0:T(8,128)(2,1)S(1)} %convert_element_type.124), channel_id=1, source_target_pairs={{0,3},{1,2},{2,1},{3,0},{4,7},{5,6},{6,5},{7,4},{8,11},{9,10},{10,... | collective-permute-start | bytes 147464 | tf_op jit(solution)/shard_map/ppermute | solution.py:16
  153.0 13.2 %collective-permute-start.23 = (f32[512,32]{0,1:T(8,128)S(1)}, f32[512,32]{0,1:T(8,128)S(1)}, u32[]{:S(2)}, u32[]{:S(2)}) collective-permute-start(f32[512,32]{0,1:T(8,128)S(1)} %fusion.21), channel_id=1, source_target_pairs={{0,256},{256,0},{1,257},{257,1},{2,258},{258,2},{3,259},{259,3},{4... | collective-permute-start | bytes 196616 | tf_op jit(solution)/shard_map/ppermute | solution.py:16
  167.2 8.6 %collective-permute-start.21 = (bf16[384,512]{1,0:T(8,128)(2,1)S(1)}, bf16[384,512]{1,0:T(8,128)(2,1)S(1)}, u32[]{:S(2)}, u32[]{:S(2)}) collective-permute-start(bf16[384,512]{1,0:T(8,128)(2,1)S(1)} %fusion.30), channel_id=1, source_target_pairs={{0,32},{32,0},{1,33},{33,1},{2,34},{34,2},{3,35},{35,3},{4,36},{36... | collective-permute-start | bytes 1179656 | tf_op jit(solution)/shard_map/ppermute | solution.py:16
  175.9 1.3 collective-permute-start.22
  177.2 4.4 %collective-permute-start.24 = (f32[2,16,1024]{2,1,0:T(8,128)S(1)}, f32[2,16,1024]{2,1,0:T(8,128)S(1)}, u32[]{:S(2)}, u32[]{:S(2)}) collective-permute-start(f32[2,16,1024]{2,1,0:T(8,128)S(1)} %maximum_multiply_fusion), channel_id=1, source_target_pairs={{0,256},{256,0},{1,257},{257,1},{2,258},{258,2},{3,259},{259,3},{4... | collective-permute-start | bytes 393224 | tf_op jit(solution)/shard_map/ppermute | solution.py:16
  181.6 0.6 add_bitcast_fusion.1
  182.6 0.7 add_bitcast_fusion
  183.3 29.3 %collective-permute-done.21 = bf16[384,512]{1,0:T(8,128)(2,1)S(1)} collective-permute-done((bf16[384,512]{1,0:T(8,128)(2,1)S(1)}, bf16[384,512]{1,0:T(8,128)(2,1)S(1)}, u32[]{:S(2)}, u32[]{:S(2)}) %collective-permute-start.21) | collective-permute-done | bytes 393248 | tf_op jit(solution)/shard_map/ppermute | solution.py:16
  212.6 1.5 fusion.31
  214.0 0.9 maximum_bitcast_fusion
  (80 shorter events, 4.3 us)
Async XLA Ops:
  0.6 81.3 %copy-start = (bf16[1,512,2048]{2,1,0:T(8,128)(2,1)S(1)}, bf16[1,512,2048]{2,1,0:T(8,128)(2,1)}, u32[]{:S(2)}) copy-start(bf16[1,512,2048]{2,1,0:T(8,128)(2,1)} %param.8) | copy-start | bytes 6291460
  0.6 15.1 %collective-permute-start = (bf16[24,2048]{1,0:T(8,128)(2,1)}, bf16[24,2048]{1,0:T(8,128)(2,1)S(1)}, u32[]{:S(2)}, u32[]{:S(2)}) collective-permute-start(bf16[24,2048]{1,0:T(8,128)(2,1)} %bitcast.111), channel_id=1, source_target_pairs={{0,16},{4,20},{8,24},{12,28},{16,0},{20,4},{24,8},{28,12},{1,17},{... | collective-permute-start | bytes 294920 | tf_op jit(solution)/shard_map/ppermute | solution.py:16
  16.7 19.3 %collective-permute-start.5 = (bf16[32,768]{1,0:T(8,128)(2,1)S(1)}, bf16[32,768]{1,0:T(8,128)(2,1)S(1)}, u32[]{:S(2)}, u32[]{:S(2)}) collective-permute-start(bf16[32,768]{1,0:T(8,128)(2,1)S(1)} %convert_element_type.109), channel_id=1, source_target_pairs={{0,16},{4,20},{8,24},{12,28},{16,0},{20,4},{24,8},{28,12},{1,17},{... | collective-permute-start | bytes 147464 | tf_op jit(solution)/shard_map/ppermute | solution.py:16
  24.7 11.3 %collective-permute-start.1 = (bf16[2,24,2048]{2,1,0:T(8,128)(2,1)S(1)}, bf16[2,24,2048]{2,1,0:T(8,128)(2,1)S(1)}, u32[]{:S(2)}, u32[]{:S(2)}) collective-permute-start(bf16[2,24,2048]{2,1,0:T(8,128)(2,1)S(1)} %pad_maximum_fusion.2), channel_id=1, source_target_pairs={{0,8},{4,12},{8,0},{12,4},{16,24},{20,28},{24,16},{28,20},{1,9},{5... | collective-permute-start | bytes 589832 | tf_op jit(solution)/shard_map/ppermute | solution.py:16
  26.6 9.4 %collective-permute-start.2 = (bf16[2,24,2048]{2,1,0:T(8,128)(2,1)S(1)}, bf16[2,24,2048]{2,1,0:T(8,128)(2,1)S(1)}, u32[]{:S(2)}, u32[]{:S(2)}) collective-permute-start(bf16[2,24,2048]{2,1,0:T(8,128)(2,1)S(1)} %pad_maximum_fusion.2), channel_id=1, source_target_pairs={{0,2},{1,3},{2,0},{3,1},{4,6},{5,7},{6,4},{7,5},{8,10},{9,11},{10,... | collective-permute-start | bytes 589832 | tf_op jit(solution)/shard_map/ppermute | solution.py:16
  31.3 8.9 %collective-permute-start.3 = (bf16[2,24,2048]{2,1,0:T(8,128)(2,1)S(1)}, bf16[2,24,2048]{2,1,0:T(8,128)(2,1)S(1)}, u32[]{:S(2)}, u32[]{:S(2)}) collective-permute-start(bf16[2,24,2048]{2,1,0:T(8,128)(2,1)S(1)} %pad_maximum_fusion.2), channel_id=1, source_target_pairs={{0,1},{1,0},{2,3},{3,2},{4,5},{5,4},{6,7},{7,6},{8,9},{9,8},{10,11... | collective-permute-start | bytes 589832 | tf_op jit(solution)/shard_map/ppermute | solution.py:16
  33.5 8.1 %collective-permute-start.4 = (bf16[2,24,2048]{2,1,0:T(8,128)(2,1)S(1)}, bf16[2,24,2048]{2,1,0:T(8,128)(2,1)S(1)}, u32[]{:S(2)}, u32[]{:S(2)}) collective-permute-start(bf16[2,24,2048]{2,1,0:T(8,128)(2,1)S(1)} %pad_maximum_fusion.2), channel_id=1, source_target_pairs={{0,3},{1,2},{2,1},{3,0},{4,7},{5,6},{6,5},{7,4},{8,11},{9,10},{10,... | collective-permute-start | bytes 589832 | tf_op jit(solution)/shard_map/ppermute | solution.py:16
  41.6 22.4 %collective-permute-start.7 = (bf16[2,24,2048]{2,1,0:T(8,128)(2,1)S(1)}, bf16[2,24,2048]{2,1,0:T(8,128)(2,1)S(1)}, u32[]{:S(2)}, u32[]{:S(2)}) collective-permute-start(bf16[2,24,2048]{2,1,0:T(8,128)(2,1)S(1)} %collective-permute-done.1), channel_id=1, source_target_pairs={{0,2},{1,3},{2,0},{3,1},{4,6},{5,7},{6,4},{7,5},{8,10},{9,11},{10,... | collective-permute-start | bytes 589832 | tf_op jit(solution)/shard_map/ppermute | solution.py:16
  45.2 18.8 %collective-permute-start.8 = (bf16[2,24,2048]{2,1,0:T(8,128)(2,1)S(1)}, bf16[2,24,2048]{2,1,0:T(8,128)(2,1)S(1)}, u32[]{:S(2)}, u32[]{:S(2)}) collective-permute-start(bf16[2,24,2048]{2,1,0:T(8,128)(2,1)S(1)} %collective-permute-done.1), channel_id=1, source_target_pairs={{0,1},{1,0},{2,3},{3,2},{4,5},{5,4},{6,7},{7,6},{8,9},{9,8},{10,11... | collective-permute-start | bytes 589832 | tf_op jit(solution)/shard_map/ppermute | solution.py:16
  47.5 16.5 %collective-permute-start.9 = (bf16[2,24,2048]{2,1,0:T(8,128)(2,1)S(1)}, bf16[2,24,2048]{2,1,0:T(8,128)(2,1)S(1)}, u32[]{:S(2)}, u32[]{:S(2)}) collective-permute-start(bf16[2,24,2048]{2,1,0:T(8,128)(2,1)S(1)} %collective-permute-done.1), channel_id=1, source_target_pairs={{0,3},{1,2},{2,1},{3,0},{4,7},{5,6},{6,5},{7,4},{8,11},{9,10},{10,... | collective-permute-start | bytes 589832 | tf_op jit(solution)/shard_map/ppermute | solution.py:16
  50.7 13.3 %collective-permute-start.6 = (bf16[2,2,24,2048]{3,2,1,0:T(8,128)(2,1)S(1)}, bf16[2,2,24,2048]{3,2,1,0:T(8,128)(2,1)S(1)}, u32[]{:S(2)}, u32[]{:S(2)}) collective-permute-start(bf16[2,2,24,2048]{3,2,1,0:T(8,128)(2,1)S(1)} %pad_maximum_fusion), channel_id=1, source_target_pairs={{0,4},{4,0},{8,12},{12,8},{16,20},{20,16},{24,28},{28,24},{1,5},{5... | collective-permute-start | bytes 1179656 | tf_op jit(solution)/shard_map/ppermute | solution.py:16
  55.9 8.0 %collective-permute-start.10 = (bf16[32,768]{1,0:T(8,128)(2,1)S(1)}, bf16[32,768]{1,0:T(8,128)(2,1)S(1)}, u32[]{:S(2)}, u32[]{:S(2)}) collective-permute-start(bf16[32,768]{1,0:T(8,128)(2,1)S(1)} %convert_element_type.111), channel_id=1, source_target_pairs={{0,8},{4,12},{8,0},{12,4},{16,24},{20,28},{24,16},{28,20},{1,9},{5... | collective-permute-start | bytes 147464 | tf_op jit(solution)/shard_map/ppermute | solution.py:16
  64.0 17.0 %copy-start.8 = (bf16[1,2,16,1024]{3,2,1,0:T(8,128)(2,1)S(1)}, bf16[1,2,16,1024]{3,2,1,0:T(8,128)(2,1)}, u32[]{:S(2)}) copy-start(bf16[1,2,16,1024]{3,2,1,0:T(8,128)(2,1)} %param.10) | copy-start | bytes 196612
  64.0 16.7 %collective-permute-start.12 = (bf16[2,2,24,2048]{3,2,1,0:T(8,128)(2,1)S(1)}, bf16[2,2,24,2048]{3,2,1,0:T(8,128)(2,1)S(1)}, u32[]{:S(2)}, u32[]{:S(2)}) collective-permute-start(bf16[2,2,24,2048]{3,2,1,0:T(8,128)(2,1)S(1)} %collective-permute-done.6), channel_id=1, source_target_pairs={{0,1},{1,0},{2,3},{3,2},{4,5},{5,4},{6,7},{7,6},{8,9},{9,8},{10,11... | collective-permute-start | bytes 1179656 | tf_op jit(solution)/shard_map/ppermute | solution.py:16
  67.1 13.7 %collective-permute-start.13 = (bf16[2,2,24,2048]{3,2,1,0:T(8,128)(2,1)S(1)}, bf16[2,2,24,2048]{3,2,1,0:T(8,128)(2,1)S(1)}, u32[]{:S(2)}, u32[]{:S(2)}) collective-permute-start(bf16[2,2,24,2048]{3,2,1,0:T(8,128)(2,1)S(1)} %collective-permute-done.6), channel_id=1, source_target_pairs={{0,3},{1,2},{2,1},{3,0},{4,7},{5,6},{6,5},{7,4},{8,11},{9,10},{10,... | collective-permute-start | bytes 1179656 | tf_op jit(solution)/shard_map/ppermute | solution.py:16
  71.4 9.4 %collective-permute-start.11 = (bf16[2,2,24,2048]{3,2,0,1:T(8,128)(2,1)S(1)}, bf16[2,2,24,2048]{3,2,0,1:T(8,128)(2,1)S(1)}, u32[]{:S(2)}, u32[]{:S(2)}) collective-permute-start(bf16[2,2,24,2048]{3,2,0,1:T(8,128)(2,1)S(1)} %pad_maximum_fusion.1), channel_id=1, source_target_pairs={{0,4},{4,0},{8,12},{12,8},{16,20},{20,16},{24,28},{28,24},{1,5},{5... | collective-permute-start | bytes 1179656 | tf_op jit(solution)/shard_map/ppermute | solution.py:16
  73.3 7.4 %collective-permute-start.14 = (bf16[32,768]{1,0:T(8,128)(2,1)S(1)}, bf16[32,768]{1,0:T(8,128)(2,1)S(1)}, u32[]{:S(2)}, u32[]{:S(2)}) collective-permute-start(bf16[32,768]{1,0:T(8,128)(2,1)S(1)} %convert_element_type.113), channel_id=1, source_target_pairs={{0,4},{4,0},{8,12},{12,8},{16,20},{20,16},{24,28},{28,24},{1,5},{5... | collective-permute-start | bytes 147464 | tf_op jit(solution)/shard_map/ppermute | solution.py:16
  80.9 2.9 %copy-start.4 = (bf16[2,2,2,4,24,2048]{5,4,3,2,1,0:T(8,128)(2,1)}, bf16[2,2,2,4,24,2048]{5,4,3,2,1,0:T(8,128)(2,1)S(1)}, u32[]{:S(2)}) copy-start(bf16[2,2,2,4,24,2048]{5,4,3,2,1,0:T(8,128)(2,1)S(1)} %bitcast_dynamic-update-slice_fusion.3) | copy-start | bytes 9437188
  82.0 1.9 copy-start.1
  82.0 1.9 copy-start.6
  82.0 1.9 copy-start.7
  92.7 11.0 %all-to-all-start = ((f32[8,12,128]{2,1,0:T(8,128)}), f32[8,12,128]{2,1,0:T(8,128)S(1)}, u32[]{:S(2)}, u32[]{:S(2)}) async-start(f32[8,12,128]{2,1,0:T(8,128)} %broadcast_in_dim.30), calls=%async_computation | async-start | bytes 131072 | tf_op jit(solution)/shard_map/all_to_all | solution.py:166
  96.4 25.1 %collective-permute-start.17 = (bf16[32,768]{1,0:T(8,128)(2,1)S(1)}, bf16[32,768]{1,0:T(8,128)(2,1)S(1)}, u32[]{:S(2)}, u32[]{:S(2)}) collective-permute-start(bf16[32,768]{1,0:T(8,128)(2,1)S(1)} %convert_element_type.117), channel_id=1, source_target_pairs={{0,1},{1,0},{2,3},{3,2},{4,5},{5,4},{6,7},{7,6},{8,9},{9,8},{10,11... | collective-permute-start | bytes 147464 | tf_op jit(solution)/shard_map/ppermute | solution.py:16
  105.5 0.9 copy-start.2
  107.3 36.1 %collective-permute-start.15 = (bf16[384,512]{1,0:T(8,128)(2,1)}, bf16[384,512]{1,0:T(8,128)(2,1)}, u32[]{:S(2)}, u32[]{:S(2)}) collective-permute-start(bf16[384,512]{1,0:T(8,128)(2,1)} %get-tuple-element.54), channel_id=1, source_target_pairs={{0,32},{32,0},{1,33},{33,1},{2,34},{34,2},{3,35},{35,3},{4,36},{36... | collective-permute-start | bytes 1179656 | tf_op jit(solution)/shard_map/ppermute | solution.py:16
  118.5 24.9 %collective-permute-start.16 = (bf16[384,512]{1,0:T(8,128)(2,1)}, bf16[384,512]{1,0:T(8,128)(2,1)S(1)}, u32[]{:S(2)}, u32[]{:S(2)}) collective-permute-start(bf16[384,512]{1,0:T(8,128)(2,1)} %get-tuple-element.53), channel_id=1, source_target_pairs={{192,128},{128,192},{64,0},{193,129},{129,193},{65,1},{194,130},{1... | collective-permute-start | bytes 1179656 | tf_op jit(solution)/shard_map/ppermute | solution.py:26
  121.4 44.9 %copy-start.5 = (bf16[2,2,2,4,24,2048]{5,4,3,2,1,0:T(8,128)(2,1)S(1)}, bf16[2,2,2,4,24,2048]{5,4,3,2,1,0:T(8,128)(2,1)}, u32[]{:S(2)}) copy-start(bf16[2,2,2,4,24,2048]{5,4,3,2,1,0:T(8,128)(2,1)} %copy-done.4) | copy-start | bytes 9437188
  121.5 45.5 %copy-start.3 = (bf16[768,512]{1,0:T(8,128)(2,1)S(1)}, bf16[768,512]{1,0:T(8,128)(2,1)}, u32[]{:S(2)}) copy-start(bf16[768,512]{1,0:T(8,128)(2,1)} %copy-done.2) | copy-start | bytes 2359300
  144.8 21.4 %collective-permute-start.18 = (bf16[384,512]{1,0:T(8,128)(2,1)S(1)}, bf16[384,512]{1,0:T(8,128)(2,1)S(1)}, u32[]{:S(2)}, u32[]{:S(2)}) collective-permute-start(bf16[384,512]{1,0:T(8,128)(2,1)S(1)} %get-tuple-element.52), channel_id=1, source_target_pairs={{128,64},{192,0},{129,65},{193,1},{130,66},{194,2},{131,67},{195,3... | collective-permute-start | bytes 1179656 | tf_op jit(solution)/shard_map/ppermute | solution.py:30
  147.0 19.3 %collective-permute-start.19 = (bf16[384,512]{1,0:T(8,128)(2,1)S(1)}, bf16[384,512]{1,0:T(8,128)(2,1)S(1)}, u32[]{:S(2)}, u32[]{:S(2)}) collective-permute-start(bf16[384,512]{1,0:T(8,128)(2,1)S(1)} %get-tuple-element.51), channel_id=1, source_target_pairs={{192,128},{128,192},{64,0},{193,129},{129,193},{65,1},{194,130},{1... | collective-permute-start | bytes 1179656 | tf_op jit(solution)/shard_map/ppermute | solution.py:26
  149.7 16.6 %collective-permute-start.20 = (bf16[32,768]{1,0:T(8,128)(2,1)S(1)}, bf16[32,768]{1,0:T(8,128)(2,1)S(1)}, u32[]{:S(2)}, u32[]{:S(2)}) collective-permute-start(bf16[32,768]{1,0:T(8,128)(2,1)S(1)} %convert_element_type.124), channel_id=1, source_target_pairs={{0,3},{1,2},{2,1},{3,0},{4,7},{5,6},{6,5},{7,4},{8,11},{9,10},{10,... | collective-permute-start | bytes 147464 | tf_op jit(solution)/shard_map/ppermute | solution.py:16
  153.0 28.6 %collective-permute-start.23 = (f32[512,32]{0,1:T(8,128)S(1)}, f32[512,32]{0,1:T(8,128)S(1)}, u32[]{:S(2)}, u32[]{:S(2)}) collective-permute-start(f32[512,32]{0,1:T(8,128)S(1)} %fusion.21), channel_id=1, source_target_pairs={{0,256},{256,0},{1,257},{257,1},{2,258},{258,2},{3,259},{259,3},{4... | collective-permute-start | bytes 196616 | tf_op jit(solution)/shard_map/ppermute | solution.py:16
  167.2 45.4 %collective-permute-start.21 = (bf16[384,512]{1,0:T(8,128)(2,1)S(1)}, bf16[384,512]{1,0:T(8,128)(2,1)S(1)}, u32[]{:S(2)}, u32[]{:S(2)}) collective-permute-start(bf16[384,512]{1,0:T(8,128)(2,1)S(1)} %fusion.30), channel_id=1, source_target_pairs={{0,32},{32,0},{1,33},{33,1},{2,34},{34,2},{3,35},{35,3},{4,36},{36... | collective-permute-start | bytes 1179656 | tf_op jit(solution)/shard_map/ppermute | solution.py:16
  175.9 36.7 %collective-permute-start.22 = (bf16[384,512]{1,0:T(8,128)(2,1)S(1)}, bf16[384,512]{1,0:T(8,128)(2,1)S(1)}, u32[]{:S(2)}, u32[]{:S(2)}) collective-permute-start(bf16[384,512]{1,0:T(8,128)(2,1)S(1)} %fusion.37), channel_id=1, source_target_pairs={{128,64},{192,0},{129,65},{193,1},{130,66},{194,2},{131,67},{195,3... | collective-permute-start | bytes 1179656 | tf_op jit(solution)/shard_map/ppermute | solution.py:30
  177.2 5.4 %collective-permute-start.24 = (f32[2,16,1024]{2,1,0:T(8,128)S(1)}, f32[2,16,1024]{2,1,0:T(8,128)S(1)}, u32[]{:S(2)}, u32[]{:S(2)}) collective-permute-start(f32[2,16,1024]{2,1,0:T(8,128)S(1)} %maximum_multiply_fusion), channel_id=1, source_target_pairs={{0,256},{256,0},{1,257},{257,1},{2,258},{258,2},{3,259},{259,3},{4... | collective-permute-start | bytes 393224 | tf_op jit(solution)/shard_map/ppermute | solution.py:16

commit v3 on v2

v3 whole, which is shorter than its diff:
```python
import jax
import jax.numpy as jnp
from jax import lax
from jax.sharding import Mesh, PartitionSpec as P

adapter_scale = 2.0
norm_epsilon = 1e-05
sizes = {"dp": 2, "y": 4, "zh": 2, "zl": 8, "x": 4}
section_axes = ("y", "zh")
tensor_axes = ("zl", "x")
together = lax.optimization_barrier


def swap(value, axis, mask):
    count = lax.axis_size(axis)
    return lax.ppermute(value, axis, [(i, i ^ mask) for i in range(count)])


def ordered(mine, other, bit, axis):
    low = jnp.where(bit, other, mine)
    high = jnp.where(bit, mine, other)
    return jnp.stack([low, high], axis=axis)


def later_y(value):
    count = lax.axis_size("y")
    return [lax.ppermute(value, "y", [(i, i - d) for i in range(d, count)]) for d in range(1, count)]


def local(
    layer_saved_input,
    key_value_gradient,
    key_value_weight,
    adapter_down_weight,
    adapter_up_weight,
    attention_norm_scale,
):
    f32, b16 = jnp.float32, jnp.bfloat16
    x = layer_saved_input[0]
    kv_own = key_value_gradient[0]
    weight = key_value_weight[0]
    down_map = adapter_down_weight[0]
    up_map = adapter_up_weight[0]
    gain = attention_norm_scale[0]
    tokens, span = x.shape
    own, kv_width = kv_own.shape
    half = kv_width // 2
    rank_two = down_map.shape[1]
    rank = rank_two // 2
    width = span * lax.axis_size(tensor_axes)
    factor = adapter_scale / (tokens * lax.axis_size("dp"))
    x_at, z_at = lax.axis_index("x"), lax.axis_index("zl")
    zh = lax.axis_index("zh")

    wide = x.astype(f32)
    gained = (down_map.astype(f32) * gain[:, None]).astype(b16)
    low = lax.dot_general(gained, x, (((0,), (1,)), ((), ())), preferred_element_type=f32)
    lanes = 128
    chunk = kv_width // lanes
    low = low.reshape(rank_two // chunk, chunk, tokens // lanes, lanes)
    low = jnp.swapaxes(low, 1, 2).reshape(-1, kv_width)

    def low_step(low, axis, mask):
        return low + swap(low.astype(b16), axis, mask).astype(f32)

    def both_swap(part, low, axis, mask):
        rows = part.size // kv_width
        got = swap(jnp.concatenate([part.reshape(rows, kv_width), low.astype(b16)]), axis, mask)
        return got[:rows].reshape(part.shape), low + got[rows:].astype(f32)

    kv_all = jnp.zeros((2, 2, 2, sizes["x"], own, kv_width), b16)
    bits = [(z_at >> i) & 1 for i in range(3)]

    def place(kv_all, part, bit, at):
        part = part.reshape((2, 2, 1, 1, own, kv_width))
        return lax.dynamic_update_slice(kv_all, part, (0, 0, bit, at, 0, 0))

    other = swap(kv_own, "zl", 4)
    two = ordered(kv_own, other, bits[2] == 1, 0)
    square = jnp.sum(wide * wide, axis=1)
    two, low, square = together((two, low, square))

    other_two, low = both_swap(two, low, "zl", 2)
    four = ordered(two, other_two, bits[1] == 1, 1)
    four, low = together((four, low))

    other_four, low = both_swap(four, low, "zl", 1)
    parts = [swap(four, "x", mask) for mask in (2, 1, 3)]
    other_four, parts, low = together((other_four, parts, low))
    kv_all = place(kv_all, four, bits[0], x_at)
    kv_all = place(kv_all, other_four, 1 - bits[0], x_at)
    for mask, part in zip((2, 1, 3), parts):
        kv_all = place(kv_all, part, bits[0], x_at ^ mask)

    parts = [swap(parts[0], "zl", 1)] + [swap(other_four, "x", mask) for mask in (1, 3)]
    parts, low = together((parts, low))
    for mask, part in zip((2, 1, 3), parts):
        kv_all = place(kv_all, part, 1 - bits[0], x_at ^ mask)
    kv_all = kv_all.reshape(tokens, kv_width)

    lift = jnp.concatenate(
        [jnp.dot(down_map[:, c * rank : (c + 1) * rank], up_map[c], preferred_element_type=f32) for c in range(2)], axis=1
    )
    weight = (weight.astype(f32) + adapter_scale * lift).astype(b16)
    base = lax.dot_general(kv_all, weight, (((1,), (1,)), ((), ())), preferred_element_type=f32)
    scaled_grad = base * gain[None, :]
    center = jnp.sum(scaled_grad * wide, axis=1)
    rows = reduce_rows(jnp.stack([square, center]))
    low = low_step(low, "zl", 4)
    (square, center), low, kv_all = together((rows, low, kv_all))
    inverse = lax.rsqrt(square / width + norm_epsilon)
    pull = center * (inverse * inverse / width)
    branch = ((scaled_grad - wide * pull[:, None]) * inverse[:, None]).astype(b16)

    cut = tokens // 2
    early, late = branch[:cut], branch[cut:]
    late_other = swap(late, "zh", 1)
    low = low_step(low, "x", 1)
    early, low = together((early, low))
    early_three = later_y(early)
    late_other, early_three, low = together((late_other, early_three, low))
    early_tail = sum(part.astype(f32) for part in early_three)
    early_sum = early.astype(f32) + early_tail
    late_pair = late.astype(f32) + late_other.astype(f32)
    early_other = swap(jnp.where(zh == 1, early_sum, early_tail).astype(b16), "zh", 1)
    low = low_step(low, "x", 3)
    late_sent, low = together((late_pair.astype(b16), low))
    late_three = later_y(late_sent)
    late_tail = sum(part.astype(f32) for part in late_three)
    late_out = (jnp.where(zh == 0, late_pair, late.astype(f32)) + late_tail).astype(b16)
    early_out = (early_sum + early_other.astype(f32)).astype(b16)
    result = lax.dynamic_update_slice(jnp.pad(late_out, ((cut, 0), (0, 0))), early_out, (0, 0))
    low = jnp.swapaxes(low.reshape(rank_two // chunk, tokens // lanes, chunk, lanes), 1, 2).reshape(rank_two, tokens)
    lowered = (low * inverse[None, :]).astype(b16)

    hidden = jnp.concatenate(
        [
            lax.dot_general(
                kv_all[:, c * half : (c + 1) * half], up_map[c], (((1,), (1,)), ((), ())), preferred_element_type=f32
            )
            for c in range(2)
        ],
        axis=1,
    ).astype(b16)
    normed_hidden = (hidden.astype(f32) * inverse[:, None]).astype(b16)
    down = lax.dot_general(x, normed_hidden, (((0,), (0,)), ((), ())), preferred_element_type=f32)
    down = down * (factor * gain[:, None])
    down = down + swap(down, "dp", 1)
    up = factor * jnp.stack(
        [
            jnp.dot(
                lowered[c * rank : (c + 1) * rank],
                kv_all[:, c * half : (c + 1) * half],
                preferred_element_type=f32,
            )
            for c in range(2)
        ]
    )
    up = up + swap(up, "dp", 1)
    return (result[None], down[None], up[None])


def reduce_rows(rows):
    rows = lax.psum(rows, "x")
    spread = jnp.broadcast_to(rows[None], (sizes["zl"],) + rows.shape)
    return jnp.sum(lax.all_to_all(spread, "zl", 0, 0), axis=0)


def solution(mesh):
    mesh = Mesh(mesh.devices.reshape(tuple(sizes.values())), tuple(sizes))
    in_specs = (
        P(section_axes, "dp", tensor_axes),
        P(section_axes, ("dp",) + tensor_axes, None),
        P(section_axes, tensor_axes, None),
        P(section_axes, tensor_axes, None),
        P(section_axes, None, None, None),
        P(section_axes, tensor_axes),
    )
    out_specs = (
        P(section_axes, "dp", tensor_axes),
        P(section_axes, tensor_axes, None),
        P(section_axes, None, None, None),
    )
    return jax.shard_map(local, mesh=mesh, in_specs=in_specs, out_specs=out_specs, check_vma=False)
```

time: 216 us -> 199 us (0.921)
  the two profiles are of different devices: /device:TPU:81 before, /device:TPU:41 now
where the time goes in v3:
time: 199 us; the launch traced here: 198 us
  starting transfers between devices  97.5 us (49%)
  waiting for transfers between devices  71.4 us (36%)
  matrix products  10.8 us (5%)
  other arithmetic  8.42 us (4%)
  blocking collectives  7.35 us (4%)
    ppermute x16, starting transfers between devices, swap(): return lax.ppermute(value, axis, [(i, i ^ mask) for i in range(count)])  83.7 us
    ppermute x16, waiting for transfers between devices, swap(): return lax.ppermute(value, axis, [(i, i ^ mask) for i in range(count)])  63.9 us
    ppermute x6, starting transfers between devices, later_y(): lax.ppermute(value, 'y', [(i, i - d) for i in range(d, count)])  8.66 us
    all_to_all x1, waiting for transfers between devices, reduce_rows(): return jnp.sum(lax.all_to_all(spread, 'zl', 0, 0), axis=0)  7.45 us
    psum x1, blocking collectives, reduce_rows(): rows = lax.psum(rows, 'x')  7.35 us
    all_to_all x1, starting transfers between devices, reduce_rows(): return jnp.sum(lax.all_to_all(spread, 'zl', 0, 0), axis=0)  5.15 us
    dot_general x2, matrix products, local(): jnp.dot(down_map[:, c * rank:(c + 1) * rank], up_map[c], preferred_elemen...  4.34 us
  transfers between devices with their start and end apart: 23, of which 8 were waited for; matrix products, arithmetic and copies ran while one was open for 7% of the time, Pallas kernels for 0%

profile of v3, /device:TPU:41, one launch (start us, length us, event | category | flops | bytes accessed | tf_op | source)
XLA Modules:
  0.0 198.4 jit_solution(7437367760661136556)
XLA Ops:
  0.7 8.9 %collective-permute-start = (bf16[24,2048]{1,0:T(8,128)(2,1)}, bf16[24,2048]{1,0:T(8,128)(2,1)S(1)}, u32[]{:S(2)}, u32[]{:S(2)}) collective-permute-start(bf16[24,2048]{1,0:T(8,128)(2,1)} %bitcast.142), channel_id=1, source_target_pairs={{0,16},{4,20},{8,24},{12,28},{16,0},{20,4},{24,8},{28,12},{1,17},{... | collective-permute-start | bytes 294920 | tf_op jit(solution)/shard_map/ppermute | solution.py:16
  9.6 1.4 fusion.6
  11.0 0.8 multiply_convert_fusion.1
  11.8 1.5 fusion.60
  13.3 2.6 %convolution_bitcast_fusion = f32[1,512,1024]{2,1,0:T(8,128)} fusion(bf16[1,2,16,1024]{3,2,1,0:T(8,128)(2,1)} %param.10, bf16[512,32]{0,1:T(8,128)(2,1)} %bitcast.139), kind=kOutput, calls=%fused_computation.9 | convolution fusion | flops 16777216 | bytes 2146304 | tf_op jit(solution)/shard_map/dot_general | solution.py:102
  16.0 6.4 %collective-permute-start.1 = (bf16[60,2048]{1,0:T(8,128)(2,1)S(1)}, bf16[60,2048]{1,0:T(8,128)(2,1)S(1)}, u32[]{:S(2)}, u32[]{:S(2)}) collective-permute-start(bf16[60,2048]{1,0:T(8,128)(2,1)S(1)} %pad_maximum_fusion.2), channel_id=1, source_target_pairs={{0,8},{4,12},{8,0},{12,4},{16,24},{20,28},{24,16},{28,20},{1,9},{5... | collective-permute-start | bytes 737288 | tf_op jit(solution)/shard_map/ppermute | solution.py:16
  22.4 1.8 convolution_bitcast_fusion.1
  24.2 7.9 %collective-permute-done.1 = bf16[60,2048]{1,0:T(8,128)(2,1)S(1)} collective-permute-done((bf16[60,2048]{1,0:T(8,128)(2,1)S(1)}, bf16[60,2048]{1,0:T(8,128)(2,1)S(1)}, u32[]{:S(2)}, u32[]{:S(2)}) %collective-permute-start.1) | collective-permute-done | bytes 245792 | tf_op jit(solution)/shard_map/ppermute | solution.py:16
  32.2 4.7 %collective-permute-start.3 = (bf16[2,2,24,2048]{3,2,1,0:T(8,128)(2,1)S(1)}, bf16[2,2,24,2048]{3,2,1,0:T(8,128)(2,1)S(1)}, u32[]{:S(2)}, u32[]{:S(2)}) collective-permute-start(bf16[2,2,24,2048]{3,2,1,0:T(8,128)(2,1)S(1)} %pad_maximum_fusion.1), channel_id=1, source_target_pairs={{0,2},{1,3},{2,0},{3,1},{4,6},{5,7},{6,4},{7,5},{8,10},{9,11},{10,... | collective-permute-start | bytes 1179656 | tf_op jit(solution)/shard_map/ppermute | solution.py:16
  36.9 2.2 %collective-permute-start.4 = (bf16[2,2,24,2048]{3,2,1,0:T(8,128)(2,1)S(1)}, bf16[2,2,24,2048]{3,2,1,0:T(8,128)(2,1)S(1)}, u32[]{:S(2)}, u32[]{:S(2)}) collective-permute-start(bf16[2,2,24,2048]{3,2,1,0:T(8,128)(2,1)S(1)} %pad_maximum_fusion.1), channel_id=1, source_target_pairs={{0,1},{1,0},{2,3},{3,2},{4,5},{5,4},{6,7},{7,6},{8,9},{9,8},{10,11... | collective-permute-start | bytes 1179656 | tf_op jit(solution)/shard_map/ppermute | solution.py:16
  39.1 2.5 %collective-permute-start.5 = (bf16[2,2,24,2048]{3,2,1,0:T(8,128)(2,1)S(1)}, bf16[2,2,24,2048]{3,2,1,0:T(8,128)(2,1)S(1)}, u32[]{:S(2)}, u32[]{:S(2)}) collective-permute-start(bf16[2,2,24,2048]{3,2,1,0:T(8,128)(2,1)S(1)} %pad_maximum_fusion.1), channel_id=1, source_target_pairs={{0,3},{1,2},{2,1},{3,0},{4,7},{5,6},{6,5},{7,4},{8,11},{9,10},{10,... | collective-permute-start | bytes 1179656 | tf_op jit(solution)/shard_map/ppermute | solution.py:16
  41.6 1.9 collective-permute-start.2
  43.6 0.4 broadcast_in_dim.10
  44.0 10.5 %collective-permute-done.2 = bf16[108,2048]{1,0:T(8,128)(2,1)S(1)} collective-permute-done((bf16[108,2048]{1,0:T(8,128)(2,1)S(1)}, bf16[108,2048]{1,0:T(8,128)(2,1)S(1)}, u32[]{:S(2)}, u32[]{:S(2)}) %collective-permute-start.2) | collective-permute-done | bytes 442400 | tf_op jit(solution)/shard_map/ppermute | solution.py:16
  54.9 3.3 %collective-permute-start.7 = (bf16[2,2,24,2048]{3,2,1,0:T(8,128)(2,1)S(1)}, bf16[2,2,24,2048]{3,2,1,0:T(8,128)(2,1)S(1)}, u32[]{:S(2)}, u32[]{:S(2)}) collective-permute-start(bf16[2,2,24,2048]{3,2,1,0:T(8,128)(2,1)S(1)} %bitcast.127), channel_id=1, source_target_pairs={{0,1},{1,0},{2,3},{3,2},{4,5},{5,4},{6,7},{7,6},{8,9},{9,8},{10,11... | collective-permute-start | bytes 1179656 | tf_op jit(solution)/shard_map/ppermute | solution.py:16
  58.2 3.7 %collective-permute-start.8 = (bf16[2,2,24,2048]{3,2,1,0:T(8,128)(2,1)S(1)}, bf16[2,2,24,2048]{3,2,1,0:T(8,128)(2,1)S(1)}, u32[]{:S(2)}, u32[]{:S(2)}) collective-permute-start(bf16[2,2,24,2048]{3,2,1,0:T(8,128)(2,1)S(1)} %bitcast.128), channel_id=1, source_target_pairs={{0,3},{1,2},{2,1},{3,0},{4,7},{5,6},{6,5},{7,4},{8,11},{9,10},{10,... | collective-permute-start | bytes 1179656 | tf_op jit(solution)/shard_map/ppermute | solution.py:16
  61.9 1.9 collective-permute-start.6
  64.0 8.7 %collective-permute-done.6 = bf16[2,2,24,2048]{3,2,1,0:T(8,128)(2,1)S(1)} collective-permute-done((bf16[2,2,24,2048]{3,2,1,0:T(8,128)(2,1)S(1)}, bf16[2,2,24,2048]{3,2,1,0:T(8,128)(2,1)S(1)}, u32[]{:S(2)}, u32[]{:S(2)}) %collective-permute-start.6) | collective-permute-done | bytes 393248 | tf_op jit(solution)/shard_map/ppermute | solution.py:16
  72.9 3.1 %fusion.7 = (f32[768]{0:T(1024)S(1)}, f32[768,512]{1,0:T(8,128)}) fusion(bf16[1,768,512]{2,1,0:T(8,128)(2,1)S(1)} %copy-done, f32[512]{0:T(512)S(1)} %bitcast.145, bf16[768,2048]{1,0:T(8,128)(2,1)S(1)} %bitcast.119, f32[1,512,1024]{2,1,0:T(8,128)S(1)} %copy-done.2, f32[1,512,1024]{2,1,0:T(8,128)S(1)} %copy-done.3, bf16[1,512,2048]{2,1,0:T(8,128)(2,1)S(1)} %copy-done.8), kind=kOutput, calls=%fused_computation.12 | convolution fusion | flops 1617427712 | bytes 11801600 | tf_op jit(solution)/shard_map/dot_general | solution.py:105
  76.0 7.8 %collective-permute-start.9 = (bf16[12,2048]{1,0:T(8,128)(2,1)S(1)}, bf16[12,2048]{1,0:T(8,128)(2,1)}, u32[]{:S(2)}, u32[]{:S(2)}) collective-permute-start(bf16[12,2048]{1,0:T(8,128)(2,1)S(1)} %convert_element_type.117), channel_id=1, source_target_pairs={{0,16},{4,20},{8,24},{12,28},{16,0},{20,4},{24,8},{28,12},{1,17},{... | collective-permute-start | bytes 147464 | tf_op jit(solution)/shard_map/ppermute | solution.py:16
  83.8 7.4 %psum.7 = f32[2,768]{1,0:T(2,128)S(1)} all-reduce(f32[2,768]{1,0:T(2,128)S(1)} %pad_maximum_fusion.4), channel_id=1, replica_groups=mesh['dp'=2,'y'=4,'zh'=2,'zl'=8,'x'=4] {'x'}, use_global_device_ids=true, to_apply=%region_2.3 | all-reduce | flops 1536 | bytes 12288 | tf_op jit(solution)/shard_map/psum | solution.py:164
  91.2 0.6 broadcast_in_dim.11
  91.8 5.2 %all-to-all-start = ((f32[8,2,768]{2,1,0:T(2,128)}), f32[8,2,768]{2,1,0:T(2,128)S(1)}, u32[]{:S(2)}, u32[]{:S(2)}) async-start(f32[8,2,768]{2,1,0:T(2,128)} %broadcast_in_dim.11), calls=%async_computation | async-start | bytes 98304 | tf_op jit(solution)/shard_map/all_to_all | solution.py:166
  97.0 0.9 convert_add_fusion.5
  97.8 7.5 %all-to-all-done = f32[8,2,768]{2,1,0:T(2,128)S(1)} async-done(((f32[8,2,768]{2,1,0:T(2,128)}), f32[8,2,768]{2,1,0:T(2,128)S(1)}, u32[]{:S(2)}, u32[]{:S(2)}) %all-to-all-start) | async-done | bytes 49184 | tf_op jit(solution)/shard_map/all_to_all | solution.py:166
  105.4 1.9 fusion.10
  107.4 11.2 %collective-permute-start.11 = (bf16[384,512]{1,0:T(8,128)(2,1)S(1)}, bf16[384,512]{1,0:T(8,128)(2,1)S(1)}, u32[]{:S(2)}, u32[]{:S(2)}) collective-permute-start(bf16[384,512]{1,0:T(8,128)(2,1)S(1)} %get-tuple-element.58), channel_id=1, source_target_pairs={{0,32},{32,0},{1,33},{33,1},{2,34},{34,2},{3,35},{35,3},{4,36},{36... | collective-permute-start | bytes 1179656 | tf_op jit(solution)/shard_map/ppermute | solution.py:16
  118.6 2.6 %collective-permute-start.10 = (bf16[12,2048]{1,0:T(8,128)(2,1)S(1)}, bf16[12,2048]{1,0:T(8,128)(2,1)S(1)}, u32[]{:S(2)}, u32[]{:S(2)}) collective-permute-start(bf16[12,2048]{1,0:T(8,128)(2,1)S(1)} %convert_element_type.120), channel_id=1, source_target_pairs={{0,1},{1,0},{2,3},{3,2},{4,5},{5,4},{6,7},{7,6},{8,9},{9,8},{10,11... | collective-permute-start | bytes 147464 | tf_op jit(solution)/shard_map/ppermute | solution.py:16
  121.2 0.5 fusion.32
  121.7 1.9 collective-permute-done.10
  123.6 2.1 %collective-permute-start.12 = (bf16[384,512]{1,0:T(8,128)(2,1)S(1)}, bf16[384,512]{1,0:T(8,128)(2,1)S(1)}, u32[]{:S(2)}, u32[]{:S(2)}) collective-permute-start(bf16[384,512]{1,0:T(8,128)(2,1)S(1)} %get-tuple-element.45), channel_id=1, source_target_pairs={{64,0},{128,64},{192,128},{65,1},{129,65},{193,129},{66,2},{130,66... | collective-permute-start | bytes 1179656 | tf_op jit(solution)/shard_map/ppermute | solution.py:27
  125.7 1.3 collective-permute-start.13
  127.0 0.7 collective-permute-start.14
  127.7 0.5 fusion.29
  128.4 9.8 %collective-permute-start.20 = (f32[512,32]{0,1:T(8,128)S(1)}, f32[512,32]{0,1:T(8,128)S(1)}, u32[]{:S(2)}, u32[]{:S(2)}) collective-permute-start(f32[512,32]{0,1:T(8,128)S(1)} %fusion.28), channel_id=1, source_target_pairs={{0,256},{256,0},{1,257},{257,1},{2,258},{258,2},{3,259},{259,3},{4... | collective-permute-start | bytes 196616 | tf_op jit(solution)/shard_map/ppermute | solution.py:16
  138.3 16.1 %collective-permute-done.11 = bf16[384,512]{1,0:T(8,128)(2,1)S(1)} collective-permute-done((bf16[384,512]{1,0:T(8,128)(2,1)S(1)}, bf16[384,512]{1,0:T(8,128)(2,1)S(1)}, u32[]{:S(2)}, u32[]{:S(2)}) %collective-permute-start.11) | collective-permute-done | bytes 393248 | tf_op jit(solution)/shard_map/ppermute | solution.py:16
  154.4 2.5 %collective-permute-start.16 = (bf16[12,2048]{1,0:T(8,128)(2,1)S(1)}, bf16[12,2048]{1,0:T(8,128)(2,1)S(1)}, u32[]{:S(2)}, u32[]{:S(2)}) collective-permute-start(bf16[12,2048]{1,0:T(8,128)(2,1)S(1)} %convert_element_type.132), channel_id=1, source_target_pairs={{0,3},{1,2},{2,1},{3,0},{4,7},{5,6},{6,5},{7,4},{8,11},{9,10},{10,... | collective-permute-start | bytes 147464 | tf_op jit(solution)/shard_map/ppermute | solution.py:16
  157.3 11.2 %collective-permute-start.15 = (bf16[384,512]{1,0:T(8,128)(2,1)S(1)}, bf16[384,512]{1,0:T(8,128)(2,1)S(1)}, u32[]{:S(2)}, u32[]{:S(2)}) collective-permute-start(bf16[384,512]{1,0:T(8,128)(2,1)S(1)} %select_convert_fusion), channel_id=1, source_target_pairs={{0,32},{32,0},{1,33},{33,1},{2,34},{34,2},{3,35},{35,3},{4,36},{36... | collective-permute-start | bytes 1179656 | tf_op jit(solution)/shard_map/ppermute | solution.py:16
  168.6 0.3 fusion.25
  168.9 0.3 fusion.22
  169.3 3.0 %collective-permute-start.21 = (f32[2,16,1024]{2,1,0:T(8,128)S(1)}, f32[2,16,1024]{2,1,0:T(8,128)S(1)}, u32[]{:S(2)}, u32[]{:S(2)}) collective-permute-start(f32[2,16,1024]{2,1,0:T(8,128)S(1)} %maximum_multiply_fusion.1), channel_id=1, source_target_pairs={{0,256},{256,0},{1,257},{257,1},{2,258},{258,2},{3,259},{259,3},{4... | collective-permute-start | bytes 393224 | tf_op jit(solution)/shard_map/ppermute | solution.py:16
  172.3 0.6 add_bitcast_fusion.1
  173.0 0.7 collective-permute-start.19
  173.7 1.3 collective-permute-start.18
  175.0 2.6 %collective-permute-start.17 = (bf16[384,512]{1,0:T(8,128)(2,1)S(1)}, bf16[384,512]{1,0:T(8,128)(2,1)S(1)}, u32[]{:S(2)}, u32[]{:S(2)}) collective-permute-start(bf16[384,512]{1,0:T(8,128)(2,1)S(1)} %fusion.38), channel_id=1, source_target_pairs={{64,0},{128,64},{192,128},{65,1},{129,65},{193,129},{66,2},{130,66... | collective-permute-start | bytes 1179656 | tf_op jit(solution)/shard_map/ppermute | solution.py:27
  177.6 0.7 add_bitcast_fusion
  178.3 18.6 %collective-permute-done.15 = bf16[384,512]{1,0:T(8,128)(2,1)S(1)} collective-permute-done((bf16[384,512]{1,0:T(8,128)(2,1)S(1)}, bf16[384,512]{1,0:T(8,128)(2,1)S(1)}, u32[]{:S(2)}, u32[]{:S(2)}) %collective-permute-start.15) | collective-permute-done | bytes 393248 | tf_op jit(solution)/shard_map/ppermute | solution.py:16
  197.5 0.9 maximum_bitcast_fusion
  (79 shorter events, 2.4 us)
Async XLA Ops:
  0.6 15.3 %copy-start.5 = (bf16[1,24,2048]{2,1,0:T(8,128)(2,1)S(1)}, bf16[1,24,2048]{2,1,0:T(8,128)(2,1)}, u32[]{:S(2)}) copy-start(bf16[1,24,2048]{2,1,0:T(8,128)(2,1)} %param.7) | copy-start | bytes 294916
  0.6 21.8 %copy-start.4 = (bf16[1,512,32]{1,2,0:T(8,128)(2,1)S(1)}, bf16[1,512,32]{1,2,0:T(8,128)(2,1)}, u32[]{:S(2)}) copy-start(bf16[1,512,32]{1,2,0:T(8,128)(2,1)} %param.9) | copy-start | bytes 98308
  0.7 21.8 %copy-start.6 = (bf16[1,2,16,1024]{3,2,1,0:T(8,128)(2,1)S(1)}, bf16[1,2,16,1024]{3,2,1,0:T(8,128)(2,1)}, u32[]{:S(2)}) copy-start(bf16[1,2,16,1024]{3,2,1,0:T(8,128)(2,1)} %param.10) | copy-start | bytes 196612
  0.7 15.2 %collective-permute-start = (bf16[24,2048]{1,0:T(8,128)(2,1)}, bf16[24,2048]{1,0:T(8,128)(2,1)S(1)}, u32[]{:S(2)}, u32[]{:S(2)}) collective-permute-start(bf16[24,2048]{1,0:T(8,128)(2,1)} %bitcast.142), channel_id=1, source_target_pairs={{0,16},{4,20},{8,24},{12,28},{16,0},{20,4},{24,8},{28,12},{1,17},{... | collective-permute-start | bytes 294920 | tf_op jit(solution)/shard_map/ppermute | solution.py:16
  13.2 11.0 %copy-start.7 = (f32[1,512]{1,0:T(1,128)S(1)}, f32[1,512]{1,0:T(1,128)}, u32[]{:S(2)}) copy-start(f32[1,512]{1,0:T(1,128)} %param.11) | copy-start | bytes 6148
  16.0 16.1 %collective-permute-start.1 = (bf16[60,2048]{1,0:T(8,128)(2,1)S(1)}, bf16[60,2048]{1,0:T(8,128)(2,1)S(1)}, u32[]{:S(2)}, u32[]{:S(2)}) collective-permute-start(bf16[60,2048]{1,0:T(8,128)(2,1)S(1)} %pad_maximum_fusion.2), channel_id=1, source_target_pairs={{0,8},{4,12},{8,0},{12,4},{16,24},{20,28},{24,16},{28,20},{1,9},{5... | collective-permute-start | bytes 737288 | tf_op jit(solution)/shard_map/ppermute | solution.py:16
  32.2 22.3 %collective-permute-start.3 = (bf16[2,2,24,2048]{3,2,1,0:T(8,128)(2,1)S(1)}, bf16[2,2,24,2048]{3,2,1,0:T(8,128)(2,1)S(1)}, u32[]{:S(2)}, u32[]{:S(2)}) collective-permute-start(bf16[2,2,24,2048]{3,2,1,0:T(8,128)(2,1)S(1)} %pad_maximum_fusion.1), channel_id=1, source_target_pairs={{0,2},{1,3},{2,0},{3,1},{4,6},{5,7},{6,4},{7,5},{8,10},{9,11},{10,... | collective-permute-start | bytes 1179656 | tf_op jit(solution)/shard_map/ppermute | solution.py:16
  36.9 17.7 %collective-permute-start.4 = (bf16[2,2,24,2048]{3,2,1,0:T(8,128)(2,1)S(1)}, bf16[2,2,24,2048]{3,2,1,0:T(8,128)(2,1)S(1)}, u32[]{:S(2)}, u32[]{:S(2)}) collective-permute-start(bf16[2,2,24,2048]{3,2,1,0:T(8,128)(2,1)S(1)} %pad_maximum_fusion.1), channel_id=1, source_target_pairs={{0,1},{1,0},{2,3},{3,2},{4,5},{5,4},{6,7},{7,6},{8,9},{9,8},{10,11... | collective-permute-start | bytes 1179656 | tf_op jit(solution)/shard_map/ppermute | solution.py:16
  39.1 15.8 %collective-permute-start.5 = (bf16[2,2,24,2048]{3,2,1,0:T(8,128)(2,1)S(1)}, bf16[2,2,24,2048]{3,2,1,0:T(8,128)(2,1)S(1)}, u32[]{:S(2)}, u32[]{:S(2)}) collective-permute-start(bf16[2,2,24,2048]{3,2,1,0:T(8,128)(2,1)S(1)} %pad_maximum_fusion.1), channel_id=1, source_target_pairs={{0,3},{1,2},{2,1},{3,0},{4,7},{5,6},{6,5},{7,4},{8,11},{9,10},{10,... | collective-permute-start | bytes 1179656 | tf_op jit(solution)/shard_map/ppermute | solution.py:16
  41.6 12.9 %collective-permute-start.2 = (bf16[108,2048]{1,0:T(8,128)(2,1)S(1)}, bf16[108,2048]{1,0:T(8,128)(2,1)S(1)}, u32[]{:S(2)}, u32[]{:S(2)}) collective-permute-start(bf16[108,2048]{1,0:T(8,128)(2,1)S(1)} %pad_maximum_fusion), channel_id=1, source_target_pairs={{0,4},{4,0},{8,12},{12,8},{16,20},{20,16},{24,28},{28,24},{1,5},{5... | collective-permute-start | bytes 1327112 | tf_op jit(solution)/shard_map/ppermute | solution.py:16
  43.9 28.9 %copy-start.8 = (bf16[1,512,2048]{2,1,0:T(8,128)(2,1)S(1)}, bf16[1,512,2048]{2,1,0:T(8,128)(2,1)}, u32[]{:S(2)}) copy-start(bf16[1,512,2048]{2,1,0:T(8,128)(2,1)} %param.8) | copy-start | bytes 6291460
  44.0 28.9 %copy-start = (bf16[1,768,512]{2,1,0:T(8,128)(2,1)S(1)}, bf16[1,768,512]{2,1,0:T(8,128)(2,1)}, u32[]{:S(2)}) copy-start(bf16[1,768,512]{2,1,0:T(8,128)(2,1)} %param.6) | copy-start | bytes 2359300
  44.0 28.9 %copy-start.2 = (f32[1,512,1024]{2,1,0:T(8,128)S(1)}, f32[1,512,1024]{2,1,0:T(8,128)}, u32[]{:S(2)}) copy-start(f32[1,512,1024]{2,1,0:T(8,128)} %convolution_bitcast_fusion) | copy-start | bytes 6291460
  44.0 28.9 %copy-start.3 = (f32[1,512,1024]{2,1,0:T(8,128)S(1)}, f32[1,512,1024]{2,1,0:T(8,128)}, u32[]{:S(2)}) copy-start(f32[1,512,1024]{2,1,0:T(8,128)} %convolution_bitcast_fusion.1) | copy-start | bytes 6291460
  54.9 17.9 %collective-permute-start.7 = (bf16[2,2,24,2048]{3,2,1,0:T(8,128)(2,1)S(1)}, bf16[2,2,24,2048]{3,2,1,0:T(8,128)(2,1)S(1)}, u32[]{:S(2)}, u32[]{:S(2)}) collective-permute-start(bf16[2,2,24,2048]{3,2,1,0:T(8,128)(2,1)S(1)} %bitcast.127), channel_id=1, source_target_pairs={{0,1},{1,0},{2,3},{3,2},{4,5},{5,4},{6,7},{7,6},{8,9},{9,8},{10,11... | collective-permute-start | bytes 1179656 | tf_op jit(solution)/shard_map/ppermute | solution.py:16
  58.2 14.6 %collective-permute-start.8 = (bf16[2,2,24,2048]{3,2,1,0:T(8,128)(2,1)S(1)}, bf16[2,2,24,2048]{3,2,1,0:T(8,128)(2,1)S(1)}, u32[]{:S(2)}, u32[]{:S(2)}) collective-permute-start(bf16[2,2,24,2048]{3,2,1,0:T(8,128)(2,1)S(1)} %bitcast.128), channel_id=1, source_target_pairs={{0,3},{1,2},{2,1},{3,0},{4,7},{5,6},{6,5},{7,4},{8,11},{9,10},{10,... | collective-permute-start | bytes 1179656 | tf_op jit(solution)/shard_map/ppermute | solution.py:16
  61.9 10.8 %collective-permute-start.6 = (bf16[2,2,24,2048]{3,2,1,0:T(8,128)(2,1)S(1)}, bf16[2,2,24,2048]{3,2,1,0:T(8,128)(2,1)S(1)}, u32[]{:S(2)}, u32[]{:S(2)}) collective-permute-start(bf16[2,2,24,2048]{3,2,1,0:T(8,128)(2,1)S(1)} %collective-permute-done.3), channel_id=1, source_target_pairs={{0,4},{4,0},{8,12},{12,8},{16,20},{20,16},{24,28},{28,24},{1,5},{5... | collective-permute-start | bytes 1179656 | tf_op jit(solution)/shard_map/ppermute | solution.py:16
  76.0 21.0 %collective-permute-start.9 = (bf16[12,2048]{1,0:T(8,128)(2,1)S(1)}, bf16[12,2048]{1,0:T(8,128)(2,1)}, u32[]{:S(2)}, u32[]{:S(2)}) collective-permute-start(bf16[12,2048]{1,0:T(8,128)(2,1)S(1)} %convert_element_type.117), channel_id=1, source_target_pairs={{0,16},{4,20},{8,24},{12,28},{16,0},{20,4},{24,8},{28,12},{1,17},{... | collective-permute-start | bytes 147464 | tf_op jit(solution)/shard_map/ppermute | solution.py:16
  91.8 13.5 %all-to-all-start = ((f32[8,2,768]{2,1,0:T(2,128)}), f32[8,2,768]{2,1,0:T(2,128)S(1)}, u32[]{:S(2)}, u32[]{:S(2)}) async-start(f32[8,2,768]{2,1,0:T(2,128)} %broadcast_in_dim.11), calls=%async_computation | async-start | bytes 98304 | tf_op jit(solution)/shard_map/all_to_all | solution.py:166
  107.3 20.9 %copy-start.1 = (bf16[1,768,512]{2,1,0:T(8,128)(2,1)S(1)}, bf16[1,768,512]{2,1,0:T(8,128)(2,1)}, u32[]{:S(2)}) copy-start(bf16[1,768,512]{2,1,0:T(8,128)(2,1)} %param.6) | copy-start | bytes 2359300
  107.4 47.0 %collective-permute-start.11 = (bf16[384,512]{1,0:T(8,128)(2,1)S(1)}, bf16[384,512]{1,0:T(8,128)(2,1)S(1)}, u32[]{:S(2)}, u32[]{:S(2)}) collective-permute-start(bf16[384,512]{1,0:T(8,128)(2,1)S(1)} %get-tuple-element.58), channel_id=1, source_target_pairs={{0,32},{32,0},{1,33},{33,1},{2,34},{34,2},{3,35},{35,3},{4,36},{36... | collective-permute-start | bytes 1179656 | tf_op jit(solution)/shard_map/ppermute | solution.py:16
  118.6 5.0 %collective-permute-start.10 = (bf16[12,2048]{1,0:T(8,128)(2,1)S(1)}, bf16[12,2048]{1,0:T(8,128)(2,1)S(1)}, u32[]{:S(2)}, u32[]{:S(2)}) collective-permute-start(bf16[12,2048]{1,0:T(8,128)(2,1)S(1)} %convert_element_type.120), channel_id=1, source_target_pairs={{0,1},{1,0},{2,3},{3,2},{4,5},{5,4},{6,7},{7,6},{8,9},{9,8},{10,11... | collective-permute-start | bytes 147464 | tf_op jit(solution)/shard_map/ppermute | solution.py:16
  123.6 30.8 %collective-permute-start.12 = (bf16[384,512]{1,0:T(8,128)(2,1)S(1)}, bf16[384,512]{1,0:T(8,128)(2,1)S(1)}, u32[]{:S(2)}, u32[]{:S(2)}) collective-permute-start(bf16[384,512]{1,0:T(8,128)(2,1)S(1)} %get-tuple-element.45), channel_id=1, source_target_pairs={{64,0},{128,64},{192,128},{65,1},{129,65},{193,129},{66,2},{130,66... | collective-permute-start | bytes 1179656 | tf_op jit(solution)/shard_map/ppermute | solution.py:27
  125.7 28.7 %collective-permute-start.13 = (bf16[384,512]{1,0:T(8,128)(2,1)S(1)}, bf16[384,512]{1,0:T(8,128)(2,1)S(1)}, u32[]{:S(2)}, u32[]{:S(2)}) collective-permute-start(bf16[384,512]{1,0:T(8,128)(2,1)S(1)} %get-tuple-element.45), channel_id=1, source_target_pairs={{128,0},{192,64},{129,1},{193,65},{130,2},{194,66},{131,3},{195,67... | collective-permute-start | bytes 1179656 | tf_op jit(solution)/shard_map/ppermute | solution.py:27
  127.0 27.4 %collective-permute-start.14 = (bf16[384,512]{1,0:T(8,128)(2,1)S(1)}, bf16[384,512]{1,0:T(8,128)(2,1)S(1)}, u32[]{:S(2)}, u32[]{:S(2)}) collective-permute-start(bf16[384,512]{1,0:T(8,128)(2,1)S(1)} %get-tuple-element.45), channel_id=1, source_target_pairs={{192,0},{193,1},{194,2},{195,3},{196,4},{197,5},{198,6},{199,7},{2... | collective-permute-start | bytes 1179656 | tf_op jit(solution)/shard_map/ppermute | solution.py:27
  128.4 43.9 %collective-permute-start.20 = (f32[512,32]{0,1:T(8,128)S(1)}, f32[512,32]{0,1:T(8,128)S(1)}, u32[]{:S(2)}, u32[]{:S(2)}) collective-permute-start(f32[512,32]{0,1:T(8,128)S(1)} %fusion.28), channel_id=1, source_target_pairs={{0,256},{256,0},{1,257},{257,1},{2,258},{258,2},{3,259},{259,3},{4... | collective-permute-start | bytes 196616 | tf_op jit(solution)/shard_map/ppermute | solution.py:16
  154.4 14.1 %collective-permute-start.16 = (bf16[12,2048]{1,0:T(8,128)(2,1)S(1)}, bf16[12,2048]{1,0:T(8,128)(2,1)S(1)}, u32[]{:S(2)}, u32[]{:S(2)}) collective-permute-start(bf16[12,2048]{1,0:T(8,128)(2,1)S(1)} %convert_element_type.132), channel_id=1, source_target_pairs={{0,3},{1,2},{2,1},{3,0},{4,7},{5,6},{6,5},{7,4},{8,11},{9,10},{10,... | collective-permute-start | bytes 147464 | tf_op jit(solution)/shard_map/ppermute | solution.py:16
  157.3 39.7 %collective-permute-start.15 = (bf16[384,512]{1,0:T(8,128)(2,1)S(1)}, bf16[384,512]{1,0:T(8,128)(2,1)S(1)}, u32[]{:S(2)}, u32[]{:S(2)}) collective-permute-start(bf16[384,512]{1,0:T(8,128)(2,1)S(1)} %select_convert_fusion), channel_id=1, source_target_pairs={{0,32},{32,0},{1,33},{33,1},{2,34},{34,2},{3,35},{35,3},{4,36},{36... | collective-permute-start | bytes 1179656 | tf_op jit(solution)/shard_map/ppermute | solution.py:16
  169.3 8.3 %collective-permute-start.21 = (f32[2,16,1024]{2,1,0:T(8,128)S(1)}, f32[2,16,1024]{2,1,0:T(8,128)S(1)}, u32[]{:S(2)}, u32[]{:S(2)}) collective-permute-start(f32[2,16,1024]{2,1,0:T(8,128)S(1)} %maximum_multiply_fusion.1), channel_id=1, source_target_pairs={{0,256},{256,0},{1,257},{257,1},{2,258},{258,2},{3,259},{259,3},{4... | collective-permute-start | bytes 393224 | tf_op jit(solution)/shard_map/ppermute | solution.py:16
  173.0 24.2 %collective-permute-start.19 = (bf16[384,512]{1,0:T(8,128)(2,1)S(1)}, bf16[384,512]{1,0:T(8,128)(2,1)S(1)}, u32[]{:S(2)}, u32[]{:S(2)}) collective-permute-start(bf16[384,512]{1,0:T(8,128)(2,1)S(1)} %fusion.38), channel_id=1, source_target_pairs={{192,0},{193,1},{194,2},{195,3},{196,4},{197,5},{198,6},{199,7},{2... | collective-permute-start | bytes 1179656 | tf_op jit(solution)/shard_map/ppermute | solution.py:27
  173.7 23.5 %collective-permute-start.18 = (bf16[384,512]{1,0:T(8,128)(2,1)S(1)}, bf16[384,512]{1,0:T(8,128)(2,1)S(1)}, u32[]{:S(2)}, u32[]{:S(2)}) collective-permute-start(bf16[384,512]{1,0:T(8,128)(2,1)S(1)} %fusion.38), channel_id=1, source_target_pairs={{128,0},{192,64},{129,1},{193,65},{130,2},{194,66},{131,3},{195,67... | collective-permute-start | bytes 1179656 | tf_op jit(solution)/shard_map/ppermute | solution.py:27
  175.0 22.2 %collective-permute-start.17 = (bf16[384,512]{1,0:T(8,128)(2,1)S(1)}, bf16[384,512]{1,0:T(8,128)(2,1)S(1)}, u32[]{:S(2)}, u32[]{:S(2)}) collective-permute-start(bf16[384,512]{1,0:T(8,128)(2,1)S(1)} %fusion.38), channel_id=1, source_target_pairs={{64,0},{128,64},{192,128},{65,1},{129,65},{193,129},{66,2},{130,66... | collective-permute-start | bytes 1179656 | tf_op jit(solution)/shard_map/ppermute | solution.py:27

commit v4 on v3

--- a/solution.py
+++ b/solution.py
@@ -80,21 +80,26 @@
     square = jnp.sum(wide * wide, axis=1)
     two, low, square = together((two, low, square))
 
+    far = swap(two, "x", 2)
     other_two, low = both_swap(two, low, "zl", 2)
     four = ordered(two, other_two, bits[1] == 1, 1)
-    four, low = together((four, low))
+    four, other_two, far, low = together((four, other_two, far, low))
 
-    other_four, low = both_swap(four, low, "zl", 1)
-    parts = [swap(four, "x", mask) for mask in (2, 1, 3)]
-    other_four, parts, low = together((other_four, parts, low))
+    other_far = swap(other_two, "x", 2)
+    other_four = swap(four, "zl", 1)
+    parts = [swap(four, "x", mask) for mask in (1, 3)]
+    low = low_step(low, "zl", 4)
+    other_far, other_four, parts, low = together((other_far, other_four, parts, low))
+    far = ordered(far, other_far, bits[1] == 1, 1)
     kv_all = place(kv_all, four, bits[0], x_at)
     kv_all = place(kv_all, other_four, 1 - bits[0], x_at)
-    for mask, part in zip((2, 1, 3), parts):
+    for mask, part in zip((2, 1, 3), [far] + parts):
         kv_all = place(kv_all, part, bits[0], x_at ^ mask)
 
-    parts = [swap(parts[0], "zl", 1)] + [swap(other_four, "x", mask) for mask in (1, 3)]
-    parts, low = together((parts, low))
-    for mask, part in zip((2, 1, 3), parts):
+    far, low = both_swap(far, low, "zl", 1)
+    parts = [swap(other_four, "x", mask) for mask in (1, 3)]
+    far, parts, low = together((far, parts, low))
+    for mask, part in zip((2, 1, 3), [far] + parts):
         kv_all = place(kv_all, part, 1 - bits[0], x_at ^ mask)
     kv_all = kv_all.reshape(tokens, kv_width)
 
@@ -106,8 +111,7 @@
     scaled_grad = base * gain[None, :]
     center = jnp.sum(scaled_grad * wide, axis=1)
     rows = reduce_rows(jnp.stack([square, center]))
-    low = low_step(low, "zl", 4)
-    (square, center), low, kv_all = together((rows, low, kv_all))
+    (square, center), kv_all, low = together((rows, kv_all, low))
     inverse = lax.rsqrt(square / width + norm_epsilon)
     pull = center * (inverse * inverse / width)
     branch = ((scaled_grad - wide * pull[:, None]) * inverse[:, None]).astype(b16)
@@ -118,13 +122,16 @@
     low = low_step(low, "x", 1)
     early, low = together((early, low))
     early_three = later_y(early)
-    late_other, early_three, low = together((late_other, early_three, low))
+    early_three, low = together((early_three, low))
     early_tail = sum(part.astype(f32) for part in early_three)
     early_sum = early.astype(f32) + early_tail
+    early_sent = jnp.where(zh == 1, early_sum, early_tail).astype(b16)
+    early_sent, low = together((early_sent, low))
+    early_other = swap(early_sent, "zh", 1)
+    low = low_step(low, "x", 3)
+    late_other, low = together((late_other, low))
     late_pair = late.astype(f32) + late_other.astype(f32)
-    early_other = swap(jnp.where(zh == 1, early_sum, early_tail).astype(b16), "zh", 1)
-    low = low_step(low, "x", 3)
-    late_sent, low = together((late_pair.astype(b16), low))
+    late_sent = late_pair.astype(b16)
     late_three = later_y(late_sent)
     late_tail = sum(part.astype(f32) for part in late_three)
     late_out = (jnp.where(zh == 0, late_pair, late.astype(f32)) + late_tail).astype(b16)

time: 199 us -> 198 us (level)
  the two profiles are of different devices: /device:TPU:41 before, /device:TPU:105 now
where the time goes in v4:
time: 198 us; the launch traced here: 197 us
  starting transfers between devices  106 us (54%)
  waiting for transfers between devices  65 us (33%)
  other arithmetic  8.59 us (4%)
  matrix products  7.35 us (4%)
  blocking collectives  6.95 us (4%)
    ppermute x17, starting transfers between devices, swap(): return lax.ppermute(value, axis, [(i, i ^ mask) for i in range(count)])  81.8 us
    ppermute x17, waiting for transfers between devices, swap(): return lax.ppermute(value, axis, [(i, i ^ mask) for i in range(count)])  57.5 us
    all_to_all x1, starting transfers between devices, reduce_rows(): return jnp.sum(lax.all_to_all(spread, 'zl', 0, 0), axis=0)  13.3 us
    ppermute x6, starting transfers between devices, later_y(): lax.ppermute(value, 'y', [(i, i - d) for i in range(d, count)])  10.6 us
    psum x1, blocking collectives, reduce_rows(): rows = lax.psum(rows, 'x')  6.95 us
    all_to_all x1, waiting for transfers between devices, reduce_rows(): return jnp.sum(lax.all_to_all(spread, 'zl', 0, 0), axis=0)  6.7 us
  transfers between devices with their start and end apart: 24, of which 10 were waited for; matrix products, arithmetic and copies ran while one was open for 5% of the time, Pallas kernels for 0%

profile of v4, /device:TPU:105, one launch (start us, length us, event | category | flops | bytes accessed | tf_op | source)
XLA Modules:
  0.0 196.7 jit_solution(4637159576406724082)
XLA Ops:
  0.7 9.0 %collective-permute-start = (bf16[24,2048]{1,0:T(8,128)(2,1)}, bf16[24,2048]{1,0:T(8,128)(2,1)S(1)}, u32[]{:S(2)}, u32[]{:S(2)}) collective-permute-start(bf16[24,2048]{1,0:T(8,128)(2,1)} %bitcast.139), channel_id=1, source_target_pairs={{0,16},{4,20},{8,24},{12,28},{16,0},{20,4},{24,8},{28,12},{1,17},{... | collective-permute-start | bytes 294920 | tf_op jit(solution)/shard_map/ppermute | solution.py:16
  9.6 0.8 multiply_convert_fusion.1
  10.4 1.5 fusion.60
  12.0 1.4 fusion.6
  13.3 4.0 %collective-permute-done = bf16[24,2048]{1,0:T(8,128)(2,1)S(1)} collective-permute-done((bf16[24,2048]{1,0:T(8,128)(2,1)}, bf16[24,2048]{1,0:T(8,128)(2,1)S(1)}, u32[]{:S(2)}, u32[]{:S(2)}) %collective-permute-start) | collective-permute-done | bytes 98336 | tf_op jit(solution)/shard_map/ppermute | solution.py:16
  17.4 0.9 select_bitcast_fusion.5
  18.4 1.9 collective-permute-start.1
  20.3 0.5 convolution_bitcast_fusion
  20.8 0.5 convolution_bitcast_fusion.1
  21.2 4.6 %collective-permute-start.2 = (bf16[2,24,2048]{2,1,0:T(8,128)(2,1)S(1)}, bf16[2,24,2048]{2,1,0:T(8,128)(2,1)S(1)}, u32[]{:S(2)}, u32[]{:S(2)}) collective-permute-start(bf16[2,24,2048]{2,1,0:T(8,128)(2,1)S(1)} %pad_maximum_fusion.4), channel_id=1, source_target_pairs={{0,2},{1,3},{2,0},{3,1},{4,6},{5,7},{6,4},{7,5},{8,10},{9,11},{10,... | collective-permute-start | bytes 589832 | tf_op jit(solution)/shard_map/ppermute | solution.py:16
  25.9 7.1 %collective-permute-done.1 = bf16[60,2048]{1,0:T(8,128)(2,1)S(1)} collective-permute-done((bf16[60,2048]{1,0:T(8,128)(2,1)S(1)}, bf16[60,2048]{1,0:T(8,128)(2,1)S(1)}, u32[]{:S(2)}, u32[]{:S(2)}) %collective-permute-start.1) | collective-permute-done | bytes 245792 | tf_op jit(solution)/shard_map/ppermute | solution.py:16
  33.1 1.9 collective-permute-start.4
  35.0 3.1 %collective-permute-start.5 = (bf16[2,2,24,2048]{3,2,0,1:T(8,128)(2,1)S(1)}, bf16[2,2,24,2048]{3,2,0,1:T(8,128)(2,1)S(1)}, u32[]{:S(2)}, u32[]{:S(2)}) collective-permute-start(bf16[2,2,24,2048]{3,2,0,1:T(8,128)(2,1)S(1)} %pad_maximum_fusion.1), channel_id=1, source_target_pairs={{0,1},{1,0},{2,3},{3,2},{4,5},{5,4},{6,7},{7,6},{8,9},{9,8},{10,11... | collective-permute-start | bytes 1179656 | tf_op jit(solution)/shard_map/ppermute | solution.py:16
  38.1 3.7 %collective-permute-start.6 = (bf16[2,2,24,2048]{3,2,0,1:T(8,128)(2,1)S(1)}, bf16[2,2,24,2048]{3,2,0,1:T(8,128)(2,1)S(1)}, u32[]{:S(2)}, u32[]{:S(2)}) collective-permute-start(bf16[2,2,24,2048]{3,2,0,1:T(8,128)(2,1)S(1)} %pad_maximum_fusion.1), channel_id=1, source_target_pairs={{0,3},{1,2},{2,1},{3,0},{4,7},{5,6},{6,5},{7,4},{8,11},{9,10},{10,... | collective-permute-start | bytes 1179656 | tf_op jit(solution)/shard_map/ppermute | solution.py:16
  41.9 2.6 %collective-permute-start.3 = (bf16[2,24,2048]{2,1,0:T(8,128)(2,1)S(1)}, bf16[2,24,2048]{2,1,0:T(8,128)(2,1)S(1)}, u32[]{:S(2)}, u32[]{:S(2)}) collective-permute-start(bf16[2,24,2048]{2,1,0:T(8,128)(2,1)S(1)} %bitcast.129), channel_id=1, source_target_pairs={{0,2},{1,3},{2,0},{3,1},{4,6},{5,7},{6,4},{7,5},{8,10},{9,11},{10,... | collective-permute-start | bytes 589832 | tf_op jit(solution)/shard_map/ppermute | solution.py:16
  44.4 7.9 %collective-permute-start.7 = (bf16[12,2048]{1,0:T(8,128)(2,1)S(1)}, bf16[12,2048]{1,0:T(8,128)(2,1)S(1)}, u32[]{:S(2)}, u32[]{:S(2)}) collective-permute-start(bf16[12,2048]{1,0:T(8,128)(2,1)S(1)} %convert_element_type.112), channel_id=1, source_target_pairs={{0,16},{4,20},{8,24},{12,28},{16,0},{20,4},{24,8},{28,12},{1,17},{... | collective-permute-start | bytes 147464 | tf_op jit(solution)/shard_map/ppermute | solution.py:16
  52.8 3.1 %collective-permute-done.7 = bf16[12,2048]{1,0:T(8,128)(2,1)S(1)} collective-permute-done((bf16[12,2048]{1,0:T(8,128)(2,1)S(1)}, bf16[12,2048]{1,0:T(8,128)(2,1)S(1)}, u32[]{:S(2)}, u32[]{:S(2)}) %collective-permute-start.7) | collective-permute-done | bytes 49184 | tf_op jit(solution)/shard_map/ppermute | solution.py:16
  56.0 2.0 %collective-permute-start.9 = (bf16[2,2,24,2048]{3,2,0,1:T(8,128)(2,1)S(1)}, bf16[2,2,24,2048]{3,2,0,1:T(8,128)(2,1)S(1)}, u32[]{:S(2)}, u32[]{:S(2)}) collective-permute-start(bf16[2,2,24,2048]{3,2,0,1:T(8,128)(2,1)S(1)} %collective-permute-done.4), channel_id=1, source_target_pairs={{0,1},{1,0},{2,3},{3,2},{4,5},{5,4},{6,7},{7,6},{8,9},{9,8},{10,11... | collective-permute-start | bytes 1179656 | tf_op jit(solution)/shard_map/ppermute | solution.py:16
  58.0 3.7 %collective-permute-start.10 = (bf16[2,2,24,2048]{3,2,0,1:T(8,128)(2,1)S(1)}, bf16[2,2,24,2048]{3,2,0,1:T(8,128)(2,1)S(1)}, u32[]{:S(2)}, u32[]{:S(2)}) collective-permute-start(bf16[2,2,24,2048]{3,2,0,1:T(8,128)(2,1)S(1)} %collective-permute-done.4), channel_id=1, source_target_pairs={{0,3},{1,2},{2,1},{3,0},{4,7},{5,6},{6,5},{7,4},{8,11},{9,10},{10,... | collective-permute-start | bytes 1179656 | tf_op jit(solution)/shard_map/ppermute | solution.py:16
  61.9 3.1 %collective-permute-start.8 = (bf16[108,2048]{1,0:T(8,128)(2,1)S(1)}, bf16[108,2048]{1,0:T(8,128)(2,1)S(1)}, u32[]{:S(2)}, u32[]{:S(2)}) collective-permute-start(bf16[108,2048]{1,0:T(8,128)(2,1)S(1)} %pad_maximum_fusion), channel_id=1, source_target_pairs={{0,4},{4,0},{8,12},{12,8},{16,20},{20,16},{24,28},{28,24},{1,5},{5... | collective-permute-start | bytes 1327112 | tf_op jit(solution)/shard_map/ppermute | solution.py:16
  65.1 7.2 %collective-permute-done.8 = bf16[108,2048]{1,0:T(8,128)(2,1)S(1)} collective-permute-done((bf16[108,2048]{1,0:T(8,128)(2,1)S(1)}, bf16[108,2048]{1,0:T(8,128)(2,1)S(1)}, u32[]{:S(2)}, u32[]{:S(2)}) %collective-permute-start.8) | collective-permute-done | bytes 442400 | tf_op jit(solution)/shard_map/ppermute | solution.py:16
  72.6 3.1 %fusion.7 = (f32[768]{0:T(1024)S(1)}, f32[768,512]{1,0:T(8,128)}) fusion(bf16[1,768,512]{2,1,0:T(8,128)(2,1)S(1)} %copy-done, f32[512]{0:T(512)S(1)} %bitcast.141, bf16[768,2048]{1,0:T(8,128)(2,1)S(1)} %bitcast.117, f32[1,512,1024]{2,1,0:T(8,128)S(1)} %convolution_bitcast_fusion, f32[1,512,1024]{2,1,0:T(8,128)S(1)} %convolution_bitcast_fusion.1, ...), kind=kOutput, calls=%fused_computation.12 | convolution fusion | flops 1617427712 | bytes 11801600 | tf_op jit(solution)/shard_map/dot_general | solution.py:110
  75.7 7.0 %psum.7 = f32[2,768]{1,0:T(2,128)S(1)} all-reduce(f32[2,768]{1,0:T(2,128)S(1)} %pad_maximum_fusion.5), channel_id=1, replica_groups=mesh['dp'=2,'y'=4,'zh'=2,'zl'=8,'x'=4] {'x'}, use_global_device_ids=true, to_apply=%region_2.3 | all-reduce | flops 1536 | bytes 12288 | tf_op jit(solution)/shard_map/psum | solution.py:171
  82.7 0.6 broadcast_in_dim.11
  83.3 13.3 %all-to-all-start = ((f32[8,2,768]{2,1,0:T(2,128)}), f32[8,2,768]{2,1,0:T(2,128)S(1)}, u32[]{:S(2)}, u32[]{:S(2)}) async-start(f32[8,2,768]{2,1,0:T(2,128)} %broadcast_in_dim.11), calls=%async_computation | async-start | bytes 98304 | tf_op jit(solution)/shard_map/all_to_all | solution.py:173
  96.7 6.7 %all-to-all-done = f32[8,2,768]{2,1,0:T(2,128)S(1)} async-done(((f32[8,2,768]{2,1,0:T(2,128)}), f32[8,2,768]{2,1,0:T(2,128)S(1)}, u32[]{:S(2)}, u32[]{:S(2)}) %all-to-all-start) | async-done | bytes 49184 | tf_op jit(solution)/shard_map/all_to_all | solution.py:173
  103.4 1.9 fusion.10
  105.5 11.4 %collective-permute-start.16 = (bf16[384,512]{1,0:T(8,128)(2,1)S(1)}, bf16[384,512]{1,0:T(8,128)(2,1)S(1)}, u32[]{:S(2)}, u32[]{:S(2)}) collective-permute-start(bf16[384,512]{1,0:T(8,128)(2,1)S(1)} %get-tuple-element.64), channel_id=1, source_target_pairs={{0,32},{32,0},{1,33},{33,1},{2,34},{34,2},{3,35},{35,3},{4,36},{36... | collective-permute-start | bytes 1179656 | tf_op jit(solution)/shard_map/ppermute | solution.py:16
  116.9 2.5 %collective-permute-start.11 = (bf16[12,2048]{1,0:T(8,128)(2,1)S(1)}, bf16[12,2048]{1,0:T(8,128)(2,1)S(1)}, u32[]{:S(2)}, u32[]{:S(2)}) collective-permute-start(bf16[12,2048]{1,0:T(8,128)(2,1)S(1)} %convert_element_type.120), channel_id=1, source_target_pairs={{0,1},{1,0},{2,3},{3,2},{4,5},{5,4},{6,7},{7,6},{8,9},{9,8},{10,11... | collective-permute-start | bytes 147464 | tf_op jit(solution)/shard_map/ppermute | solution.py:16
  119.5 0.5 fusion.32
  120.0 1.9 collective-permute-done.11
  121.9 2.1 %collective-permute-start.12 = (bf16[384,512]{1,0:T(8,128)(2,1)S(1)}, bf16[384,512]{1,0:T(8,128)(2,1)S(1)}, u32[]{:S(2)}, u32[]{:S(2)}) collective-permute-start(bf16[384,512]{1,0:T(8,128)(2,1)S(1)} %get-tuple-element.50), channel_id=1, source_target_pairs={{64,0},{128,64},{192,128},{65,1},{129,65},{193,129},{66,2},{130,66... | collective-permute-start | bytes 1179656 | tf_op jit(solution)/shard_map/ppermute | solution.py:27
  124.0 1.3 collective-permute-start.13
  125.3 0.7 collective-permute-start.14
  126.0 0.5 fusion.29
  126.8 9.2 %collective-permute-start.21 = (f32[512,32]{0,1:T(8,128)S(1)}, f32[512,32]{0,1:T(8,128)S(1)}, u32[]{:S(2)}, u32[]{:S(2)}) collective-permute-start(f32[512,32]{0,1:T(8,128)S(1)} %fusion.28), channel_id=1, source_target_pairs={{0,256},{256,0},{1,257},{257,1},{2,258},{258,2},{3,259},{259,3},{4... | collective-permute-start | bytes 196616 | tf_op jit(solution)/shard_map/ppermute | solution.py:16
  136.0 0.9 collective-permute-done.13
  137.1 2.7 %collective-permute-start.17 = (bf16[12,2048]{1,0:T(8,128)(2,1)S(1)}, bf16[12,2048]{1,0:T(8,128)(2,1)S(1)}, u32[]{:S(2)}, u32[]{:S(2)}) collective-permute-start(bf16[12,2048]{1,0:T(8,128)(2,1)S(1)} %convert_element_type.130), channel_id=1, source_target_pairs={{0,3},{1,2},{2,1},{3,0},{4,7},{5,6},{6,5},{7,4},{8,11},{9,10},{10,... | collective-permute-start | bytes 147464 | tf_op jit(solution)/shard_map/ppermute | solution.py:16
  139.8 0.6 add_bitcast_fusion.1
  140.5 2.0 %collective-permute-start.15 = (bf16[384,512]{1,0:T(8,128)(2,1)S(1)}, bf16[384,512]{1,0:T(8,128)(2,1)S(1)}, u32[]{:S(2)}, u32[]{:S(2)}) collective-permute-start(bf16[384,512]{1,0:T(8,128)(2,1)S(1)} %select_convert_fusion), channel_id=1, source_target_pairs={{0,32},{32,0},{1,33},{33,1},{2,34},{34,2},{3,35},{35,3},{4,36},{36... | collective-permute-start | bytes 1179656 | tf_op jit(solution)/shard_map/ppermute | solution.py:16
  142.5 1.1 collective-permute-done.17
  144.7 10.4 %collective-permute-start.22 = (f32[2,16,1024]{2,1,0:T(8,128)S(1)}, f32[2,16,1024]{2,1,0:T(8,128)S(1)}, u32[]{:S(2)}, u32[]{:S(2)}) collective-permute-start(f32[2,16,1024]{2,1,0:T(8,128)S(1)} %maximum_multiply_fusion.1), channel_id=1, source_target_pairs={{0,256},{256,0},{1,257},{257,1},{2,258},{258,2},{3,259},{259,3},{4... | collective-permute-start | bytes 393224 | tf_op jit(solution)/shard_map/ppermute | solution.py:16
  155.3 0.7 collective-permute-start.20
  155.9 1.3 collective-permute-start.19
  157.2 4.6 %collective-permute-start.18 = (bf16[384,512]{1,0:T(8,128)(2,1)S(1)}, bf16[384,512]{1,0:T(8,128)(2,1)S(1)}, u32[]{:S(2)}, u32[]{:S(2)}) collective-permute-start(bf16[384,512]{1,0:T(8,128)(2,1)S(1)} %fusion.38), channel_id=1, source_target_pairs={{64,0},{128,64},{192,128},{65,1},{129,65},{193,129},{66,2},{130,66... | collective-permute-start | bytes 1179656 | tf_op jit(solution)/shard_map/ppermute | solution.py:27
  161.9 0.7 add_bitcast_fusion
  162.5 32.6 %collective-permute-done.15 = bf16[384,512]{1,0:T(8,128)(2,1)S(1)} collective-permute-done((bf16[384,512]{1,0:T(8,128)(2,1)S(1)}, bf16[384,512]{1,0:T(8,128)(2,1)S(1)}, u32[]{:S(2)}, u32[]{:S(2)}) %collective-permute-start.15) | collective-permute-done | bytes 393248 | tf_op jit(solution)/shard_map/ppermute | solution.py:16
  195.7 0.9 maximum_bitcast_fusion
  (77 shorter events, 3.5 us)
Async XLA Ops:
  0.6 19.7 %copy-start.2 = (bf16[1,512,32]{1,2,0:T(8,128)(2,1)S(1)}, bf16[1,512,32]{1,2,0:T(8,128)(2,1)}, u32[]{:S(2)}) copy-start(bf16[1,512,32]{1,2,0:T(8,128)(2,1)} %param.9) | copy-start | bytes 98308
  0.6 19.7 %copy-start.3 = (bf16[1,2,16,1024]{3,2,1,0:T(8,128)(2,1)S(1)}, bf16[1,2,16,1024]{3,2,1,0:T(8,128)(2,1)}, u32[]{:S(2)}) copy-start(bf16[1,2,16,1024]{3,2,1,0:T(8,128)(2,1)} %param.10) | copy-start | bytes 196612
  0.7 16.7 %collective-permute-start = (bf16[24,2048]{1,0:T(8,128)(2,1)}, bf16[24,2048]{1,0:T(8,128)(2,1)S(1)}, u32[]{:S(2)}, u32[]{:S(2)}) collective-permute-start(bf16[24,2048]{1,0:T(8,128)(2,1)} %bitcast.139), channel_id=1, source_target_pairs={{0,16},{4,20},{8,24},{12,28},{16,0},{20,4},{24,8},{28,12},{1,17},{... | collective-permute-start | bytes 294920 | tf_op jit(solution)/shard_map/ppermute | solution.py:16
  18.4 14.6 %collective-permute-start.1 = (bf16[60,2048]{1,0:T(8,128)(2,1)S(1)}, bf16[60,2048]{1,0:T(8,128)(2,1)S(1)}, u32[]{:S(2)}, u32[]{:S(2)}) collective-permute-start(bf16[60,2048]{1,0:T(8,128)(2,1)S(1)} %pad_maximum_fusion.3), channel_id=1, source_target_pairs={{0,8},{4,12},{8,0},{12,4},{16,24},{20,28},{24,16},{28,20},{1,9},{5... | collective-permute-start | bytes 737288 | tf_op jit(solution)/shard_map/ppermute | solution.py:16
  21.2 11.9 %collective-permute-start.2 = (bf16[2,24,2048]{2,1,0:T(8,128)(2,1)S(1)}, bf16[2,24,2048]{2,1,0:T(8,128)(2,1)S(1)}, u32[]{:S(2)}, u32[]{:S(2)}) collective-permute-start(bf16[2,24,2048]{2,1,0:T(8,128)(2,1)S(1)} %pad_maximum_fusion.4), channel_id=1, source_target_pairs={{0,2},{1,3},{2,0},{3,1},{4,6},{5,7},{6,4},{7,5},{8,10},{9,11},{10,... | collective-permute-start | bytes 589832 | tf_op jit(solution)/shard_map/ppermute | solution.py:16
  33.1 22.8 %collective-permute-start.4 = (bf16[2,2,24,2048]{3,2,0,1:T(8,128)(2,1)S(1)}, bf16[2,2,24,2048]{3,2,0,1:T(8,128)(2,1)S(1)}, u32[]{:S(2)}, u32[]{:S(2)}) collective-permute-start(bf16[2,2,24,2048]{3,2,0,1:T(8,128)(2,1)S(1)} %pad_maximum_fusion.1), channel_id=1, source_target_pairs={{0,4},{4,0},{8,12},{12,8},{16,20},{20,16},{24,28},{28,24},{1,5},{5... | collective-permute-start | bytes 1179656 | tf_op jit(solution)/shard_map/ppermute | solution.py:16
  35.0 20.9 %collective-permute-start.5 = (bf16[2,2,24,2048]{3,2,0,1:T(8,128)(2,1)S(1)}, bf16[2,2,24,2048]{3,2,0,1:T(8,128)(2,1)S(1)}, u32[]{:S(2)}, u32[]{:S(2)}) collective-permute-start(bf16[2,2,24,2048]{3,2,0,1:T(8,128)(2,1)S(1)} %pad_maximum_fusion.1), channel_id=1, source_target_pairs={{0,1},{1,0},{2,3},{3,2},{4,5},{5,4},{6,7},{7,6},{8,9},{9,8},{10,11... | collective-permute-start | bytes 1179656 | tf_op jit(solution)/shard_map/ppermute | solution.py:16
  38.1 17.8 %collective-permute-start.6 = (bf16[2,2,24,2048]{3,2,0,1:T(8,128)(2,1)S(1)}, bf16[2,2,24,2048]{3,2,0,1:T(8,128)(2,1)S(1)}, u32[]{:S(2)}, u32[]{:S(2)}) collective-permute-start(bf16[2,2,24,2048]{3,2,0,1:T(8,128)(2,1)S(1)} %pad_maximum_fusion.1), channel_id=1, source_target_pairs={{0,3},{1,2},{2,1},{3,0},{4,7},{5,6},{6,5},{7,4},{8,11},{9,10},{10,... | collective-permute-start | bytes 1179656 | tf_op jit(solution)/shard_map/ppermute | solution.py:16
  41.9 14.0 %collective-permute-start.3 = (bf16[2,24,2048]{2,1,0:T(8,128)(2,1)S(1)}, bf16[2,24,2048]{2,1,0:T(8,128)(2,1)S(1)}, u32[]{:S(2)}, u32[]{:S(2)}) collective-permute-start(bf16[2,24,2048]{2,1,0:T(8,128)(2,1)S(1)} %bitcast.129), channel_id=1, source_target_pairs={{0,2},{1,3},{2,0},{3,1},{4,6},{5,7},{6,4},{7,5},{8,10},{9,11},{10,... | collective-permute-start | bytes 589832 | tf_op jit(solution)/shard_map/ppermute | solution.py:16
  44.4 11.4 %collective-permute-start.7 = (bf16[12,2048]{1,0:T(8,128)(2,1)S(1)}, bf16[12,2048]{1,0:T(8,128)(2,1)S(1)}, u32[]{:S(2)}, u32[]{:S(2)}) collective-permute-start(bf16[12,2048]{1,0:T(8,128)(2,1)S(1)} %convert_element_type.112), channel_id=1, source_target_pairs={{0,16},{4,20},{8,24},{12,28},{16,0},{20,4},{24,8},{28,12},{1,17},{... | collective-permute-start | bytes 147464 | tf_op jit(solution)/shard_map/ppermute | solution.py:16
  56.0 16.5 %collective-permute-start.9 = (bf16[2,2,24,2048]{3,2,0,1:T(8,128)(2,1)S(1)}, bf16[2,2,24,2048]{3,2,0,1:T(8,128)(2,1)S(1)}, u32[]{:S(2)}, u32[]{:S(2)}) collective-permute-start(bf16[2,2,24,2048]{3,2,0,1:T(8,128)(2,1)S(1)} %collective-permute-done.4), channel_id=1, source_target_pairs={{0,1},{1,0},{2,3},{3,2},{4,5},{5,4},{6,7},{7,6},{8,9},{9,8},{10,11... | collective-permute-start | bytes 1179656 | tf_op jit(solution)/shard_map/ppermute | solution.py:16
  58.0 14.5 %collective-permute-start.10 = (bf16[2,2,24,2048]{3,2,0,1:T(8,128)(2,1)S(1)}, bf16[2,2,24,2048]{3,2,0,1:T(8,128)(2,1)S(1)}, u32[]{:S(2)}, u32[]{:S(2)}) collective-permute-start(bf16[2,2,24,2048]{3,2,0,1:T(8,128)(2,1)S(1)} %collective-permute-done.4), channel_id=1, source_target_pairs={{0,3},{1,2},{2,1},{3,0},{4,7},{5,6},{6,5},{7,4},{8,11},{9,10},{10,... | collective-permute-start | bytes 1179656 | tf_op jit(solution)/shard_map/ppermute | solution.py:16
  61.8 10.8 %copy-start = (bf16[1,768,512]{2,1,0:T(8,128)(2,1)S(1)}, bf16[1,768,512]{2,1,0:T(8,128)(2,1)}, u32[]{:S(2)}) copy-start(bf16[1,768,512]{2,1,0:T(8,128)(2,1)} %param.6) | copy-start | bytes 2359300
  61.9 10.8 %copy-start.4 = (f32[1,512]{1,0:T(1,128)S(1)}, f32[1,512]{1,0:T(1,128)}, u32[]{:S(2)}) copy-start(f32[1,512]{1,0:T(1,128)} %param.11) | copy-start | bytes 6148
  61.9 10.8 %copy-start.5 = (bf16[1,512,2048]{2,1,0:T(8,128)(2,1)S(1)}, bf16[1,512,2048]{2,1,0:T(8,128)(2,1)}, u32[]{:S(2)}) copy-start(bf16[1,512,2048]{2,1,0:T(8,128)(2,1)} %param.8) | copy-start | bytes 6291460
  61.9 10.5 %collective-permute-start.8 = (bf16[108,2048]{1,0:T(8,128)(2,1)S(1)}, bf16[108,2048]{1,0:T(8,128)(2,1)S(1)}, u32[]{:S(2)}, u32[]{:S(2)}) collective-permute-start(bf16[108,2048]{1,0:T(8,128)(2,1)S(1)} %pad_maximum_fusion), channel_id=1, source_target_pairs={{0,4},{4,0},{8,12},{12,8},{16,20},{20,16},{24,28},{28,24},{1,5},{5... | collective-permute-start | bytes 1327112 | tf_op jit(solution)/shard_map/ppermute | solution.py:16
  83.3 20.0 %all-to-all-start = ((f32[8,2,768]{2,1,0:T(2,128)}), f32[8,2,768]{2,1,0:T(2,128)S(1)}, u32[]{:S(2)}, u32[]{:S(2)}) async-start(f32[8,2,768]{2,1,0:T(2,128)} %broadcast_in_dim.11), calls=%async_computation | async-start | bytes 98304 | tf_op jit(solution)/shard_map/all_to_all | solution.py:173
  105.4 21.1 %copy-start.1 = (bf16[1,768,512]{2,1,0:T(8,128)(2,1)S(1)}, bf16[1,768,512]{2,1,0:T(8,128)(2,1)}, u32[]{:S(2)}) copy-start(bf16[1,768,512]{2,1,0:T(8,128)(2,1)} %param.6) | copy-start | bytes 2359300
  105.5 38.5 %collective-permute-start.16 = (bf16[384,512]{1,0:T(8,128)(2,1)S(1)}, bf16[384,512]{1,0:T(8,128)(2,1)S(1)}, u32[]{:S(2)}, u32[]{:S(2)}) collective-permute-start(bf16[384,512]{1,0:T(8,128)(2,1)S(1)} %get-tuple-element.64), channel_id=1, source_target_pairs={{0,32},{32,0},{1,33},{33,1},{2,34},{34,2},{3,35},{35,3},{4,36},{36... | collective-permute-start | bytes 1179656 | tf_op jit(solution)/shard_map/ppermute | solution.py:16
  116.9 5.0 %collective-permute-start.11 = (bf16[12,2048]{1,0:T(8,128)(2,1)S(1)}, bf16[12,2048]{1,0:T(8,128)(2,1)S(1)}, u32[]{:S(2)}, u32[]{:S(2)}) collective-permute-start(bf16[12,2048]{1,0:T(8,128)(2,1)S(1)} %convert_element_type.120), channel_id=1, source_target_pairs={{0,1},{1,0},{2,3},{3,2},{4,5},{5,4},{6,7},{7,6},{8,9},{9,8},{10,11... | collective-permute-start | bytes 147464 | tf_op jit(solution)/shard_map/ppermute | solution.py:16
  121.9 14.1 %collective-permute-start.12 = (bf16[384,512]{1,0:T(8,128)(2,1)S(1)}, bf16[384,512]{1,0:T(8,128)(2,1)S(1)}, u32[]{:S(2)}, u32[]{:S(2)}) collective-permute-start(bf16[384,512]{1,0:T(8,128)(2,1)S(1)} %get-tuple-element.50), channel_id=1, source_target_pairs={{64,0},{128,64},{192,128},{65,1},{129,65},{193,129},{66,2},{130,66... | collective-permute-start | bytes 1179656 | tf_op jit(solution)/shard_map/ppermute | solution.py:27
  124.0 12.8 %collective-permute-start.13 = (bf16[384,512]{1,0:T(8,128)(2,1)S(1)}, bf16[384,512]{1,0:T(8,128)(2,1)S(1)}, u32[]{:S(2)}, u32[]{:S(2)}) collective-permute-start(bf16[384,512]{1,0:T(8,128)(2,1)S(1)} %get-tuple-element.50), channel_id=1, source_target_pairs={{128,0},{192,64},{129,1},{193,65},{130,2},{194,66},{131,3},{195,67... | collective-permute-start | bytes 1179656 | tf_op jit(solution)/shard_map/ppermute | solution.py:27
  125.3 11.5 %collective-permute-start.14 = (bf16[384,512]{1,0:T(8,128)(2,1)S(1)}, bf16[384,512]{1,0:T(8,128)(2,1)S(1)}, u32[]{:S(2)}, u32[]{:S(2)}) collective-permute-start(bf16[384,512]{1,0:T(8,128)(2,1)S(1)} %get-tuple-element.50), channel_id=1, source_target_pairs={{192,0},{193,1},{194,2},{195,3},{196,4},{197,5},{198,6},{199,7},{2... | collective-permute-start | bytes 1179656 | tf_op jit(solution)/shard_map/ppermute | solution.py:27
  126.8 13.1 %collective-permute-start.21 = (f32[512,32]{0,1:T(8,128)S(1)}, f32[512,32]{0,1:T(8,128)S(1)}, u32[]{:S(2)}, u32[]{:S(2)}) collective-permute-start(f32[512,32]{0,1:T(8,128)S(1)} %fusion.28), channel_id=1, source_target_pairs={{0,256},{256,0},{1,257},{257,1},{2,258},{258,2},{3,259},{259,3},{4... | collective-permute-start | bytes 196616 | tf_op jit(solution)/shard_map/ppermute | solution.py:16
  137.1 6.5 %collective-permute-start.17 = (bf16[12,2048]{1,0:T(8,128)(2,1)S(1)}, bf16[12,2048]{1,0:T(8,128)(2,1)S(1)}, u32[]{:S(2)}, u32[]{:S(2)}) collective-permute-start(bf16[12,2048]{1,0:T(8,128)(2,1)S(1)} %convert_element_type.130), channel_id=1, source_target_pairs={{0,3},{1,2},{2,1},{3,0},{4,7},{5,6},{6,5},{7,4},{8,11},{9,10},{10,... | collective-permute-start | bytes 147464 | tf_op jit(solution)/shard_map/ppermute | solution.py:16
  140.5 54.7 %collective-permute-start.15 = (bf16[384,512]{1,0:T(8,128)(2,1)S(1)}, bf16[384,512]{1,0:T(8,128)(2,1)S(1)}, u32[]{:S(2)}, u32[]{:S(2)}) collective-permute-start(bf16[384,512]{1,0:T(8,128)(2,1)S(1)} %select_convert_fusion), channel_id=1, source_target_pairs={{0,32},{32,0},{1,33},{33,1},{2,34},{34,2},{3,35},{35,3},{4,36},{36... | collective-permute-start | bytes 1179656 | tf_op jit(solution)/shard_map/ppermute | solution.py:16
  144.7 17.1 %collective-permute-start.22 = (f32[2,16,1024]{2,1,0:T(8,128)S(1)}, f32[2,16,1024]{2,1,0:T(8,128)S(1)}, u32[]{:S(2)}, u32[]{:S(2)}) collective-permute-start(f32[2,16,1024]{2,1,0:T(8,128)S(1)} %maximum_multiply_fusion.1), channel_id=1, source_target_pairs={{0,256},{256,0},{1,257},{257,1},{2,258},{258,2},{3,259},{259,3},{4... | collective-permute-start | bytes 393224 | tf_op jit(solution)/shard_map/ppermute | solution.py:16
  155.3 40.2 %collective-permute-start.20 = (bf16[384,512]{1,0:T(8,128)(2,1)S(1)}, bf16[384,512]{1,0:T(8,128)(2,1)S(1)}, u32[]{:S(2)}, u32[]{:S(2)}) collective-permute-start(bf16[384,512]{1,0:T(8,128)(2,1)S(1)} %fusion.38), channel_id=1, source_target_pairs={{192,0},{193,1},{194,2},{195,3},{196,4},{197,5},{198,6},{199,7},{2... | collective-permute-start | bytes 1179656 | tf_op jit(solution)/shard_map/ppermute | solution.py:27
  155.9 39.5 %collective-permute-start.19 = (bf16[384,512]{1,0:T(8,128)(2,1)S(1)}, bf16[384,512]{1,0:T(8,128)(2,1)S(1)}, u32[]{:S(2)}, u32[]{:S(2)}) collective-permute-start(bf16[384,512]{1,0:T(8,128)(2,1)S(1)} %fusion.38), channel_id=1, source_target_pairs={{128,0},{192,64},{129,1},{193,65},{130,2},{194,66},{131,3},{195,67... | collective-permute-start | bytes 1179656 | tf_op jit(solution)/shard_map/ppermute | solution.py:27
  157.2 38.2 %collective-permute-start.18 = (bf16[384,512]{1,0:T(8,128)(2,1)S(1)}, bf16[384,512]{1,0:T(8,128)(2,1)S(1)}, u32[]{:S(2)}, u32[]{:S(2)}) collective-permute-start(bf16[384,512]{1,0:T(8,128)(2,1)S(1)} %fusion.38), channel_id=1, source_target_pairs={{64,0},{128,64},{192,128},{65,1},{129,65},{193,129},{66,2},{130,66... | collective-permute-start | bytes 1179656 | tf_op jit(solution)/shard_map/ppermute | solution.py:27

commit v5 on v4

--- a/solution.py
+++ b/solution.py
@@ -25,6 +25,11 @@
 def later_y(value):
     count = lax.axis_size("y")
     return [lax.ppermute(value, "y", [(i, i - d) for i in range(d, count)]) for d in range(1, count)]
+
+
+def cross(value, lower):
+    pairs = [(2 * y + 1, 2 * y) for y in range(sizes["y"])] + [(2 * y, 2 * y + 1) for y in lower]
+    return lax.ppermute(value, section_axes, pairs)
 
 
 def local(
@@ -118,7 +123,7 @@
 
     cut = tokens // 2
     early, late = branch[:cut], branch[cut:]
-    late_other = swap(late, "zh", 1)
+    late_other = cross(late, range(1, sizes["y"]))
     low = low_step(low, "x", 1)
     early, low = together((early, low))
     early_three = later_y(early)
@@ -127,7 +132,7 @@
     early_sum = early.astype(f32) + early_tail
     early_sent = jnp.where(zh == 1, early_sum, early_tail).astype(b16)
     early_sent, low = together((early_sent, low))
-    early_other = swap(early_sent, "zh", 1)
+    early_other = cross(early_sent, range(sizes["y"] - 1))
     low = low_step(low, "x", 3)
     late_other, low = together((late_other, low))
     late_pair = late.astype(f32) + late_other.astype(f32)

time: 198 us -> 198 us (level)
  the two profiles are of different devices: /device:TPU:105 before, /device:TPU:32 now
where the time goes in v5:
time: 198 us; the launch traced here: 197 us
  waiting for transfers between devices  85.9 us (43%)
  starting transfers between devices  83.5 us (42%)
  blocking collectives  8.97 us (5%)
  other arithmetic  8.59 us (4%)
  matrix products  7.35 us (4%)
    ppermute x15, starting transfers between devices, swap(): return lax.ppermute(value, axis, [(i, i ^ mask) for i in range(count)])  59.7 us
    ppermute x2, waiting for transfers between devices, cross(): return lax.ppermute(value, section_axes, pairs)  32.2 us
    ppermute x15, waiting for transfers between devices, swap(): return lax.ppermute(value, axis, [(i, i ^ mask) for i in range(count)])  24 us
    ppermute x6, waiting for transfers between devices, later_y(): lax.ppermute(value, 'y', [(i, i - d) for i in range(d, count)])  20.5 us
    all_to_all x1, starting transfers between devices, reduce_rows(): return jnp.sum(lax.all_to_all(spread, 'zl', 0, 0), axis=0)  12 us
    all_to_all x1, waiting for transfers between devices, reduce_rows(): return jnp.sum(lax.all_to_all(spread, 'zl', 0, 0), axis=0)  9.18 us
    psum x1, blocking collectives, reduce_rows(): rows = lax.psum(rows, 'x')  8.97 us
    ppermute x6, starting transfers between devices, later_y(): lax.ppermute(value, 'y', [(i, i - d) for i in range(d, count)])  7.75 us
  transfers between devices with their start and end apart: 24, of which 12 were waited for; matrix products, arithmetic and copies ran while one was open for 5% of the time, Pallas kernels for 0%

profile of v5, /device:TPU:32, one launch (start us, length us, event | category | flops | bytes accessed | tf_op | source)
XLA Modules:
  0.0 197.3 jit_solution(27546943637170684)
XLA Ops:
  0.7 9.2 %collective-permute-start = (bf16[24,2048]{1,0:T(8,128)(2,1)}, bf16[24,2048]{1,0:T(8,128)(2,1)S(1)}, u32[]{:S(2)}, u32[]{:S(2)}) collective-permute-start(bf16[24,2048]{1,0:T(8,128)(2,1)} %bitcast.139), channel_id=1, source_target_pairs={{0,16},{4,20},{8,24},{12,28},{16,0},{20,4},{24,8},{28,12},{1,17},{... | collective-permute-start | bytes 294920 | tf_op jit(solution)/shard_map/ppermute | solution.py:16
  9.9 0.8 multiply_convert_fusion.1
  10.7 1.5 fusion.60
  12.3 1.4 fusion.6
  13.6 3.6 %collective-permute-done = bf16[24,2048]{1,0:T(8,128)(2,1)S(1)} collective-permute-done((bf16[24,2048]{1,0:T(8,128)(2,1)}, bf16[24,2048]{1,0:T(8,128)(2,1)S(1)}, u32[]{:S(2)}, u32[]{:S(2)}) %collective-permute-start) | collective-permute-done | bytes 98336 | tf_op jit(solution)/shard_map/ppermute | solution.py:16
  17.2 0.9 select_bitcast_fusion.5
  18.2 5.2 %collective-permute-start.1 = (bf16[60,2048]{1,0:T(8,128)(2,1)S(1)}, bf16[60,2048]{1,0:T(8,128)(2,1)S(1)}, u32[]{:S(2)}, u32[]{:S(2)}) collective-permute-start(bf16[60,2048]{1,0:T(8,128)(2,1)S(1)} %pad_maximum_fusion.3), channel_id=1, source_target_pairs={{0,8},{4,12},{8,0},{12,4},{16,24},{20,28},{24,16},{28,20},{1,9},{5... | collective-permute-start | bytes 737288 | tf_op jit(solution)/shard_map/ppermute | solution.py:16
  24.3 4.9 %collective-permute-start.2 = (bf16[2,24,2048]{2,1,0:T(8,128)(2,1)S(1)}, bf16[2,24,2048]{2,1,0:T(8,128)(2,1)S(1)}, u32[]{:S(2)}, u32[]{:S(2)}) collective-permute-start(bf16[2,24,2048]{2,1,0:T(8,128)(2,1)S(1)} %pad_maximum_fusion.4), channel_id=1, source_target_pairs={{0,2},{1,3},{2,0},{3,1},{4,6},{5,7},{6,4},{7,5},{8,10},{9,11},{10,... | collective-permute-start | bytes 589832 | tf_op jit(solution)/shard_map/ppermute | solution.py:16
  29.2 3.4 %collective-permute-done.1 = bf16[60,2048]{1,0:T(8,128)(2,1)S(1)} collective-permute-done((bf16[60,2048]{1,0:T(8,128)(2,1)S(1)}, bf16[60,2048]{1,0:T(8,128)(2,1)S(1)}, u32[]{:S(2)}, u32[]{:S(2)}) %collective-permute-start.1) | collective-permute-done | bytes 245792 | tf_op jit(solution)/shard_map/ppermute | solution.py:16
  32.8 1.5 collective-permute-done.2
  34.2 1.9 collective-permute-start.4
  36.2 3.4 %collective-permute-start.5 = (bf16[2,2,24,2048]{3,2,0,1:T(8,128)(2,1)S(1)}, bf16[2,2,24,2048]{3,2,0,1:T(8,128)(2,1)S(1)}, u32[]{:S(2)}, u32[]{:S(2)}) collective-permute-start(bf16[2,2,24,2048]{3,2,0,1:T(8,128)(2,1)S(1)} %pad_maximum_fusion.1), channel_id=1, source_target_pairs={{0,1},{1,0},{2,3},{3,2},{4,5},{5,4},{6,7},{7,6},{8,9},{9,8},{10,11... | collective-permute-start | bytes 1179656 | tf_op jit(solution)/shard_map/ppermute | solution.py:16
  39.6 4.0 %collective-permute-start.6 = (bf16[2,2,24,2048]{3,2,0,1:T(8,128)(2,1)S(1)}, bf16[2,2,24,2048]{3,2,0,1:T(8,128)(2,1)S(1)}, u32[]{:S(2)}, u32[]{:S(2)}) collective-permute-start(bf16[2,2,24,2048]{3,2,0,1:T(8,128)(2,1)S(1)} %pad_maximum_fusion.1), channel_id=1, source_target_pairs={{0,3},{1,2},{2,1},{3,0},{4,7},{5,6},{6,5},{7,4},{8,11},{9,10},{10,... | collective-permute-start | bytes 1179656 | tf_op jit(solution)/shard_map/ppermute | solution.py:16
  43.6 2.6 %collective-permute-start.3 = (bf16[2,24,2048]{2,1,0:T(8,128)(2,1)S(1)}, bf16[2,24,2048]{2,1,0:T(8,128)(2,1)S(1)}, u32[]{:S(2)}, u32[]{:S(2)}) collective-permute-start(bf16[2,24,2048]{2,1,0:T(8,128)(2,1)S(1)} %bitcast.129), channel_id=1, source_target_pairs={{0,2},{1,3},{2,0},{3,1},{4,6},{5,7},{6,4},{7,5},{8,10},{9,11},{10,... | collective-permute-start | bytes 589832 | tf_op jit(solution)/shard_map/ppermute | solution.py:16
  46.2 8.2 %collective-permute-start.7 = (bf16[12,2048]{1,0:T(8,128)(2,1)S(1)}, bf16[12,2048]{1,0:T(8,128)(2,1)S(1)}, u32[]{:S(2)}, u32[]{:S(2)}) collective-permute-start(bf16[12,2048]{1,0:T(8,128)(2,1)S(1)} %convert_element_type.112), channel_id=1, source_target_pairs={{0,16},{4,20},{8,24},{12,28},{16,0},{20,4},{24,8},{28,12},{1,17},{... | collective-permute-start | bytes 147464 | tf_op jit(solution)/shard_map/ppermute | solution.py:16
  54.8 4.7 %collective-permute-done.7 = bf16[12,2048]{1,0:T(8,128)(2,1)S(1)} collective-permute-done((bf16[12,2048]{1,0:T(8,128)(2,1)S(1)}, bf16[12,2048]{1,0:T(8,128)(2,1)S(1)}, u32[]{:S(2)}, u32[]{:S(2)}) %collective-permute-start.7) | collective-permute-done | bytes 49184 | tf_op jit(solution)/shard_map/ppermute | solution.py:16
  59.6 3.1 %collective-permute-start.9 = (bf16[2,2,24,2048]{3,2,0,1:T(8,128)(2,1)S(1)}, bf16[2,2,24,2048]{3,2,0,1:T(8,128)(2,1)S(1)}, u32[]{:S(2)}, u32[]{:S(2)}) collective-permute-start(bf16[2,2,24,2048]{3,2,0,1:T(8,128)(2,1)S(1)} %collective-permute-done.4), channel_id=1, source_target_pairs={{0,1},{1,0},{2,3},{3,2},{4,5},{5,4},{6,7},{7,6},{8,9},{9,8},{10,11... | collective-permute-start | bytes 1179656 | tf_op jit(solution)/shard_map/ppermute | solution.py:16
  62.7 4.0 %collective-permute-start.10 = (bf16[2,2,24,2048]{3,2,0,1:T(8,128)(2,1)S(1)}, bf16[2,2,24,2048]{3,2,0,1:T(8,128)(2,1)S(1)}, u32[]{:S(2)}, u32[]{:S(2)}) collective-permute-start(bf16[2,2,24,2048]{3,2,0,1:T(8,128)(2,1)S(1)} %collective-permute-done.4), channel_id=1, source_target_pairs={{0,3},{1,2},{2,1},{3,0},{4,7},{5,6},{6,5},{7,4},{8,11},{9,10},{10,... | collective-permute-start | bytes 1179656 | tf_op jit(solution)/shard_map/ppermute | solution.py:16
  66.9 4.2 %collective-permute-start.8 = (bf16[108,2048]{1,0:T(8,128)(2,1)S(1)}, bf16[108,2048]{1,0:T(8,128)(2,1)S(1)}, u32[]{:S(2)}, u32[]{:S(2)}) collective-permute-start(bf16[108,2048]{1,0:T(8,128)(2,1)S(1)} %pad_maximum_fusion), channel_id=1, source_target_pairs={{0,4},{4,0},{8,12},{12,8},{16,20},{20,16},{24,28},{28,24},{1,5},{5... | collective-permute-start | bytes 1327112 | tf_op jit(solution)/shard_map/ppermute | solution.py:16
  71.3 6.2 %collective-permute-done.8 = bf16[108,2048]{1,0:T(8,128)(2,1)S(1)} collective-permute-done((bf16[108,2048]{1,0:T(8,128)(2,1)S(1)}, bf16[108,2048]{1,0:T(8,128)(2,1)S(1)}, u32[]{:S(2)}, u32[]{:S(2)}) %collective-permute-start.8) | collective-permute-done | bytes 442400 | tf_op jit(solution)/shard_map/ppermute | solution.py:16
  77.8 3.1 %fusion.7 = (f32[768]{0:T(1024)S(1)}, f32[768,512]{1,0:T(8,128)}) fusion(bf16[1,768,512]{2,1,0:T(8,128)(2,1)S(1)} %copy-done, f32[512]{0:T(512)S(1)} %bitcast.141, bf16[768,2048]{1,0:T(8,128)(2,1)S(1)} %bitcast.117, f32[1,512,1024]{2,1,0:T(8,128)S(1)} %convolution_bitcast_fusion, f32[1,512,1024]{2,1,0:T(8,128)S(1)} %convolution_bitcast_fusion.1, ...), kind=kOutput, calls=%fused_computation.12 | convolution fusion | flops 1617427712 | bytes 11801600 | tf_op jit(solution)/shard_map/dot_general | solution.py:115
  80.9 9.0 %psum.7 = f32[2,768]{1,0:T(2,128)S(1)} all-reduce(f32[2,768]{1,0:T(2,128)S(1)} %pad_maximum_fusion.5), channel_id=1, replica_groups=mesh['dp'=2,'y'=4,'zh'=2,'zl'=8,'x'=4] {'x'}, use_global_device_ids=true, to_apply=%region_2.3 | all-reduce | flops 1536 | bytes 12288 | tf_op jit(solution)/shard_map/psum | solution.py:176
  89.9 0.6 broadcast_in_dim.11
  90.5 12.0 %all-to-all-start = ((f32[8,2,768]{2,1,0:T(2,128)}), f32[8,2,768]{2,1,0:T(2,128)S(1)}, u32[]{:S(2)}, u32[]{:S(2)}) async-start(f32[8,2,768]{2,1,0:T(2,128)} %broadcast_in_dim.11), calls=%async_computation | async-start | bytes 98304 | tf_op jit(solution)/shard_map/all_to_all | solution.py:178
  102.6 9.2 %all-to-all-done = f32[8,2,768]{2,1,0:T(2,128)S(1)} async-done(((f32[8,2,768]{2,1,0:T(2,128)}), f32[8,2,768]{2,1,0:T(2,128)S(1)}, u32[]{:S(2)}, u32[]{:S(2)}) %all-to-all-start) | async-done | bytes 49184 | tf_op jit(solution)/shard_map/all_to_all | solution.py:178
  111.8 1.9 fusion.10
  113.8 1.4 collective-permute-start.16
  115.3 2.2 %collective-permute-start.11 = (bf16[12,2048]{1,0:T(8,128)(2,1)S(1)}, bf16[12,2048]{1,0:T(8,128)(2,1)S(1)}, u32[]{:S(2)}, u32[]{:S(2)}) collective-permute-start(bf16[12,2048]{1,0:T(8,128)(2,1)S(1)} %convert_element_type.120), channel_id=1, source_target_pairs={{0,1},{1,0},{2,3},{3,2},{4,5},{5,4},{6,7},{7,6},{8,9},{9,8},{10,11... | collective-permute-start | bytes 147464 | tf_op jit(solution)/shard_map/ppermute | solution.py:16
  117.9 3.5 %collective-permute-done.11 = bf16[12,2048]{1,0:T(8,128)(2,1)S(1)} collective-permute-done((bf16[12,2048]{1,0:T(8,128)(2,1)S(1)}, bf16[12,2048]{1,0:T(8,128)(2,1)S(1)}, u32[]{:S(2)}, u32[]{:S(2)}) %collective-permute-start.11) | collective-permute-done | bytes 49184 | tf_op jit(solution)/shard_map/ppermute | solution.py:16
  121.5 1.3 collective-permute-start.12
  122.8 1.3 collective-permute-start.13
  124.1 1.3 collective-permute-start.14
  125.4 0.5 fusion.29
  126.1 1.9 collective-permute-start.21
  128.0 12.0 %collective-permute-done.12 = bf16[384,512]{1,0:T(8,128)(2,1)S(1)} collective-permute-done((bf16[384,512]{1,0:T(8,128)(2,1)S(1)}, bf16[384,512]{1,0:T(8,128)(2,1)S(1)}, u32[]{:S(2)}, u32[]{:S(2)}) %collective-permute-start.12) | collective-permute-done | bytes 393248 | tf_op jit(solution)/shard_map/ppermute | solution.py:27
  140.0 3.5 %collective-permute-done.13 = bf16[384,512]{1,0:T(8,128)(2,1)S(1)} collective-permute-done((bf16[384,512]{1,0:T(8,128)(2,1)S(1)}, bf16[384,512]{1,0:T(8,128)(2,1)S(1)}, u32[]{:S(2)}, u32[]{:S(2)}) %collective-permute-start.13) | collective-permute-done | bytes 393248 | tf_op jit(solution)/shard_map/ppermute | solution.py:27
  143.5 5.1 %collective-permute-done.14 = bf16[384,512]{1,0:T(8,128)(2,1)S(1)} collective-permute-done((bf16[384,512]{1,0:T(8,128)(2,1)S(1)}, bf16[384,512]{1,0:T(8,128)(2,1)S(1)}, u32[]{:S(2)}, u32[]{:S(2)}) %collective-permute-start.14) | collective-permute-done | bytes 393248 | tf_op jit(solution)/shard_map/ppermute | solution.py:27
  148.8 2.9 %collective-permute-start.17 = (bf16[12,2048]{1,0:T(8,128)(2,1)S(1)}, bf16[12,2048]{1,0:T(8,128)(2,1)S(1)}, u32[]{:S(2)}, u32[]{:S(2)}) collective-permute-start(bf16[12,2048]{1,0:T(8,128)(2,1)S(1)} %convert_element_type.130), channel_id=1, source_target_pairs={{0,3},{1,2},{2,1},{3,0},{4,7},{5,6},{6,5},{7,4},{8,11},{9,10},{10,... | collective-permute-start | bytes 147464 | tf_op jit(solution)/shard_map/ppermute | solution.py:16
  151.7 0.6 add_bitcast_fusion.1
  152.4 2.6 %collective-permute-start.15 = (bf16[384,512]{1,0:T(8,128)(2,1)S(1)}, bf16[384,512]{1,0:T(8,128)(2,1)S(1)}, u32[]{:S(2)}, u32[]{:S(2)}) collective-permute-start(bf16[384,512]{1,0:T(8,128)(2,1)S(1)} %select_convert_fusion), channel_id=1, source_target_pairs={{32,0},{96,64},{160,128},{224,192},{0,32},{64,96},{128,160},{33,1}... | collective-permute-start | bytes 1179656 | tf_op jit(solution)/shard_map/ppermute | solution.py:32
  155.0 1.1 collective-permute-done.17
  157.0 1.9 collective-permute-start.22
  159.0 1.3 collective-permute-start.20
  160.3 1.3 collective-permute-start.19
  161.6 1.3 collective-permute-start.18
  162.9 0.7 add_bitcast_fusion
  163.6 32.2 %collective-permute-done.15 = bf16[384,512]{1,0:T(8,128)(2,1)S(1)} collective-permute-done((bf16[384,512]{1,0:T(8,128)(2,1)S(1)}, bf16[384,512]{1,0:T(8,128)(2,1)S(1)}, u32[]{:S(2)}, u32[]{:S(2)}) %collective-permute-start.15) | collective-permute-done | bytes 393248 | tf_op jit(solution)/shard_map/ppermute | solution.py:32
  196.4 0.9 maximum_bitcast_fusion
  (77 shorter events, 4.6 us)
Async XLA Ops:
  0.6 22.7 %copy-start.2 = (bf16[1,512,32]{1,2,0:T(8,128)(2,1)S(1)}, bf16[1,512,32]{1,2,0:T(8,128)(2,1)}, u32[]{:S(2)}) copy-start(bf16[1,512,32]{1,2,0:T(8,128)(2,1)} %param.9) | copy-start | bytes 98308
  0.6 22.7 %copy-start.3 = (bf16[1,2,16,1024]{3,2,1,0:T(8,128)(2,1)S(1)}, bf16[1,2,16,1024]{3,2,1,0:T(8,128)(2,1)}, u32[]{:S(2)}) copy-start(bf16[1,2,16,1024]{3,2,1,0:T(8,128)(2,1)} %param.10) | copy-start | bytes 196612
  0.7 16.5 %collective-permute-start = (bf16[24,2048]{1,0:T(8,128)(2,1)}, bf16[24,2048]{1,0:T(8,128)(2,1)S(1)}, u32[]{:S(2)}, u32[]{:S(2)}) collective-permute-start(bf16[24,2048]{1,0:T(8,128)(2,1)} %bitcast.139), channel_id=1, source_target_pairs={{0,16},{4,20},{8,24},{12,28},{16,0},{20,4},{24,8},{28,12},{1,17},{... | collective-permute-start | bytes 294920 | tf_op jit(solution)/shard_map/ppermute | solution.py:16
  18.2 14.5 %collective-permute-start.1 = (bf16[60,2048]{1,0:T(8,128)(2,1)S(1)}, bf16[60,2048]{1,0:T(8,128)(2,1)S(1)}, u32[]{:S(2)}, u32[]{:S(2)}) collective-permute-start(bf16[60,2048]{1,0:T(8,128)(2,1)S(1)} %pad_maximum_fusion.3), channel_id=1, source_target_pairs={{0,8},{4,12},{8,0},{12,4},{16,24},{20,28},{24,16},{28,20},{1,9},{5... | collective-permute-start | bytes 737288 | tf_op jit(solution)/shard_map/ppermute | solution.py:16
  24.3 9.9 %collective-permute-start.2 = (bf16[2,24,2048]{2,1,0:T(8,128)(2,1)S(1)}, bf16[2,24,2048]{2,1,0:T(8,128)(2,1)S(1)}, u32[]{:S(2)}, u32[]{:S(2)}) collective-permute-start(bf16[2,24,2048]{2,1,0:T(8,128)(2,1)S(1)} %pad_maximum_fusion.4), channel_id=1, source_target_pairs={{0,2},{1,3},{2,0},{3,1},{4,6},{5,7},{6,4},{7,5},{8,10},{9,11},{10,... | collective-permute-start | bytes 589832 | tf_op jit(solution)/shard_map/ppermute | solution.py:16
  34.2 25.3 %collective-permute-start.4 = (bf16[2,2,24,2048]{3,2,0,1:T(8,128)(2,1)S(1)}, bf16[2,2,24,2048]{3,2,0,1:T(8,128)(2,1)S(1)}, u32[]{:S(2)}, u32[]{:S(2)}) collective-permute-start(bf16[2,2,24,2048]{3,2,0,1:T(8,128)(2,1)S(1)} %pad_maximum_fusion.1), channel_id=1, source_target_pairs={{0,4},{4,0},{8,12},{12,8},{16,20},{20,16},{24,28},{28,24},{1,5},{5... | collective-permute-start | bytes 1179656 | tf_op jit(solution)/shard_map/ppermute | solution.py:16
  36.2 23.4 %collective-permute-start.5 = (bf16[2,2,24,2048]{3,2,0,1:T(8,128)(2,1)S(1)}, bf16[2,2,24,2048]{3,2,0,1:T(8,128)(2,1)S(1)}, u32[]{:S(2)}, u32[]{:S(2)}) collective-permute-start(bf16[2,2,24,2048]{3,2,0,1:T(8,128)(2,1)S(1)} %pad_maximum_fusion.1), channel_id=1, source_target_pairs={{0,1},{1,0},{2,3},{3,2},{4,5},{5,4},{6,7},{7,6},{8,9},{9,8},{10,11... | collective-permute-start | bytes 1179656 | tf_op jit(solution)/shard_map/ppermute | solution.py:16
  39.6 20.0 %collective-permute-start.6 = (bf16[2,2,24,2048]{3,2,0,1:T(8,128)(2,1)S(1)}, bf16[2,2,24,2048]{3,2,0,1:T(8,128)(2,1)S(1)}, u32[]{:S(2)}, u32[]{:S(2)}) collective-permute-start(bf16[2,2,24,2048]{3,2,0,1:T(8,128)(2,1)S(1)} %pad_maximum_fusion.1), channel_id=1, source_target_pairs={{0,3},{1,2},{2,1},{3,0},{4,7},{5,6},{6,5},{7,4},{8,11},{9,10},{10,... | collective-permute-start | bytes 1179656 | tf_op jit(solution)/shard_map/ppermute | solution.py:16
  43.6 15.9 %collective-permute-start.3 = (bf16[2,24,2048]{2,1,0:T(8,128)(2,1)S(1)}, bf16[2,24,2048]{2,1,0:T(8,128)(2,1)S(1)}, u32[]{:S(2)}, u32[]{:S(2)}) collective-permute-start(bf16[2,24,2048]{2,1,0:T(8,128)(2,1)S(1)} %bitcast.129), channel_id=1, source_target_pairs={{0,2},{1,3},{2,0},{3,1},{4,6},{5,7},{6,4},{7,5},{8,10},{9,11},{10,... | collective-permute-start | bytes 589832 | tf_op jit(solution)/shard_map/ppermute | solution.py:16
  46.2 13.3 %collective-permute-start.7 = (bf16[12,2048]{1,0:T(8,128)(2,1)S(1)}, bf16[12,2048]{1,0:T(8,128)(2,1)S(1)}, u32[]{:S(2)}, u32[]{:S(2)}) collective-permute-start(bf16[12,2048]{1,0:T(8,128)(2,1)S(1)} %convert_element_type.112), channel_id=1, source_target_pairs={{0,16},{4,20},{8,24},{12,28},{16,0},{20,4},{24,8},{28,12},{1,17},{... | collective-permute-start | bytes 147464 | tf_op jit(solution)/shard_map/ppermute | solution.py:16
  59.6 18.1 %collective-permute-start.9 = (bf16[2,2,24,2048]{3,2,0,1:T(8,128)(2,1)S(1)}, bf16[2,2,24,2048]{3,2,0,1:T(8,128)(2,1)S(1)}, u32[]{:S(2)}, u32[]{:S(2)}) collective-permute-start(bf16[2,2,24,2048]{3,2,0,1:T(8,128)(2,1)S(1)} %collective-permute-done.4), channel_id=1, source_target_pairs={{0,1},{1,0},{2,3},{3,2},{4,5},{5,4},{6,7},{7,6},{8,9},{9,8},{10,11... | collective-permute-start | bytes 1179656 | tf_op jit(solution)/shard_map/ppermute | solution.py:16
  62.7 15.0 %collective-permute-start.10 = (bf16[2,2,24,2048]{3,2,0,1:T(8,128)(2,1)S(1)}, bf16[2,2,24,2048]{3,2,0,1:T(8,128)(2,1)S(1)}, u32[]{:S(2)}, u32[]{:S(2)}) collective-permute-start(bf16[2,2,24,2048]{3,2,0,1:T(8,128)(2,1)S(1)} %collective-permute-done.4), channel_id=1, source_target_pairs={{0,3},{1,2},{2,1},{3,0},{4,7},{5,6},{6,5},{7,4},{8,11},{9,10},{10,... | collective-permute-start | bytes 1179656 | tf_op jit(solution)/shard_map/ppermute | solution.py:16
  66.8 10.9 %copy-start = (bf16[1,768,512]{2,1,0:T(8,128)(2,1)S(1)}, bf16[1,768,512]{2,1,0:T(8,128)(2,1)}, u32[]{:S(2)}) copy-start(bf16[1,768,512]{2,1,0:T(8,128)(2,1)} %param.6) | copy-start | bytes 2359300
  66.9 10.9 %copy-start.4 = (f32[1,512]{1,0:T(1,128)S(1)}, f32[1,512]{1,0:T(1,128)}, u32[]{:S(2)}) copy-start(f32[1,512]{1,0:T(1,128)} %param.11) | copy-start | bytes 6148
  66.9 10.9 %copy-start.5 = (bf16[1,512,2048]{2,1,0:T(8,128)(2,1)S(1)}, bf16[1,512,2048]{2,1,0:T(8,128)(2,1)}, u32[]{:S(2)}) copy-start(bf16[1,512,2048]{2,1,0:T(8,128)(2,1)} %param.8) | copy-start | bytes 6291460
  66.9 10.7 %collective-permute-start.8 = (bf16[108,2048]{1,0:T(8,128)(2,1)S(1)}, bf16[108,2048]{1,0:T(8,128)(2,1)S(1)}, u32[]{:S(2)}, u32[]{:S(2)}) collective-permute-start(bf16[108,2048]{1,0:T(8,128)(2,1)S(1)} %pad_maximum_fusion), channel_id=1, source_target_pairs={{0,4},{4,0},{8,12},{12,8},{16,20},{20,16},{24,28},{28,24},{1,5},{5... | collective-permute-start | bytes 1327112 | tf_op jit(solution)/shard_map/ppermute | solution.py:16
  90.5 21.2 %all-to-all-start = ((f32[8,2,768]{2,1,0:T(2,128)}), f32[8,2,768]{2,1,0:T(2,128)S(1)}, u32[]{:S(2)}, u32[]{:S(2)}) async-start(f32[8,2,768]{2,1,0:T(2,128)} %broadcast_in_dim.11), calls=%async_computation | async-start | bytes 98304 | tf_op jit(solution)/shard_map/all_to_all | solution.py:178
  113.8 12.1 %copy-start.1 = (bf16[1,768,512]{2,1,0:T(8,128)(2,1)S(1)}, bf16[1,768,512]{2,1,0:T(8,128)(2,1)}, u32[]{:S(2)}) copy-start(bf16[1,768,512]{2,1,0:T(8,128)(2,1)} %param.6) | copy-start | bytes 2359300
  113.8 42.4 %collective-permute-start.16 = (bf16[384,512]{1,0:T(8,128)(2,1)S(1)}, bf16[384,512]{1,0:T(8,128)(2,1)S(1)}, u32[]{:S(2)}, u32[]{:S(2)}) collective-permute-start(bf16[384,512]{1,0:T(8,128)(2,1)S(1)} %get-tuple-element.64), channel_id=1, source_target_pairs={{32,0},{96,64},{160,128},{224,192},{64,96},{128,160},{192,224},{33... | collective-permute-start | bytes 1179656 | tf_op jit(solution)/shard_map/ppermute | solution.py:32
  115.3 6.2 %collective-permute-start.11 = (bf16[12,2048]{1,0:T(8,128)(2,1)S(1)}, bf16[12,2048]{1,0:T(8,128)(2,1)S(1)}, u32[]{:S(2)}, u32[]{:S(2)}) collective-permute-start(bf16[12,2048]{1,0:T(8,128)(2,1)S(1)} %convert_element_type.120), channel_id=1, source_target_pairs={{0,1},{1,0},{2,3},{3,2},{4,5},{5,4},{6,7},{7,6},{8,9},{9,8},{10,11... | collective-permute-start | bytes 147464 | tf_op jit(solution)/shard_map/ppermute | solution.py:16
  121.5 18.6 %collective-permute-start.12 = (bf16[384,512]{1,0:T(8,128)(2,1)S(1)}, bf16[384,512]{1,0:T(8,128)(2,1)S(1)}, u32[]{:S(2)}, u32[]{:S(2)}) collective-permute-start(bf16[384,512]{1,0:T(8,128)(2,1)S(1)} %get-tuple-element.50), channel_id=1, source_target_pairs={{64,0},{128,64},{192,128},{65,1},{129,65},{193,129},{66,2},{130,66... | collective-permute-start | bytes 1179656 | tf_op jit(solution)/shard_map/ppermute | solution.py:27
  122.8 20.7 %collective-permute-start.13 = (bf16[384,512]{1,0:T(8,128)(2,1)S(1)}, bf16[384,512]{1,0:T(8,128)(2,1)S(1)}, u32[]{:S(2)}, u32[]{:S(2)}) collective-permute-start(bf16[384,512]{1,0:T(8,128)(2,1)S(1)} %get-tuple-element.50), channel_id=1, source_target_pairs={{128,0},{192,64},{129,1},{193,65},{130,2},{194,66},{131,3},{195,67... | collective-permute-start | bytes 1179656 | tf_op jit(solution)/shard_map/ppermute | solution.py:27
  124.1 24.5 %collective-permute-start.14 = (bf16[384,512]{1,0:T(8,128)(2,1)S(1)}, bf16[384,512]{1,0:T(8,128)(2,1)S(1)}, u32[]{:S(2)}, u32[]{:S(2)}) collective-permute-start(bf16[384,512]{1,0:T(8,128)(2,1)S(1)} %get-tuple-element.50), channel_id=1, source_target_pairs={{192,0},{193,1},{194,2},{195,3},{196,4},{197,5},{198,6},{199,7},{2... | collective-permute-start | bytes 1179656 | tf_op jit(solution)/shard_map/ppermute | solution.py:27
  126.1 25.6 %collective-permute-start.21 = (f32[512,32]{0,1:T(8,128)S(1)}, f32[512,32]{0,1:T(8,128)S(1)}, u32[]{:S(2)}, u32[]{:S(2)}) collective-permute-start(f32[512,32]{0,1:T(8,128)S(1)} %fusion.28), channel_id=1, source_target_pairs={{0,256},{256,0},{1,257},{257,1},{2,258},{258,2},{3,259},{259,3},{4... | collective-permute-start | bytes 196616 | tf_op jit(solution)/shard_map/ppermute | solution.py:16
  148.8 7.4 %collective-permute-start.17 = (bf16[12,2048]{1,0:T(8,128)(2,1)S(1)}, bf16[12,2048]{1,0:T(8,128)(2,1)S(1)}, u32[]{:S(2)}, u32[]{:S(2)}) collective-permute-start(bf16[12,2048]{1,0:T(8,128)(2,1)S(1)} %convert_element_type.130), channel_id=1, source_target_pairs={{0,3},{1,2},{2,1},{3,0},{4,7},{5,6},{6,5},{7,4},{8,11},{9,10},{10,... | collective-permute-start | bytes 147464 | tf_op jit(solution)/shard_map/ppermute | solution.py:16
  152.4 43.4 %collective-permute-start.15 = (bf16[384,512]{1,0:T(8,128)(2,1)S(1)}, bf16[384,512]{1,0:T(8,128)(2,1)S(1)}, u32[]{:S(2)}, u32[]{:S(2)}) collective-permute-start(bf16[384,512]{1,0:T(8,128)(2,1)S(1)} %select_convert_fusion), channel_id=1, source_target_pairs={{32,0},{96,64},{160,128},{224,192},{0,32},{64,96},{128,160},{33,1}... | collective-permute-start | bytes 1179656 | tf_op jit(solution)/shard_map/ppermute | solution.py:32
  157.0 5.9 %collective-permute-start.22 = (f32[2,16,1024]{2,1,0:T(8,128)S(1)}, f32[2,16,1024]{2,1,0:T(8,128)S(1)}, u32[]{:S(2)}, u32[]{:S(2)}) collective-permute-start(f32[2,16,1024]{2,1,0:T(8,128)S(1)} %maximum_multiply_fusion.1), channel_id=1, source_target_pairs={{0,256},{256,0},{1,257},{257,1},{2,258},{258,2},{3,259},{259,3},{4... | collective-permute-start | bytes 393224 | tf_op jit(solution)/shard_map/ppermute | solution.py:16
  159.0 37.1 %collective-permute-start.20 = (bf16[384,512]{1,0:T(8,128)(2,1)S(1)}, bf16[384,512]{1,0:T(8,128)(2,1)S(1)}, u32[]{:S(2)}, u32[]{:S(2)}) collective-permute-start(bf16[384,512]{1,0:T(8,128)(2,1)S(1)} %fusion.38), channel_id=1, source_target_pairs={{192,0},{193,1},{194,2},{195,3},{196,4},{197,5},{198,6},{199,7},{2... | collective-permute-start | bytes 1179656 | tf_op jit(solution)/shard_map/ppermute | solution.py:27
  160.3 35.8 %collective-permute-start.19 = (bf16[384,512]{1,0:T(8,128)(2,1)S(1)}, bf16[384,512]{1,0:T(8,128)(2,1)S(1)}, u32[]{:S(2)}, u32[]{:S(2)}) collective-permute-start(bf16[384,512]{1,0:T(8,128)(2,1)S(1)} %fusion.38), channel_id=1, source_target_pairs={{128,0},{192,64},{129,1},{193,65},{130,2},{194,66},{131,3},{195,67... | collective-permute-start | bytes 1179656 | tf_op jit(solution)/shard_map/ppermute | solution.py:27
  161.6 34.5 %collective-permute-start.18 = (bf16[384,512]{1,0:T(8,128)(2,1)S(1)}, bf16[384,512]{1,0:T(8,128)(2,1)S(1)}, u32[]{:S(2)}, u32[]{:S(2)}) collective-permute-start(bf16[384,512]{1,0:T(8,128)(2,1)S(1)} %fusion.38), channel_id=1, source_target_pairs={{64,0},{128,64},{192,128},{65,1},{129,65},{193,129},{66,2},{130,66... | collective-permute-start | bytes 1179656 | tf_op jit(solution)/shard_map/ppermute | solution.py:27

commit v6 on v4

--- a/solution.py
+++ b/solution.py
@@ -168,9 +168,8 @@
 
 
 def reduce_rows(rows):
-    rows = lax.psum(rows, "x")
     spread = jnp.broadcast_to(rows[None], (sizes["zl"],) + rows.shape)
-    return jnp.sum(lax.all_to_all(spread, "zl", 0, 0), axis=0)
+    return lax.psum(jnp.sum(lax.all_to_all(spread, "zl", 0, 0), axis=0), "x")
 
 
 def solution(mesh):

time: 198 us -> 198 us (level)
  the two profiles are of different devices: /device:TPU:105 before, /device:TPU:38 now
where the time goes in v6:
time: 198 us; the launch traced here: 197 us
  starting transfers between devices  92.3 us (47%)
  waiting for transfers between devices  77.6 us (39%)
  other arithmetic  8.59 us (4%)
  blocking collectives  8.08 us (4%)
  matrix products  7.35 us (4%)
    ppermute x17, starting transfers between devices, swap(): return lax.ppermute(value, axis, [(i, i ^ mask) for i in range(count)])  72.5 us
    ppermute x17, waiting for transfers between devices, swap(): return lax.ppermute(value, axis, [(i, i ^ mask) for i in range(count)])  57.2 us
    all_to_all x1, starting transfers between devices, reduce_rows(): return lax.psum(jnp.sum(lax.all_to_all(spread, 'zl', 0, 0), axis=0), 'x')  12 us
    ppermute x6, waiting for transfers between devices, later_y(): lax.ppermute(value, 'y', [(i, i - d) for i in range(d, count)])  11.3 us
    all_to_all x1, waiting for transfers between devices, reduce_rows(): return lax.psum(jnp.sum(lax.all_to_all(spread, 'zl', 0, 0), axis=0), 'x')  9.18 us
    psum x1, blocking collectives, reduce_rows(): return lax.psum(jnp.sum(lax.all_to_all(spread, 'zl', 0, 0), axis=0), 'x')  8.08 us
    ppermute x6, starting transfers between devices, later_y(): lax.ppermute(value, 'y', [(i, i - d) for i in range(d, count)])  7.75 us
  transfers between devices with their start and end apart: 24, of which 11 were waited for; matrix products, arithmetic and copies ran while one was open for 5% of the time, Pallas kernels for 0%

profile of v6, /device:TPU:38, one launch (start us, length us, event | category | flops | bytes accessed | tf_op | source)
XLA Modules:
  0.0 196.9 jit_solution(4164017129634712745)
XLA Ops:
  0.7 9.2 %collective-permute-start = (bf16[24,2048]{1,0:T(8,128)(2,1)}, bf16[24,2048]{1,0:T(8,128)(2,1)S(1)}, u32[]{:S(2)}, u32[]{:S(2)}) collective-permute-start(bf16[24,2048]{1,0:T(8,128)(2,1)} %bitcast.139), channel_id=1, source_target_pairs={{0,16},{4,20},{8,24},{12,28},{16,0},{20,4},{24,8},{28,12},{1,17},{... | collective-permute-start | bytes 294920 | tf_op jit(solution)/shard_map/ppermute | solution.py:16
  9.9 0.8 multiply_convert_fusion.1
  10.7 1.5 fusion.60
  12.3 1.4 fusion.6
  13.6 3.6 %collective-permute-done = bf16[24,2048]{1,0:T(8,128)(2,1)S(1)} collective-permute-done((bf16[24,2048]{1,0:T(8,128)(2,1)}, bf16[24,2048]{1,0:T(8,128)(2,1)S(1)}, u32[]{:S(2)}, u32[]{:S(2)}) %collective-permute-start) | collective-permute-done | bytes 98336 | tf_op jit(solution)/shard_map/ppermute | solution.py:16
  17.2 0.9 select_bitcast_fusion.5
  18.2 5.2 %collective-permute-start.1 = (bf16[60,2048]{1,0:T(8,128)(2,1)S(1)}, bf16[60,2048]{1,0:T(8,128)(2,1)S(1)}, u32[]{:S(2)}, u32[]{:S(2)}) collective-permute-start(bf16[60,2048]{1,0:T(8,128)(2,1)S(1)} %pad_maximum_fusion.3), channel_id=1, source_target_pairs={{0,8},{4,12},{8,0},{12,4},{16,24},{20,28},{24,16},{28,20},{1,9},{5... | collective-permute-start | bytes 737288 | tf_op jit(solution)/shard_map/ppermute | solution.py:16
  24.3 3.3 %collective-permute-start.2 = (bf16[2,24,2048]{2,1,0:T(8,128)(2,1)S(1)}, bf16[2,24,2048]{2,1,0:T(8,128)(2,1)S(1)}, u32[]{:S(2)}, u32[]{:S(2)}) collective-permute-start(bf16[2,24,2048]{2,1,0:T(8,128)(2,1)S(1)} %pad_maximum_fusion.4), channel_id=1, source_target_pairs={{0,2},{1,3},{2,0},{3,1},{4,6},{5,7},{6,4},{7,5},{8,10},{9,11},{10,... | collective-permute-start | bytes 589832 | tf_op jit(solution)/shard_map/ppermute | solution.py:16
  27.6 5.0 %collective-permute-done.1 = bf16[60,2048]{1,0:T(8,128)(2,1)S(1)} collective-permute-done((bf16[60,2048]{1,0:T(8,128)(2,1)S(1)}, bf16[60,2048]{1,0:T(8,128)(2,1)S(1)}, u32[]{:S(2)}, u32[]{:S(2)}) %collective-permute-start.1) | collective-permute-done | bytes 245792 | tf_op jit(solution)/shard_map/ppermute | solution.py:16
  32.8 1.5 collective-permute-done.2
  34.2 1.9 collective-permute-start.4
  36.2 2.7 %collective-permute-start.5 = (bf16[2,2,24,2048]{3,2,0,1:T(8,128)(2,1)S(1)}, bf16[2,2,24,2048]{3,2,0,1:T(8,128)(2,1)S(1)}, u32[]{:S(2)}, u32[]{:S(2)}) collective-permute-start(bf16[2,2,24,2048]{3,2,0,1:T(8,128)(2,1)S(1)} %pad_maximum_fusion.1), channel_id=1, source_target_pairs={{0,1},{1,0},{2,3},{3,2},{4,5},{5,4},{6,7},{7,6},{8,9},{9,8},{10,11... | collective-permute-start | bytes 1179656 | tf_op jit(solution)/shard_map/ppermute | solution.py:16
  38.9 3.0 %collective-permute-start.6 = (bf16[2,2,24,2048]{3,2,0,1:T(8,128)(2,1)S(1)}, bf16[2,2,24,2048]{3,2,0,1:T(8,128)(2,1)S(1)}, u32[]{:S(2)}, u32[]{:S(2)}) collective-permute-start(bf16[2,2,24,2048]{3,2,0,1:T(8,128)(2,1)S(1)} %pad_maximum_fusion.1), channel_id=1, source_target_pairs={{0,3},{1,2},{2,1},{3,0},{4,7},{5,6},{6,5},{7,4},{8,11},{9,10},{10,... | collective-permute-start | bytes 1179656 | tf_op jit(solution)/shard_map/ppermute | solution.py:16
  42.0 4.0 %collective-permute-start.3 = (bf16[2,24,2048]{2,1,0:T(8,128)(2,1)S(1)}, bf16[2,24,2048]{2,1,0:T(8,128)(2,1)S(1)}, u32[]{:S(2)}, u32[]{:S(2)}) collective-permute-start(bf16[2,24,2048]{2,1,0:T(8,128)(2,1)S(1)} %bitcast.129), channel_id=1, source_target_pairs={{0,2},{1,3},{2,0},{3,1},{4,6},{5,7},{6,4},{7,5},{8,10},{9,11},{10,... | collective-permute-start | bytes 589832 | tf_op jit(solution)/shard_map/ppermute | solution.py:16
  46.0 8.2 %collective-permute-start.7 = (bf16[12,2048]{1,0:T(8,128)(2,1)S(1)}, bf16[12,2048]{1,0:T(8,128)(2,1)S(1)}, u32[]{:S(2)}, u32[]{:S(2)}) collective-permute-start(bf16[12,2048]{1,0:T(8,128)(2,1)S(1)} %convert_element_type.112), channel_id=1, source_target_pairs={{0,16},{4,20},{8,24},{12,28},{16,0},{20,4},{24,8},{28,12},{1,17},{... | collective-permute-start | bytes 147464 | tf_op jit(solution)/shard_map/ppermute | solution.py:16
  54.7 4.6 %collective-permute-done.7 = bf16[12,2048]{1,0:T(8,128)(2,1)S(1)} collective-permute-done((bf16[12,2048]{1,0:T(8,128)(2,1)S(1)}, bf16[12,2048]{1,0:T(8,128)(2,1)S(1)}, u32[]{:S(2)}, u32[]{:S(2)}) %collective-permute-start.7) | collective-permute-done | bytes 49184 | tf_op jit(solution)/shard_map/ppermute | solution.py:16
  59.3 2.7 %collective-permute-start.9 = (bf16[2,2,24,2048]{3,2,0,1:T(8,128)(2,1)S(1)}, bf16[2,2,24,2048]{3,2,0,1:T(8,128)(2,1)S(1)}, u32[]{:S(2)}, u32[]{:S(2)}) collective-permute-start(bf16[2,2,24,2048]{3,2,0,1:T(8,128)(2,1)S(1)} %collective-permute-done.4), channel_id=1, source_target_pairs={{0,1},{1,0},{2,3},{3,2},{4,5},{5,4},{6,7},{7,6},{8,9},{9,8},{10,11... | collective-permute-start | bytes 1179656 | tf_op jit(solution)/shard_map/ppermute | solution.py:16
  62.0 3.0 %collective-permute-start.10 = (bf16[2,2,24,2048]{3,2,0,1:T(8,128)(2,1)S(1)}, bf16[2,2,24,2048]{3,2,0,1:T(8,128)(2,1)S(1)}, u32[]{:S(2)}, u32[]{:S(2)}) collective-permute-start(bf16[2,2,24,2048]{3,2,0,1:T(8,128)(2,1)S(1)} %collective-permute-done.4), channel_id=1, source_target_pairs={{0,3},{1,2},{2,1},{3,0},{4,7},{5,6},{6,5},{7,4},{8,11},{9,10},{10,... | collective-permute-start | bytes 1179656 | tf_op jit(solution)/shard_map/ppermute | solution.py:16
  65.3 4.2 %collective-permute-start.8 = (bf16[108,2048]{1,0:T(8,128)(2,1)S(1)}, bf16[108,2048]{1,0:T(8,128)(2,1)S(1)}, u32[]{:S(2)}, u32[]{:S(2)}) collective-permute-start(bf16[108,2048]{1,0:T(8,128)(2,1)S(1)} %pad_maximum_fusion), channel_id=1, source_target_pairs={{0,4},{4,0},{8,12},{12,8},{16,20},{20,16},{24,28},{28,24},{1,5},{5... | collective-permute-start | bytes 1327112 | tf_op jit(solution)/shard_map/ppermute | solution.py:16
  69.7 6.2 %collective-permute-done.8 = bf16[108,2048]{1,0:T(8,128)(2,1)S(1)} collective-permute-done((bf16[108,2048]{1,0:T(8,128)(2,1)S(1)}, bf16[108,2048]{1,0:T(8,128)(2,1)S(1)}, u32[]{:S(2)}, u32[]{:S(2)}) %collective-permute-start.8) | collective-permute-done | bytes 442400 | tf_op jit(solution)/shard_map/ppermute | solution.py:16
  76.2 3.1 %fusion.7 = (f32[768]{0:T(1024)S(1)}, f32[768,512]{1,0:T(8,128)}) fusion(bf16[1,768,512]{2,1,0:T(8,128)(2,1)S(1)} %copy-done, f32[512]{0:T(512)S(1)} %bitcast.141, bf16[768,2048]{1,0:T(8,128)(2,1)S(1)} %bitcast.117, f32[1,512,1024]{2,1,0:T(8,128)S(1)} %convolution_bitcast_fusion, f32[1,512,1024]{2,1,0:T(8,128)S(1)} %convolution_bitcast_fusion.1, ...), kind=kOutput, calls=%fused_computation.12 | convolution fusion | flops 1617427712 | bytes 11801600 | tf_op jit(solution)/shard_map/dot_general | solution.py:110
  79.3 0.6 broadcast_in_dim.11
  79.9 12.0 %all-to-all-start = ((f32[8,2,768]{2,1,0:T(2,128)}), f32[8,2,768]{2,1,0:T(2,128)S(1)}, u32[]{:S(2)}, u32[]{:S(2)}) async-start(f32[8,2,768]{2,1,0:T(2,128)} %broadcast_in_dim.11), calls=%async_computation | async-start | bytes 98304 | tf_op jit(solution)/shard_map/all_to_all | solution.py:172
  92.0 9.2 %all-to-all-done = f32[8,2,768]{2,1,0:T(2,128)S(1)} async-done(((f32[8,2,768]{2,1,0:T(2,128)}), f32[8,2,768]{2,1,0:T(2,128)S(1)}, u32[]{:S(2)}, u32[]{:S(2)}) %all-to-all-start) | async-done | bytes 49184 | tf_op jit(solution)/shard_map/all_to_all | solution.py:172
  101.2 8.1 %psum.7 = f32[2,768]{1,0:T(2,128)S(1)} all-reduce(f32[2,768]{1,0:T(2,128)S(1)} %reduce_sum.29), channel_id=1, replica_groups=mesh['dp'=2,'y'=4,'zh'=2,'zl'=8,'x'=4] {'x'}, use_global_device_ids=true, to_apply=%region_3.4 | all-reduce | flops 1536 | bytes 12288 | tf_op jit(solution)/shard_map/psum | solution.py:172
  109.3 1.9 fusion.10
  111.3 11.4 %collective-permute-start.16 = (bf16[384,512]{1,0:T(8,128)(2,1)S(1)}, bf16[384,512]{1,0:T(8,128)(2,1)S(1)}, u32[]{:S(2)}, u32[]{:S(2)}) collective-permute-start(bf16[384,512]{1,0:T(8,128)(2,1)S(1)} %get-tuple-element.64), channel_id=1, source_target_pairs={{0,32},{32,0},{1,33},{33,1},{2,34},{34,2},{3,35},{35,3},{4,36},{36... | collective-permute-start | bytes 1179656 | tf_op jit(solution)/shard_map/ppermute | solution.py:16
  122.7 2.5 %collective-permute-start.11 = (bf16[12,2048]{1,0:T(8,128)(2,1)S(1)}, bf16[12,2048]{1,0:T(8,128)(2,1)S(1)}, u32[]{:S(2)}, u32[]{:S(2)}) collective-permute-start(bf16[12,2048]{1,0:T(8,128)(2,1)S(1)} %convert_element_type.120), channel_id=1, source_target_pairs={{0,1},{1,0},{2,3},{3,2},{4,5},{5,4},{6,7},{7,6},{8,9},{9,8},{10,11... | collective-permute-start | bytes 147464 | tf_op jit(solution)/shard_map/ppermute | solution.py:16
  125.2 0.5 fusion.32
  125.7 3.2 %collective-permute-done.11 = bf16[12,2048]{1,0:T(8,128)(2,1)S(1)} collective-permute-done((bf16[12,2048]{1,0:T(8,128)(2,1)S(1)}, bf16[12,2048]{1,0:T(8,128)(2,1)S(1)}, u32[]{:S(2)}, u32[]{:S(2)}) %collective-permute-start.11) | collective-permute-done | bytes 49184 | tf_op jit(solution)/shard_map/ppermute | solution.py:16
  128.9 1.3 collective-permute-start.12
  130.2 1.3 collective-permute-start.13
  131.5 1.3 collective-permute-start.14
  132.8 0.5 fusion.29
  133.6 1.9 collective-permute-start.21
  135.5 3.1 %collective-permute-done.12 = bf16[384,512]{1,0:T(8,128)(2,1)S(1)} collective-permute-done((bf16[384,512]{1,0:T(8,128)(2,1)S(1)}, bf16[384,512]{1,0:T(8,128)(2,1)S(1)}, u32[]{:S(2)}, u32[]{:S(2)}) %collective-permute-start.12) | collective-permute-done | bytes 393248 | tf_op jit(solution)/shard_map/ppermute | solution.py:27
  138.6 3.0 %collective-permute-done.13 = bf16[384,512]{1,0:T(8,128)(2,1)S(1)} collective-permute-done((bf16[384,512]{1,0:T(8,128)(2,1)S(1)}, bf16[384,512]{1,0:T(8,128)(2,1)S(1)}, u32[]{:S(2)}, u32[]{:S(2)}) %collective-permute-start.13) | collective-permute-done | bytes 393248 | tf_op jit(solution)/shard_map/ppermute | solution.py:27
  141.6 5.2 %collective-permute-done.14 = bf16[384,512]{1,0:T(8,128)(2,1)S(1)} collective-permute-done((bf16[384,512]{1,0:T(8,128)(2,1)S(1)}, bf16[384,512]{1,0:T(8,128)(2,1)S(1)}, u32[]{:S(2)}, u32[]{:S(2)}) %collective-permute-start.14) | collective-permute-done | bytes 393248 | tf_op jit(solution)/shard_map/ppermute | solution.py:27
  147.0 4.3 %collective-permute-start.17 = (bf16[12,2048]{1,0:T(8,128)(2,1)S(1)}, bf16[12,2048]{1,0:T(8,128)(2,1)S(1)}, u32[]{:S(2)}, u32[]{:S(2)}) collective-permute-start(bf16[12,2048]{1,0:T(8,128)(2,1)S(1)} %convert_element_type.130), channel_id=1, source_target_pairs={{0,3},{1,2},{2,1},{3,0},{4,7},{5,6},{6,5},{7,4},{8,11},{9,10},{10,... | collective-permute-start | bytes 147464 | tf_op jit(solution)/shard_map/ppermute | solution.py:16
  151.3 0.6 add_bitcast_fusion.1
  151.9 2.9 %collective-permute-start.15 = (bf16[384,512]{1,0:T(8,128)(2,1)S(1)}, bf16[384,512]{1,0:T(8,128)(2,1)S(1)}, u32[]{:S(2)}, u32[]{:S(2)}) collective-permute-start(bf16[384,512]{1,0:T(8,128)(2,1)S(1)} %select_convert_fusion), channel_id=1, source_target_pairs={{0,32},{32,0},{1,33},{33,1},{2,34},{34,2},{3,35},{35,3},{4,36},{36... | collective-permute-start | bytes 1179656 | tf_op jit(solution)/shard_map/ppermute | solution.py:16
  155.6 1.9 collective-permute-start.22
  157.7 1.3 collective-permute-start.20
  159.0 1.3 collective-permute-start.19
  160.3 1.3 collective-permute-start.18
  161.6 0.7 add_bitcast_fusion
  162.2 33.1 %collective-permute-done.15 = bf16[384,512]{1,0:T(8,128)(2,1)S(1)} collective-permute-done((bf16[384,512]{1,0:T(8,128)(2,1)S(1)}, bf16[384,512]{1,0:T(8,128)(2,1)S(1)}, u32[]{:S(2)}, u32[]{:S(2)}) %collective-permute-start.15) | collective-permute-done | bytes 393248 | tf_op jit(solution)/shard_map/ppermute | solution.py:16
  195.9 0.9 maximum_bitcast_fusion
  (77 shorter events, 4.1 us)
Async XLA Ops:
  0.6 22.7 %copy-start.2 = (bf16[1,512,32]{1,2,0:T(8,128)(2,1)S(1)}, bf16[1,512,32]{1,2,0:T(8,128)(2,1)}, u32[]{:S(2)}) copy-start(bf16[1,512,32]{1,2,0:T(8,128)(2,1)} %param.9) | copy-start | bytes 98308
  0.6 22.7 %copy-start.3 = (bf16[1,2,16,1024]{3,2,1,0:T(8,128)(2,1)S(1)}, bf16[1,2,16,1024]{3,2,1,0:T(8,128)(2,1)}, u32[]{:S(2)}) copy-start(bf16[1,2,16,1024]{3,2,1,0:T(8,128)(2,1)} %param.10) | copy-start | bytes 196612
  0.7 16.5 %collective-permute-start = (bf16[24,2048]{1,0:T(8,128)(2,1)}, bf16[24,2048]{1,0:T(8,128)(2,1)S(1)}, u32[]{:S(2)}, u32[]{:S(2)}) collective-permute-start(bf16[24,2048]{1,0:T(8,128)(2,1)} %bitcast.139), channel_id=1, source_target_pairs={{0,16},{4,20},{8,24},{12,28},{16,0},{20,4},{24,8},{28,12},{1,17},{... | collective-permute-start | bytes 294920 | tf_op jit(solution)/shard_map/ppermute | solution.py:16
  18.2 14.5 %collective-permute-start.1 = (bf16[60,2048]{1,0:T(8,128)(2,1)S(1)}, bf16[60,2048]{1,0:T(8,128)(2,1)S(1)}, u32[]{:S(2)}, u32[]{:S(2)}) collective-permute-start(bf16[60,2048]{1,0:T(8,128)(2,1)S(1)} %pad_maximum_fusion.3), channel_id=1, source_target_pairs={{0,8},{4,12},{8,0},{12,4},{16,24},{20,28},{24,16},{28,20},{1,9},{5... | collective-permute-start | bytes 737288 | tf_op jit(solution)/shard_map/ppermute | solution.py:16
  24.3 9.9 %collective-permute-start.2 = (bf16[2,24,2048]{2,1,0:T(8,128)(2,1)S(1)}, bf16[2,24,2048]{2,1,0:T(8,128)(2,1)S(1)}, u32[]{:S(2)}, u32[]{:S(2)}) collective-permute-start(bf16[2,24,2048]{2,1,0:T(8,128)(2,1)S(1)} %pad_maximum_fusion.4), channel_id=1, source_target_pairs={{0,2},{1,3},{2,0},{3,1},{4,6},{5,7},{6,4},{7,5},{8,10},{9,11},{10,... | collective-permute-start | bytes 589832 | tf_op jit(solution)/shard_map/ppermute | solution.py:16
  34.2 25.0 %collective-permute-start.4 = (bf16[2,2,24,2048]{3,2,0,1:T(8,128)(2,1)S(1)}, bf16[2,2,24,2048]{3,2,0,1:T(8,128)(2,1)S(1)}, u32[]{:S(2)}, u32[]{:S(2)}) collective-permute-start(bf16[2,2,24,2048]{3,2,0,1:T(8,128)(2,1)S(1)} %pad_maximum_fusion.1), channel_id=1, source_target_pairs={{0,4},{4,0},{8,12},{12,8},{16,20},{20,16},{24,28},{28,24},{1,5},{5... | collective-permute-start | bytes 1179656 | tf_op jit(solution)/shard_map/ppermute | solution.py:16
  36.2 23.1 %collective-permute-start.5 = (bf16[2,2,24,2048]{3,2,0,1:T(8,128)(2,1)S(1)}, bf16[2,2,24,2048]{3,2,0,1:T(8,128)(2,1)S(1)}, u32[]{:S(2)}, u32[]{:S(2)}) collective-permute-start(bf16[2,2,24,2048]{3,2,0,1:T(8,128)(2,1)S(1)} %pad_maximum_fusion.1), channel_id=1, source_target_pairs={{0,1},{1,0},{2,3},{3,2},{4,5},{5,4},{6,7},{7,6},{8,9},{9,8},{10,11... | collective-permute-start | bytes 1179656 | tf_op jit(solution)/shard_map/ppermute | solution.py:16
  38.9 20.4 %collective-permute-start.6 = (bf16[2,2,24,2048]{3,2,0,1:T(8,128)(2,1)S(1)}, bf16[2,2,24,2048]{3,2,0,1:T(8,128)(2,1)S(1)}, u32[]{:S(2)}, u32[]{:S(2)}) collective-permute-start(bf16[2,2,24,2048]{3,2,0,1:T(8,128)(2,1)S(1)} %pad_maximum_fusion.1), channel_id=1, source_target_pairs={{0,3},{1,2},{2,1},{3,0},{4,7},{5,6},{6,5},{7,4},{8,11},{9,10},{10,... | collective-permute-start | bytes 1179656 | tf_op jit(solution)/shard_map/ppermute | solution.py:16
  42.0 17.3 %collective-permute-start.3 = (bf16[2,24,2048]{2,1,0:T(8,128)(2,1)S(1)}, bf16[2,24,2048]{2,1,0:T(8,128)(2,1)S(1)}, u32[]{:S(2)}, u32[]{:S(2)}) collective-permute-start(bf16[2,24,2048]{2,1,0:T(8,128)(2,1)S(1)} %bitcast.129), channel_id=1, source_target_pairs={{0,2},{1,3},{2,0},{3,1},{4,6},{5,7},{6,4},{7,5},{8,10},{9,11},{10,... | collective-permute-start | bytes 589832 | tf_op jit(solution)/shard_map/ppermute | solution.py:16
  46.0 13.2 %collective-permute-start.7 = (bf16[12,2048]{1,0:T(8,128)(2,1)S(1)}, bf16[12,2048]{1,0:T(8,128)(2,1)S(1)}, u32[]{:S(2)}, u32[]{:S(2)}) collective-permute-start(bf16[12,2048]{1,0:T(8,128)(2,1)S(1)} %convert_element_type.112), channel_id=1, source_target_pairs={{0,16},{4,20},{8,24},{12,28},{16,0},{20,4},{24,8},{28,12},{1,17},{... | collective-permute-start | bytes 147464 | tf_op jit(solution)/shard_map/ppermute | solution.py:16
  59.3 16.7 %collective-permute-start.9 = (bf16[2,2,24,2048]{3,2,0,1:T(8,128)(2,1)S(1)}, bf16[2,2,24,2048]{3,2,0,1:T(8,128)(2,1)S(1)}, u32[]{:S(2)}, u32[]{:S(2)}) collective-permute-start(bf16[2,2,24,2048]{3,2,0,1:T(8,128)(2,1)S(1)} %collective-permute-done.4), channel_id=1, source_target_pairs={{0,1},{1,0},{2,3},{3,2},{4,5},{5,4},{6,7},{7,6},{8,9},{9,8},{10,11... | collective-permute-start | bytes 1179656 | tf_op jit(solution)/shard_map/ppermute | solution.py:16
  62.0 14.0 %collective-permute-start.10 = (bf16[2,2,24,2048]{3,2,0,1:T(8,128)(2,1)S(1)}, bf16[2,2,24,2048]{3,2,0,1:T(8,128)(2,1)S(1)}, u32[]{:S(2)}, u32[]{:S(2)}) collective-permute-start(bf16[2,2,24,2048]{3,2,0,1:T(8,128)(2,1)S(1)} %collective-permute-done.4), channel_id=1, source_target_pairs={{0,3},{1,2},{2,1},{3,0},{4,7},{5,6},{6,5},{7,4},{8,11},{9,10},{10,... | collective-permute-start | bytes 1179656 | tf_op jit(solution)/shard_map/ppermute | solution.py:16
  65.2 10.9 %copy-start = (bf16[1,768,512]{2,1,0:T(8,128)(2,1)S(1)}, bf16[1,768,512]{2,1,0:T(8,128)(2,1)}, u32[]{:S(2)}) copy-start(bf16[1,768,512]{2,1,0:T(8,128)(2,1)} %param.6) | copy-start | bytes 2359300
  65.2 10.9 %copy-start.4 = (f32[1,512]{1,0:T(1,128)S(1)}, f32[1,512]{1,0:T(1,128)}, u32[]{:S(2)}) copy-start(f32[1,512]{1,0:T(1,128)} %param.11) | copy-start | bytes 6148
  65.3 10.9 %copy-start.5 = (bf16[1,512,2048]{2,1,0:T(8,128)(2,1)S(1)}, bf16[1,512,2048]{2,1,0:T(8,128)(2,1)}, u32[]{:S(2)}) copy-start(bf16[1,512,2048]{2,1,0:T(8,128)(2,1)} %param.8) | copy-start | bytes 6291460
  65.3 10.7 %collective-permute-start.8 = (bf16[108,2048]{1,0:T(8,128)(2,1)S(1)}, bf16[108,2048]{1,0:T(8,128)(2,1)S(1)}, u32[]{:S(2)}, u32[]{:S(2)}) collective-permute-start(bf16[108,2048]{1,0:T(8,128)(2,1)S(1)} %pad_maximum_fusion), channel_id=1, source_target_pairs={{0,4},{4,0},{8,12},{12,8},{16,20},{20,16},{24,28},{28,24},{1,5},{5... | collective-permute-start | bytes 1327112 | tf_op jit(solution)/shard_map/ppermute | solution.py:16
  79.9 21.2 %all-to-all-start = ((f32[8,2,768]{2,1,0:T(2,128)}), f32[8,2,768]{2,1,0:T(2,128)S(1)}, u32[]{:S(2)}, u32[]{:S(2)}) async-start(f32[8,2,768]{2,1,0:T(2,128)} %broadcast_in_dim.11), calls=%async_computation | async-start | bytes 98304 | tf_op jit(solution)/shard_map/all_to_all | solution.py:172
  111.2 22.1 %copy-start.1 = (bf16[1,768,512]{2,1,0:T(8,128)(2,1)S(1)}, bf16[1,768,512]{2,1,0:T(8,128)(2,1)}, u32[]{:S(2)}) copy-start(bf16[1,768,512]{2,1,0:T(8,128)(2,1)} %param.6) | copy-start | bytes 2359300
  111.3 43.5 %collective-permute-start.16 = (bf16[384,512]{1,0:T(8,128)(2,1)S(1)}, bf16[384,512]{1,0:T(8,128)(2,1)S(1)}, u32[]{:S(2)}, u32[]{:S(2)}) collective-permute-start(bf16[384,512]{1,0:T(8,128)(2,1)S(1)} %get-tuple-element.64), channel_id=1, source_target_pairs={{0,32},{32,0},{1,33},{33,1},{2,34},{34,2},{3,35},{35,3},{4,36},{36... | collective-permute-start | bytes 1179656 | tf_op jit(solution)/shard_map/ppermute | solution.py:16
  122.7 6.2 %collective-permute-start.11 = (bf16[12,2048]{1,0:T(8,128)(2,1)S(1)}, bf16[12,2048]{1,0:T(8,128)(2,1)S(1)}, u32[]{:S(2)}, u32[]{:S(2)}) collective-permute-start(bf16[12,2048]{1,0:T(8,128)(2,1)S(1)} %convert_element_type.120), channel_id=1, source_target_pairs={{0,1},{1,0},{2,3},{3,2},{4,5},{5,4},{6,7},{7,6},{8,9},{9,8},{10,11... | collective-permute-start | bytes 147464 | tf_op jit(solution)/shard_map/ppermute | solution.py:16
  128.9 9.7 %collective-permute-start.12 = (bf16[384,512]{1,0:T(8,128)(2,1)S(1)}, bf16[384,512]{1,0:T(8,128)(2,1)S(1)}, u32[]{:S(2)}, u32[]{:S(2)}) collective-permute-start(bf16[384,512]{1,0:T(8,128)(2,1)S(1)} %get-tuple-element.50), channel_id=1, source_target_pairs={{64,0},{128,64},{192,128},{65,1},{129,65},{193,129},{66,2},{130,66... | collective-permute-start | bytes 1179656 | tf_op jit(solution)/shard_map/ppermute | solution.py:27
  130.2 11.4 %collective-permute-start.13 = (bf16[384,512]{1,0:T(8,128)(2,1)S(1)}, bf16[384,512]{1,0:T(8,128)(2,1)S(1)}, u32[]{:S(2)}, u32[]{:S(2)}) collective-permute-start(bf16[384,512]{1,0:T(8,128)(2,1)S(1)} %get-tuple-element.50), channel_id=1, source_target_pairs={{128,0},{192,64},{129,1},{193,65},{130,2},{194,66},{131,3},{195,67... | collective-permute-start | bytes 1179656 | tf_op jit(solution)/shard_map/ppermute | solution.py:27
  131.5 15.3 %collective-permute-start.14 = (bf16[384,512]{1,0:T(8,128)(2,1)S(1)}, bf16[384,512]{1,0:T(8,128)(2,1)S(1)}, u32[]{:S(2)}, u32[]{:S(2)}) collective-permute-start(bf16[384,512]{1,0:T(8,128)(2,1)S(1)} %get-tuple-element.50), channel_id=1, source_target_pairs={{192,0},{193,1},{194,2},{195,3},{196,4},{197,5},{198,6},{199,7},{2... | collective-permute-start | bytes 1179656 | tf_op jit(solution)/shard_map/ppermute | solution.py:27
  133.6 17.7 %collective-permute-start.21 = (f32[512,32]{0,1:T(8,128)S(1)}, f32[512,32]{0,1:T(8,128)S(1)}, u32[]{:S(2)}, u32[]{:S(2)}) collective-permute-start(f32[512,32]{0,1:T(8,128)S(1)} %fusion.28), channel_id=1, source_target_pairs={{0,256},{256,0},{1,257},{257,1},{2,258},{258,2},{3,259},{259,3},{4... | collective-permute-start | bytes 196616 | tf_op jit(solution)/shard_map/ppermute | solution.py:16
  147.0 7.8 %collective-permute-start.17 = (bf16[12,2048]{1,0:T(8,128)(2,1)S(1)}, bf16[12,2048]{1,0:T(8,128)(2,1)S(1)}, u32[]{:S(2)}, u32[]{:S(2)}) collective-permute-start(bf16[12,2048]{1,0:T(8,128)(2,1)S(1)} %convert_element_type.130), channel_id=1, source_target_pairs={{0,3},{1,2},{2,1},{3,0},{4,7},{5,6},{6,5},{7,4},{8,11},{9,10},{10,... | collective-permute-start | bytes 147464 | tf_op jit(solution)/shard_map/ppermute | solution.py:16
  151.9 43.4 %collective-permute-start.15 = (bf16[384,512]{1,0:T(8,128)(2,1)S(1)}, bf16[384,512]{1,0:T(8,128)(2,1)S(1)}, u32[]{:S(2)}, u32[]{:S(2)}) collective-permute-start(bf16[384,512]{1,0:T(8,128)(2,1)S(1)} %select_convert_fusion), channel_id=1, source_target_pairs={{0,32},{32,0},{1,33},{33,1},{2,34},{34,2},{3,35},{35,3},{4,36},{36... | collective-permute-start | bytes 1179656 | tf_op jit(solution)/shard_map/ppermute | solution.py:16
  155.6 5.9 %collective-permute-start.22 = (f32[2,16,1024]{2,1,0:T(8,128)S(1)}, f32[2,16,1024]{2,1,0:T(8,128)S(1)}, u32[]{:S(2)}, u32[]{:S(2)}) collective-permute-start(f32[2,16,1024]{2,1,0:T(8,128)S(1)} %maximum_multiply_fusion.1), channel_id=1, source_target_pairs={{0,256},{256,0},{1,257},{257,1},{2,258},{258,2},{3,259},{259,3},{4... | collective-permute-start | bytes 393224 | tf_op jit(solution)/shard_map/ppermute | solution.py:16
  157.7 37.9 %collective-permute-start.20 = (bf16[384,512]{1,0:T(8,128)(2,1)S(1)}, bf16[384,512]{1,0:T(8,128)(2,1)S(1)}, u32[]{:S(2)}, u32[]{:S(2)}) collective-permute-start(bf16[384,512]{1,0:T(8,128)(2,1)S(1)} %fusion.38), channel_id=1, source_target_pairs={{192,0},{193,1},{194,2},{195,3},{196,4},{197,5},{198,6},{199,7},{2... | collective-permute-start | bytes 1179656 | tf_op jit(solution)/shard_map/ppermute | solution.py:27
  159.0 36.6 %collective-permute-start.19 = (bf16[384,512]{1,0:T(8,128)(2,1)S(1)}, bf16[384,512]{1,0:T(8,128)(2,1)S(1)}, u32[]{:S(2)}, u32[]{:S(2)}) collective-permute-start(bf16[384,512]{1,0:T(8,128)(2,1)S(1)} %fusion.38), channel_id=1, source_target_pairs={{128,0},{192,64},{129,1},{193,65},{130,2},{194,66},{131,3},{195,67... | collective-permute-start | bytes 1179656 | tf_op jit(solution)/shard_map/ppermute | solution.py:27
  160.3 35.4 %collective-permute-start.18 = (bf16[384,512]{1,0:T(8,128)(2,1)S(1)}, bf16[384,512]{1,0:T(8,128)(2,1)S(1)}, u32[]{:S(2)}, u32[]{:S(2)}) collective-permute-start(bf16[384,512]{1,0:T(8,128)(2,1)S(1)} %fusion.38), channel_id=1, source_target_pairs={{64,0},{128,64},{192,128},{65,1},{129,65},{193,129},{66,2},{130,66... | collective-permute-start | bytes 1179656 | tf_op jit(solution)/shard_map/ppermute | solution.py:27
